TPU v7x, 256 devices: a whole 4x4x8 slice. The times are simulated.
256 devices in a mesh: cluster: 32 (over z, y), rep: 8 (over x, core).
Axes of the slice: x: 4, y: 4, z: 8, core: 2. Of those that a mesh axis runs over, the one named last changes fastest.
Arguments:
- vectors: float32 [65536, 768], P(('cluster', 'rep')), may hold values from -6 to 6
- parent_id: int32 [65536], P(('cluster', 'rep')), may hold values from 0 to 1023, as said below
- child_id: int32 [65536], P(('cluster', 'rep')), may hold values from 0 to 7
Outputs:
- centroids: float32 [8192, 768], P('cluster')
- shares: float32 [65536, 8], P(('cluster', 'rep'))
Inputs may be any that keep to these rules, and one draw needn't show every extreme that they name: `parent_id`: the vectors of one device (aligned blocks of 256 rows) fall under the parents of one owner block o (ids 32 o to 32 o + 31) at most 24 times for each o, and exactly 24 times for some o.
All inputs are finite; a program needn't handle non-finite values.
Results may differ from a plain program's by a relative error of at most 0.0001.
Values sent between devices are 32-bit elements; how exact they have to be, the bound alone decides.
No kernel may reach another device: no remote copies, remote signals or barrier semaphores. Data moves between devices by JAX's collectives and lax.ppermute only.
A program may use at most 64 MiB of HBM per device.

v0:
```python
import jax
import jax.numpy as jnp
from jax import lax
from jax.sharding import PartitionSpec as P

K = 8
PAR_DEV = 32


def on_device(vectors, parent_id, child_id):
    owners = lax.axis_size("cluster")
    vec_rows = vectors.shape[0]
    width = vectors.shape[1]
    cap_rows = 3 * vec_rows // owners
    slots = PAR_DEV * K
    owner = parent_id // PAR_DEV
    local_slot = (parent_id - owner * PAR_DEV) * K + child_id
    member = (owner[:, None] == jnp.arange(owners, dtype=jnp.int32)[None, :]).astype(jnp.int32)
    position = jnp.sum((jnp.cumsum(member, axis=0) - 1) * member, axis=1)
    target = owner * cap_rows + position
    send_rows = jnp.zeros((owners * cap_rows, width), jnp.float32).at[target].set(vectors)
    send_slots = jnp.full((owners * cap_rows,), -1, jnp.int32).at[target].set(local_slot)
    got_rows, got_slots = (
        lax.all_to_all(
            send_rows.reshape(owners, cap_rows, width),
            "cluster",
            split_axis=0,
            concat_axis=0,
            tiled=True,
        ),
        lax.all_to_all(
            send_slots.reshape(owners, cap_rows), "cluster", split_axis=0, concat_axis=0, tiled=True
        ),
    )
    all_rows = owners * cap_rows
    flat_rows = got_rows.reshape(all_rows, width)
    flat_slots = got_slots.reshape(all_rows)
    valid = flat_slots >= 0
    slot_hot = (flat_slots[:, None] == jnp.arange(slots, dtype=jnp.int32)[None, :]).astype(
        jnp.float32
    )
    sums = jnp.einsum("rs,rd->sd", slot_hot, flat_rows, precision=lax.Precision.HIGHEST)
    counts = jnp.sum(slot_hot, axis=0)
    sums, counts = lax.psum((sums, counts), "rep")
    first = sums / (counts + 1.0)[:, None]
    cent3 = first.reshape(PAR_DEV, K, width)
    cnt2 = counts.reshape(PAR_DEV, K)
    parents = jnp.where(valid, flat_slots // K, 0)
    block_rows = 128
    padded_rows = (all_rows + block_rows - 1) // block_rows * block_rows
    extra = padded_rows - all_rows
    pad_rows = jnp.concatenate([flat_rows, jnp.zeros((extra, width), jnp.float32)], axis=0)
    pad_parents = jnp.concatenate([parents, jnp.zeros((extra,), jnp.int32)], axis=0)

    def block_shares(item):
        rows, owned = item
        cent = cent3[owned]
        dist = jnp.sum((rows[:, None, :] - cent) ** 2, axis=-1) / width
        cnt = cnt2[owned]
        mean = jnp.sum(cnt, axis=1, keepdims=True) / K
        pen = dist + 0.5 * cnt / (mean + 1.0)
        weight = (1.0 + pen) ** (-4)
        return weight / jnp.sum(weight, axis=1, keepdims=True)

    share = lax.map(
        block_shares, (pad_rows.reshape(-1, block_rows, width), pad_parents.reshape(-1, block_rows))
    )
    share = share.reshape(padded_rows, K)[:all_rows]
    share = jnp.where(valid[:, None], share, 0.0)
    parent_hot = (
        (parents[:, None] == jnp.arange(PAR_DEV, dtype=jnp.int32)[None, :]) & valid[:, None]
    ).astype(jnp.float32)
    mixing = (parent_hot[:, :, None] * share[:, None, :]).reshape(all_rows, slots)
    weighted = jnp.einsum("rs,rd->sd", mixing, flat_rows, precision=lax.Precision.HIGHEST)
    total = jnp.sum(mixing, axis=0)
    weighted, total = lax.psum((weighted, total), "rep")
    centroids = weighted / (total + 1.0)[:, None]
    back = lax.all_to_all(
        share.reshape(owners, cap_rows, K), "cluster", split_axis=0, concat_axis=0, tiled=True
    )
    shares = back.reshape(all_rows, K)[target]
    return (centroids, shares)


def solution(mesh):
    in_specs = (P(("cluster", "rep"), None), P(("cluster", "rep")), P(("cluster", "rep")))
    out_specs = (P("cluster", None), P(("cluster", "rep"), None))
    return jax.shard_map(
        on_device, mesh=mesh, in_specs=in_specs, out_specs=out_specs, check_vma=False
    )
```

profile of v0, /device:TPU:8, one launch (start us, length us, event | category | flops | bytes accessed | tf_op | source)
XLA Modules:
  0.0 272.5 jit_solution(6645359234411163974)
XLA Ops:
  10.9 11.7 %all-to-all-start = ((s32[32,1,24]{2,1,0:T(1,128)}), s32[32,1,24]{2,1,0:T(1,128)S(1)}, u32[]{:S(2)}, u32[]{:S(2)}) async-start(s32[32,1,24]{2,1,0:T(1,128)} %bitcast.7), calls=%async_computation | async-start | bytes 32768 | tf_op jit(solution)/shard_map/all_to_all | solution.py:31
  22.6 3.5 %scatter_custom_fusion.1 = f32[768,768]{1,0:T(8,128)} fusion(s32[256]{0:T(256)S(1)} %compare_select_fusion.1, f32[256,768]{1,0:T(8,128)} %param.5, f32[]{:T(128)} %constant.78.clone.1), kind=kCustom, calls=%fused_computation.22 | custom fusion | bytes 2359808 | tf_op jit(solution)/shard_map/scatter | solution.py:21
  26.2 4.9 %all-to-all-done = s32[32,1,24]{2,1,0:T(1,128)S(1)} async-done(((s32[32,1,24]{2,1,0:T(1,128)}), s32[32,1,24]{2,1,0:T(1,128)S(1)}, u32[]{:S(2)}, u32[]{:S(2)}) %all-to-all-start) | async-done | bytes 3104 | tf_op jit(solution)/shard_map/all_to_all | solution.py:31
  31.1 5.2 %all-to-all-start.1 = ((f32[32,24,768]{2,1,0:T(8,128)}), f32[32,24,768]{2,1,0:T(8,128)S(1)}, u32[]{:S(2)}, u32[]{:S(2)}) async-start(f32[32,24,768]{2,1,0:T(8,128)} %bitcast.80), calls=%async_computation.1 | async-start | bytes 4718592 | tf_op jit(solution)/shard_map/all_to_all | solution.py:24
  37.8 13.6 %psum.29 = f32[256]{0:T(256)S(1)} all-reduce(f32[256]{0:T(256)S(1)} %convert_reduce_fusion), channel_id=1, replica_groups=mesh['cluster'=32,'rep'=8] {'rep'}, use_global_device_ids=true, to_apply=%region_7.8 | all-reduce | flops 256 | bytes 2048 | tf_op jit(solution)/shard_map/psum | solution.py:44
  51.8 38.3 %all-to-all-done.1 = f32[32,24,768]{2,1,0:T(8,128)S(1)} async-done(((f32[32,24,768]{2,1,0:T(8,128)}), f32[32,24,768]{2,1,0:T(8,128)S(1)}, u32[]{:S(2)}, u32[]{:S(2)}) %all-to-all-start.1) | async-done | bytes 2359328 | tf_op jit(solution)/shard_map/all_to_all | solution.py:24
  92.6 65.0 %all-reduce.3.cloned.1.call-done = f32[256,768]{1,0:T(8,128)} async-done(((f32[256,768]{1,0:T(8,128)}), f32[256,768]{1,0:T(8,128)}) %all-reduce.3.cloned.1.call-update) | async-done | bytes 786448 | tf_op jit(solution)/shard_map/psum | solution.py:44
  158.8 35.3 %while.10 = (s32[]{:T(128)}, f32[6,128,8]{1,2,0:T(8,128)S(1)}, f32[6,128,768]{2,1,0:T(8,128)S(1)}, s32[6,128]{1,0:T(8,128)S(1)}, f32[32,8,768]{2,1,0:T(8,128)S(1...) while((s32[]{:T(128)}, f32[6,128,8]{1,2,0:T(8,128)S(1)}, f32[6,128,768]{2,1,0:T(8,128)S(1)}, ...), condition=%wide.region_12.13_spmd, body=%wide.region_8.12_spmd.sunk | while | flops 2379138 | bytes 10680421 | solution.py:65
  158.8 2.5 gather_fusion.1
  161.3 2.4 multiply_reduce_fusion.3
  164.7 2.5 gather_fusion.1
  167.2 2.4 multiply_reduce_fusion.3
  170.6 2.5 gather_fusion.1
  173.1 2.4 multiply_reduce_fusion.3
  176.5 2.5 gather_fusion.1
  179.0 2.4 multiply_reduce_fusion.3
  182.4 2.5 gather_fusion.1
  184.9 2.4 multiply_reduce_fusion.3
  188.3 2.5 gather_fusion.1
  190.8 2.4 multiply_reduce_fusion.3
  194.1 3.0 %fusion.11 = f32[256,768]{1,0:T(8,128)} fusion(f32[768,768]{1,0:T(8,128)S(1)} %bitcast.79, f32[768,8]{0,1:T(8,128)S(1)} %bitcast_select_fusion, f32[768,32]{0,1:T(8,128)S(1)} %fusion.17), kind=kOutput, calls=%fused_computation.26 | convolution fusion | flops 1812135936 | bytes 3268608 | tf_op jit(solution)/shard_map/rs,rd->sd/dot_general | solution.py:74
  198.4 10.2 %all-to-all-start.2 = ((f32[32,1,192]{2,1,0:T(1,128)}), f32[32,1,192]{2,1,0:T(1,128)S(1)}, u32[]{:S(2)}, u32[]{:S(2)}) async-start(f32[32,1,192]{2,1,0:T(1,128)} %reshape.354), calls=%async_computation.2 | async-start | bytes 65536 | tf_op jit(solution)/shard_map/all_to_all | solution.py:78
  208.6 13.1 %psum.31 = f32[256]{0:T(256)S(1)} all-reduce(f32[256]{0:T(256)S(1)} %reduce_sum.59), channel_id=1, replica_groups=mesh['cluster'=32,'rep'=8] {'rep'}, use_global_device_ids=true, to_apply=%region_15.16 | all-reduce | flops 256 | bytes 2048 | tf_op jit(solution)/shard_map/psum | solution.py:76
  224.6 39.0 %all-reduce.5.cloned.1.call-done = f32[256,768]{1,0:T(8,128)} async-done(((f32[256,768]{1,0:T(8,128)}), f32[256,768]{1,0:T(8,128)}) %all-reduce.5.cloned.1.call-update) | async-done | bytes 786448 | tf_op jit(solution)/shard_map/psum | solution.py:76
  (109 shorter events, 21.4 us)
Async XLA Ops:
  10.9 20.2 %all-to-all-start = ((s32[32,1,24]{2,1,0:T(1,128)}), s32[32,1,24]{2,1,0:T(1,128)S(1)}, u32[]{:S(2)}, u32[]{:S(2)}) async-start(s32[32,1,24]{2,1,0:T(1,128)} %bitcast.7), calls=%async_computation | async-start | bytes 32768 | tf_op jit(solution)/shard_map/all_to_all | solution.py:31
  31.1 59.0 %all-to-all-start.1 = ((f32[32,24,768]{2,1,0:T(8,128)}), f32[32,24,768]{2,1,0:T(8,128)S(1)}, u32[]{:S(2)}, u32[]{:S(2)}) async-start(f32[32,24,768]{2,1,0:T(8,128)} %bitcast.80), calls=%async_computation.1 | async-start | bytes 4718592 | tf_op jit(solution)/shard_map/all_to_all | solution.py:24
  36.2 121.3 %all-reduce.3.cloned.1.call-start = ((), (), s32[]{:S(2)}) async-start(), calls=%async_computation.3 | async-start | bytes 1572864 | tf_op jit(solution)/shard_map/psum | solution.py:44
  92.5 171.1 %all-reduce.5.cloned.1.call-start = ((), (), s32[]{:S(2)}) async-start(), calls=%async_computation.4 | async-start | bytes 1572864 | tf_op jit(solution)/shard_map/psum | solution.py:76
  198.4 23.3 %all-to-all-start.2 = ((f32[32,1,192]{2,1,0:T(1,128)}), f32[32,1,192]{2,1,0:T(1,128)S(1)}, u32[]{:S(2)}, u32[]{:S(2)}) async-start(f32[32,1,192]{2,1,0:T(1,128)} %reshape.354), calls=%async_computation.2 | async-start | bytes 65536 | tf_op jit(solution)/shard_map/all_to_all | solution.py:78
Sparse Core Ops, SparseCore 0:
  92.6 64.8 all-reduce.2
  197.5 66.0 all-reduce.4
where the time goes:
time: 273 us
  waiting for transfers between devices  147 us (54%)
  local copies, waits for them, and re-layouts  29.5 us (11%)
  starting transfers between devices  27.1 us (10%)
  blocking collectives  26.7 us (10%)
  other arithmetic  22.1 us (8%)
  between operations  14.2 us (5%)
  matrix products  5.41 us (2%)
    psum x1, waiting for transfers between devices, on_device(): sums, counts = lax.psum((sums, counts), 'rep')  65 us
    psum x1, waiting for transfers between devices, on_device(): weighted, total = lax.psum((weighted, total), 'rep')  39 us
    all_to_all x1, waiting for transfers between devices, on_device(): lax.all_to_all(send_rows.reshape(owners, cap_rows, width), 'cluster', spl...  38.3 us
    gather x6, local copies, waits for them, and re-layouts, block_shares(): cent = cent3[owned]  14.8 us
    reduce_sum x6, other arithmetic, block_shares(): dist = jnp.sum((rows[:, None, :] - cent) ** 2, axis=-1) / width  14.3 us
    psum x1, blocking collectives, on_device(): sums, counts = lax.psum((sums, counts), 'rep')  13.6 us
    psum x1, blocking collectives, on_device(): weighted, total = lax.psum((weighted, total), 'rep')  13.1 us
    all_to_all x1, starting transfers between devices, on_device(): lax.all_to_all(send_slots.reshape(owners, cap_rows), 'cluster', split_axi...  11.7 us
  transfers between devices with their start and end apart: 5, of which 4 were waited for; matrix products, arithmetic and copies ran while one was open for 3% of the time, Pallas kernels for 0%

commit v1 on v0

v1 whole, which is shorter than its diff:
```python
import functools

import jax
import jax.numpy as jnp
from jax import lax
from jax.experimental import pallas as pl
from jax.experimental.pallas import tpu as pltpu
from jax.sharding import PartitionSpec as P

K = 8
PAR_DEV = 32
OWNERS = 32
REPS = 8
SLOTS = PAR_DEV * K
D = 768
PART = D // REPS
ROWS = PART + 8
VEC = 256
LANES = 128
PAIR = 2 * LANES
STACK = PART + 16 + PART
F32 = jnp.float32
BF16 = jnp.bfloat16
NT = (((1,), (1,)), ((), ()))


def params():
    return pltpu.CompilerParams(vmem_limit_bytes=48 * 2**20)


def iota(shape, dim):
    return lax.broadcasted_iota(jnp.int32, shape, dim)


def parts_of(x):
    high = x.astype(BF16)
    return high, (x - high.astype(F32)).astype(BF16)


def turn_kernel(v_ref, g_ref, out_ref):
    for tile in range(D // LANES):
        turned = v_ref[:, tile * LANES : (tile + 1) * LANES].T
        start = tile * LANES
        while start < (tile + 1) * LANES:
            part, row = divmod(start, PART)
            size = min(PART - row, (tile + 1) * LANES - start)
            at = start - tile * LANES
            out_ref[part, row : row + size, :] = turned[at : at + size, :]
            start += size
    slots = jnp.broadcast_to(g_ref[...], (ROWS - PART, VEC))
    for part in range(REPS):
        out_ref[part, PART:ROWS, :] = slots


def pack_kernel(cap, in_ref, out_ref, target_ref, most_ref, left, column):
    groups = OWNERS * cap // PAIR
    before = (iota((VEC, VEC), 0) < iota((VEC, VEC), 1)).astype(F32).astype(BF16)
    carry = jnp.zeros((OWNERS, 1), F32)
    targets = []
    for src in range(REPS):
        slot = in_ref[src, PART : PART + 1, :].astype(jnp.int32)
        owner = slot >> 8
        local = (slot & (SLOTS - 1)) + 1
        hot = (owner == iota((OWNERS, VEC), 0)).astype(F32)
        ahead = jnp.dot(hot.astype(BF16), before, preferred_element_type=F32) + carry
        position = jnp.sum(hot * ahead, axis=0, keepdims=True)
        carry = carry + jnp.sum(hot, axis=1, keepdims=True)
        target = owner.astype(F32) * cap + position
        targets.append(jnp.where(position < cap, target, -1.0))
        high, low = parts_of(in_ref[src, 0:PART, :])
        left[src, 0:PART, :] = high
        left[src, PART : PART + 16, :] = jnp.broadcast_to(local.astype(F32), (16, VEC)).astype(BF16)
        left[src, PART + 16 : STACK, :] = low
    rows = jnp.concatenate(targets, axis=0)
    target_ref[...] = rows.astype(jnp.int32)
    most_ref[...] = jnp.broadcast_to(jnp.max(carry, axis=0, keepdims=True), (8, LANES))
    turned = jnp.concatenate([rows, jnp.zeros((LANES - REPS, VEC), F32)], axis=0).T
    for src in range(REPS):
        column[src] = jnp.broadcast_to(turned[:, src : src + 1], (VEC, LANES))
    lane = iota((VEC, LANES), 1).astype(F32)

    def group(n, _):
        base = (n * PAIR).astype(F32)
        total = jnp.zeros((STACK, PAIR), F32)
        for src in range(REPS):
            at = column[src] - base
            hot = jnp.concatenate(
                [
                    jnp.where(at == lane, 1.0, 0.0).astype(BF16),
                    jnp.where(at == lane + LANES, 1.0, 0.0).astype(BF16),
                ],
                axis=1,
            )
            total = total + jnp.dot(left[src], hot, preferred_element_type=F32)
        values = total[0:PART] + total[PART + 16 : STACK]
        for half in range(2):
            cut = slice(half * LANES, (half + 1) * LANES)
            out_ref[2 * n + half, 0:PART, :] = values[:, cut]
            out_ref[2 * n + half, PART:ROWS, :] = total[PART : PART + 8, cut]
        return 0

    lax.fori_loop(0, groups, group, 0)


def load_pair(x_ref, n):
    x = jnp.concatenate([x_ref[2 * n, 0:PART, :], x_ref[2 * n + 1, 0:PART, :]], axis=1)
    slot = jnp.concatenate(
        [x_ref[2 * n, PART : PART + 1, :], x_ref[2 * n + 1, PART : PART + 1, :]], axis=1
    )
    return x, slot.astype(jnp.int32)


def stack_of(x):
    high, low = parts_of(x)
    return jnp.concatenate([high, jnp.ones((16, PAIR), BF16), low], axis=0)


def distance_kernel(blocks, x_ref, out_ref, total):
    total[...] = jnp.zeros_like(total)

    def add(n, _):
        x, slot = load_pair(x_ref, n)
        hot = jnp.where(iota((SLOTS, PAIR), 0) + 1 == slot, 1.0, 0.0).astype(BF16)
        total[...] += lax.dot_general(stack_of(x), hot, NT, preferred_element_type=F32)
        return 0

    lax.fori_loop(0, blocks // 2, add, 0)
    sums = total[0:PART, :] + total[PART + 16 : STACK, :]
    counts = total[PART : PART + 8, :]
    first = sums / (counts[0:1] + 1.0)
    turned = jnp.concatenate(
        [first, counts, jnp.zeros((LANES - PART - 8, SLOTS), F32)], axis=0
    ).T
    center = turned[:, 0:PART]
    count = turned[:, PART : PART + 1].reshape(PAR_DEV, K, 1)
    mean = jnp.sum(count, axis=1, keepdims=True) / K
    extra = (0.5 * count / (mean + 1.0)).reshape(SLOTS, 1) / REPS
    own = jnp.sum(center * center, axis=1, keepdims=True) / D + extra
    scaled = center * (-2.0 / D)

    def measure(n, _):
        x, slot = load_pair(x_ref, n)
        cross = jnp.dot(
            scaled, x, precision=lax.Precision.HIGHEST, preferred_element_type=F32
        )
        parent = (slot - 1) >> 3
        terms = (cross + own).reshape(PAR_DEV, K, PAIR)
        picked = jnp.where(iota((PAR_DEV, K, PAIR), 0) == parent[None], terms, 0.0)
        part = jnp.sum(picked, axis=0) + jnp.sum(x * x, axis=0, keepdims=True) / D
        out_ref[2 * n] = part[:, 0:LANES]
        out_ref[2 * n + 1] = part[:, LANES:PAIR]
        return 0

    lax.fori_loop(0, blocks // 2, measure, 0)


def share_kernel(blocks, x_ref, pen_ref, cent_ref, share_ref, total, rest):
    total[...] = jnp.zeros_like(total)
    rest[...] = jnp.zeros_like(rest)

    def add(n, _):
        x, slot = load_pair(x_ref, n)
        grown = 1.0 + jnp.concatenate([pen_ref[2 * n], pen_ref[2 * n + 1]], axis=1)
        square = grown * grown
        weight = 1.0 / (square * square)
        share = weight / jnp.sum(weight, axis=0, keepdims=True)
        share = jnp.where(slot > 0, share, 0.0)
        share_ref[2 * n] = share[:, 0:LANES]
        share_ref[2 * n + 1] = share[:, LANES:PAIR]
        parent = (slot - 1) >> 3
        mixing = jnp.where(
            iota((PAR_DEV, K, PAIR), 0) == parent[None], share[None], 0.0
        ).reshape(SLOTS, PAIR)
        high, low = parts_of(mixing)
        left = stack_of(x)
        total[...] += lax.dot_general(left, high, NT, preferred_element_type=F32)
        rest[...] += lax.dot_general(
            left[0 : PART + 16], low, NT, preferred_element_type=F32
        )
        return 0

    lax.fori_loop(0, blocks // 2, add, 0)
    weighted = total[0:PART, :] + total[PART + 16 : STACK, :] + rest[0:PART, :]
    summed = total[PART : PART + 1, :] + rest[PART : PART + 1, :]
    cent_ref[...] = weighted / (summed + 1.0)


def join_kernel(at_ref, *refs):
    *pieces, out_ref, whole = refs
    x, core = at_ref[0], at_ref[1]
    for index, piece in enumerate(pieces):
        step, other = divmod(index, 2)
        where = ((x - step) & 3) * 2 + (core ^ other)
        whole[pl.ds(pl.multiple_of(where * PART, 8), PART), :] = piece[...]
    for tile in range(D // LANES):
        cut = slice(tile * LANES, (tile + 1) * LANES)
        out_ref[:, cut] = whole[cut, :].T


def take_kernel(blocks, at_ref, back_ref, target_ref, out_ref):
    target = target_ref[pl.ds(at_ref[2], 1), :]
    total = jnp.zeros((3 * K, VEC), F32)
    for n in range(blocks):
        hot = jnp.where(iota((LANES, VEC), 0) + n * LANES == target, 1.0, 0.0).astype(BF16)
        high, low = parts_of(back_ref[n])
        least = (back_ref[n] - high.astype(F32) - low.astype(F32)).astype(BF16)
        left = jnp.concatenate([high.astype(F32), low.astype(F32), least.astype(F32)], axis=0)
        total = total + jnp.dot(left.astype(BF16), hot, preferred_element_type=F32)
    out_ref[...] = total[0:K] + total[K : 2 * K] + total[2 * K : 3 * K]


def shape(*dims, kind=F32):
    return jax.ShapeDtypeStruct(dims, kind)


def cost(flops, data):
    return pl.CostEstimate(flops=flops, bytes_accessed=data, transcendentals=0)


def along_x(step):
    return [(i, ((i // 2 + step) % 4) * 2 + i % 2) for i in range(REPS)]


CORES = [(i, i ^ 1) for i in range(REPS)]


def sum_over_rep(x):
    x = x + lax.ppermute(x, "rep", CORES)
    x = x + lax.ppermute(x, "rep", [(i, i ^ 2) for i in range(REPS)])
    return x + lax.ppermute(x, "rep", [(i, i ^ 6) for i in range(REPS)])


def refine(cap, got):
    blocks = OWNERS * cap // LANES
    packed, target, most = pl.pallas_call(
        functools.partial(pack_kernel, cap),
        out_shape=(
            shape(blocks, ROWS, LANES),
            shape(REPS, VEC, kind=jnp.int32),
            shape(8, LANES),
        ),
        scratch_shapes=[pltpu.VMEM((REPS, STACK, VEC), BF16), pltpu.VMEM((REPS, VEC, LANES), F32)],
        compiler_params=params(),
        cost_estimate=cost(2 * STACK * 2048 * OWNERS * cap, 3_000_000),
        name="pack",
    )(got)
    per = cap // LANES
    rows = lax.all_to_all(
        packed.reshape(OWNERS, per * ROWS, LANES), "cluster", 0, 0, tiled=True
    ).reshape(blocks, ROWS, LANES)
    partial = pl.pallas_call(
        functools.partial(distance_kernel, blocks),
        out_shape=shape(blocks, K, LANES),
        scratch_shapes=[pltpu.VMEM((STACK, SLOTS), F32)],
        compiler_params=params(),
        cost_estimate=cost(2 * 8 * PART * SLOTS * OWNERS * cap, 2_000_000),
        name="distance",
    )(rows)
    pen = sum_over_rep(partial)
    cent, share = pl.pallas_call(
        functools.partial(share_kernel, blocks),
        out_shape=(shape(PART, SLOTS), shape(blocks, K, LANES)),
        scratch_shapes=[
            pltpu.VMEM((STACK, SLOTS), F32),
            pltpu.VMEM((PART + 16, SLOTS), F32),
        ],
        compiler_params=params(),
        cost_estimate=cost(2 * 3 * PART * SLOTS * OWNERS * cap, 2_000_000),
        name="share",
    )(rows, pen)
    back = lax.all_to_all(
        share.reshape(OWNERS, per * K, LANES), "cluster", 0, 0, tiled=True
    ).reshape(blocks, K, LANES)
    pieces = []
    for step in range(4):
        mine = lax.ppermute(cent, "rep", along_x(step)) if step else cent
        pieces += [mine, lax.ppermute(mine, "rep", CORES)]
    return pieces, back, target, most


def finish(cap, pieces, back, target):
    blocks = OWNERS * cap // LANES
    rep = lax.axis_index("rep")
    at = jnp.stack([rep // 2, rep % 2, rep]).astype(jnp.int32)
    smem = pl.BlockSpec(memory_space=pltpu.SMEM)
    vmem = pl.BlockSpec(memory_space=pltpu.VMEM)
    centroids = pl.pallas_call(
        join_kernel,
        out_shape=shape(SLOTS, D),
        in_specs=[smem] + [vmem] * REPS,
        scratch_shapes=[pltpu.VMEM((D, SLOTS), F32)],
        compiler_params=params(),
        cost_estimate=cost(0, 1_600_000),
        name="join",
    )(at, *pieces)
    shares = pl.pallas_call(
        functools.partial(take_kernel, blocks),
        out_shape=shape(K, VEC),
        in_specs=[smem, vmem, vmem],
        compiler_params=params(),
        cost_estimate=cost(2 * 24 * VEC * OWNERS * cap, 200_000),
        name="take",
    )(at, back, target)
    return centroids, shares


def on_device(vectors, parent_id, child_id):
    slot = (parent_id * K + child_id).astype(F32).reshape(1, VEC)
    turned = pl.pallas_call(
        turn_kernel,
        out_shape=shape(REPS, ROWS, VEC),
        compiler_params=params(),
        cost_estimate=cost(0, 1_600_000),
        name="turn",
    )(vectors, slot)
    got = lax.all_to_all(turned, "rep", 0, 0, tiled=True)
    pieces, back, target, most = refine(LANES, got)
    for bit in (1, 2, 4, 8, 16):
        most = jnp.maximum(
            most, lax.ppermute(most, "cluster", [(i, i ^ bit) for i in range(OWNERS)])
        )
    over = most[0, 0] > LANES

    def wide(got, pieces, back, target):
        pieces, back, target, _ = refine(PAIR, got)
        return finish(PAIR, pieces, back, target)

    def narrow(got, pieces, back, target):
        return finish(LANES, pieces, back, target)

    centroids, shares = lax.cond(over, wide, narrow, got, pieces, back, target)
    return centroids, shares.T


def solution(mesh):
    in_specs = (P(("cluster", "rep"), None), P(("cluster", "rep")), P(("cluster", "rep")))
    out_specs = (P("cluster", None), P(("cluster", "rep"), None))
    return jax.shard_map(
        on_device, mesh=mesh, in_specs=in_specs, out_specs=out_specs, check_vma=False
    )
```

time: 273 us -> 152 us (0.56)
  waiting for transfers between devices: 147 us -> 30.4 us
  blocking collectives: 26.7 us -> 71.6 us
  local copies, waits for them, and re-layouts: 29.5 us -> 2.52 us
  Pallas kernels: 0 us -> 23.9 us
  other arithmetic: 22.1 us -> 0.84 us
  between operations: 14.2 us -> 1.41 us
  starting transfers between devices: 27.1 us -> 21.3 us
  matrix products: 5.41 us -> 0 us
    psum x2 -> x0, waiting for transfers between devices: 104 us -> none  [the longest x1 65 us: on_device(): sums, counts = lax.psum((sums, counts), 'rep')]
    all_to_all x0 -> x2, blocking collectives: none -> 71.6 us  [the longest x1 53.5 us: refine(): lax.all_to_all(packed.reshape(OWNERS, per * ROWS, LANES), 'cluster', 0, 0...]
    all_to_all x3 -> x1, waiting for transfers between devices: 43.2 us -> 0.01 us  [refine(): lax.all_to_all(share.reshape(OWNERS, per * K, LANES), 'cluster', 0, 0, ti...]
    ppermute x0 -> x15, waiting for transfers between devices: none -> 30.4 us  [the longest x5 12.8 us: on_device(): lax.ppermute(most, 'cluster', [(i, i ^ bit) for i in range(OWNERS)])]
    psum x2 -> x0, blocking collectives: 26.7 us -> none  [the longest x1 13.6 us: on_device(): sums, counts = lax.psum((sums, counts), 'rep')]
    pallas_call x0 -> x6, Pallas kernels: none -> 23.9 us  [the longest x1 9.63 us: refine(): pl.pallas_call(functools.partial(distance_kernel, blocks), out_shape=shap...]
    all_to_all x3 -> x1, starting transfers between devices: 27 us -> 5.57 us  [refine(): lax.all_to_all(share.reshape(OWNERS, per * K, LANES), 'cluster', 0, 0, ti...]
    gather x19 -> x0, local copies, waits for them, and re-layouts: 19.8 us -> none  [the longest x6 14.8 us: block_shares(): cent = cent3[owned]]
  transfers between devices with their start and end apart: 5 -> 16, of which waited for: 4 -> 11; matrix products, arithmetic and copies ran while one was open for 3% -> 0% of each run, Pallas kernels for 0% -> 0%
where the time goes in v1:
time: 152 us
  blocking collectives  71.6 us (47%)
  waiting for transfers between devices  30.4 us (20%)
  Pallas kernels  23.9 us (16%)
  starting transfers between devices  21.3 us (14%)
  local copies, waits for them, and re-layouts  2.52 us (2%)
    all_to_all x1, blocking collectives, refine(): lax.all_to_all(packed.reshape(OWNERS, per * ROWS, LANES), 'cluster', 0, 0...  53.5 us
    all_to_all x1, blocking collectives, on_device(): got = lax.all_to_all(turned, 'rep', 0, 0, tiled=True)  18 us
    ppermute x5, waiting for transfers between devices, on_device(): lax.ppermute(most, 'cluster', [(i, i ^ bit) for i in range(OWNERS)])  12.8 us
    ppermute x5, starting transfers between devices, on_device(): lax.ppermute(most, 'cluster', [(i, i ^ bit) for i in range(OWNERS)])  11.5 us
    pallas_call x1, Pallas kernels, refine(): pl.pallas_call(functools.partial(distance_kernel, blocks), out_shape=shap...  9.63 us
    pallas_call x1, Pallas kernels, refine(): pl.pallas_call(functools.partial(pack_kernel, cap), out_shape=(shape(bloc...  7.23 us
    ppermute x3, waiting for transfers between devices, refine(): mine = lax.ppermute(cent, 'rep', along_x(step)) if step else cent  6.21 us
    all_to_all x1, starting transfers between devices, refine(): lax.all_to_all(share.reshape(OWNERS, per * K, LANES), 'cluster', 0, 0, ti...  5.57 us
  transfers between devices with their start and end apart: 16, of which 11 were waited for; matrix products, arithmetic and copies ran while one was open for 0% of the time, Pallas kernels for 0%

profile of v1, /device:TPU:8, one launch (start us, length us, event | category | flops | bytes accessed | tf_op | source)
XLA Modules:
  0.0 152.2 jit_solution(10156031034543049056)
XLA Ops:
  1.3 1.1 copy-done
  2.7 18.0 %all_to_all.27.in_ref = f32[8,104,256]{2,1,0:T(8,128)S(1)} all-to-all(f32[8,104,256]{2,1,0:T(8,128)S(1)} %turn.1), channel_id=1, replica_groups=mesh['cluster'=32,'rep'=8] {'rep'}, dimensions={0} | all-to-all | bytes 1703936 | tf_op jit(solution)/shard_map/all_to_all | solution.py:316
  20.8 7.2 %pack.3 = (f32[32,104,128]{2,1,0:T(8,128)S(1)}, s32[8,256]{1,0:T(8,128)S(1)}, f32[8,128]{1,0:T(8,128)S(1)}) custom-call(f32[8,104,256]{2,1,0:T(8,128)S(1)} %all_to_all.27.in_ref), custom_call_target="tpu_custom_call" | custom-call | flops 3489660928 | bytes 3000000 | tf_op jit(solution)/shard_map/pack/pallas_call | solution.py:235
  28.0 53.5 %all_to_all.28.x_ref = f32[32,104,128]{2,1,0:T(8,128)S(1)} all-to-all(f32[32,104,128]{2,1,0:T(8,128)S(1)} %get-tuple-element.45), channel_id=1, replica_groups=mesh['cluster'=32,'rep'=8] {'cluster'}, dimensions={0} | all-to-all | bytes 3407872 | tf_op jit(solution)/shard_map/all_to_all | solution.py:248
  81.6 9.6 %distance.3 = f32[32,8,128]{2,1,0:T(8,128)S(1)} custom-call(f32[32,104,128]{2,1,0:T(8,128)S(1)} %all_to_all.28.x_ref), custom_call_target="tpu_custom_call" | custom-call | flops 1610612736 | bytes 2000000 | tf_op jit(solution)/shard_map/distance/pallas_call | solution.py:251
  91.3 1.3 collective-permute-done.15
  93.3 5.0 %collective-permute-done.16 = f32[32,8,128]{2,1,0:T(8,128)S(1)} collective-permute-done((f32[32,8,128]{2,1,0:T(8,128)S(1)}, f32[32,8,128]{2,1,0:T(8,128)S(1)}, u32[]{:S(2)}, u32[]{:S(2)}) %collective-permute-start.16) | collective-permute-done | bytes 131104 | tf_op jit(solution)/shard_map/ppermute | solution.py:229
  98.3 1.2 collective-permute-start.17
  99.5 5.0 %collective-permute-done.17 = f32[32,8,128]{2,1,0:T(8,128)S(1)} collective-permute-done((f32[32,8,128]{2,1,0:T(8,128)S(1)}, f32[32,8,128]{2,1,0:T(8,128)S(1)}, u32[]{:S(2)}, u32[]{:S(2)}) %collective-permute-start.17) | collective-permute-done | bytes 131104 | tf_op jit(solution)/shard_map/ppermute | solution.py:230
  104.6 5.0 %share.3 = (f32[96,256]{1,0:T(8,128)S(1)}, f32[32,8,128]{2,1,0:T(8,128)}) custom-call(f32[32,104,128]{2,1,0:T(8,128)S(1)} %all_to_all.28.x_ref, f32[32,8,128]{2,1,0:T(8,128)S(1)} %add.33.pen_ref), custom_call_target="tpu_custom_call" | custom-call | flops 603979776 | bytes 2000000 | tf_op jit(solution)/shard_map/share/pallas_call | solution.py:260
  109.6 5.6 %all-to-all-start.4 = ((f32[32,8,128]{2,1,0:T(8,128)}), f32[32,8,128]{2,1,0:T(8,128)S(1)}, u32[]{:S(2)}, u32[]{:S(2)}) async-start(f32[32,8,128]{2,1,0:T(8,128)} %get-tuple-element.47), calls=%async_computation.4 | async-start | bytes 262144 | tf_op jit(solution)/shard_map/all_to_all | solution.py:271
  115.1 1.2 collective-permute-start.23
  117.3 2.5 %collective-permute-done.23 = f32[96,256]{1,0:T(8,128)S(1)} collective-permute-done((f32[96,256]{1,0:T(8,128)S(1)}, f32[96,256]{1,0:T(8,128)S(1)}, u32[]{:S(2)}, u32[]{:S(2)}) %collective-permute-start.23) | collective-permute-done | bytes 98336 | tf_op jit(solution)/shard_map/ppermute | solution.py:276
  119.8 2.8 %collective-permute-done.21 = f32[96,256]{1,0:T(8,128)S(1)} collective-permute-done((f32[96,256]{1,0:T(8,128)S(1)}, f32[96,256]{1,0:T(8,128)S(1)}, u32[]{:S(2)}, u32[]{:S(2)}) %collective-permute-start.21) | collective-permute-done | bytes 98336 | tf_op jit(solution)/shard_map/ppermute | solution.py:276
  123.8 3.4 %collective-permute-done.10 = f32[8,128]{1,0:T(8,128)S(1)} collective-permute-done((f32[8,128]{1,0:T(8,128)S(1)}, f32[8,128]{1,0:T(8,128)S(1)}, u32[]{:S(2)}, u32[]{:S(2)}) %collective-permute-start.10) | collective-permute-done | bytes 4128 | tf_op jit(solution)/shard_map/ppermute | solution.py:320
  127.2 2.1 %collective-permute-start.11 = (f32[8,128]{1,0:T(8,128)S(1)}, f32[8,128]{1,0:T(8,128)S(1)}, u32[]{:S(2)}, u32[]{:S(2)}) collective-permute-start(f32[8,128]{1,0:T(8,128)S(1)} %max.15), channel_id=1, source_target_pairs={{0,16},{8,24},{16,0},{24,8},{32,48},{40,56},{48,32},{56,40},{64,80... | collective-permute-start | bytes 12296 | tf_op jit(solution)/shard_map/ppermute | solution.py:320
  129.2 3.0 %collective-permute-done.11 = f32[8,128]{1,0:T(8,128)S(1)} collective-permute-done((f32[8,128]{1,0:T(8,128)S(1)}, f32[8,128]{1,0:T(8,128)S(1)}, u32[]{:S(2)}, u32[]{:S(2)}) %collective-permute-start.11) | collective-permute-done | bytes 4128 | tf_op jit(solution)/shard_map/ppermute | solution.py:320
  132.3 1.5 collective-permute-start.12
  133.7 2.1 %collective-permute-done.12 = f32[8,128]{1,0:T(8,128)S(1)} collective-permute-done((f32[8,128]{1,0:T(8,128)S(1)}, f32[8,128]{1,0:T(8,128)S(1)}, u32[]{:S(2)}, u32[]{:S(2)}) %collective-permute-start.12) | collective-permute-done | bytes 4128 | tf_op jit(solution)/shard_map/ppermute | solution.py:320
  135.9 2.4 %collective-permute-start.13 = (f32[8,128]{1,0:T(8,128)S(1)}, f32[8,128]{1,0:T(8,128)S(1)}, u32[]{:S(2)}, u32[]{:S(2)}) collective-permute-start(f32[8,128]{1,0:T(8,128)S(1)} %max.17), channel_id=1, source_target_pairs={{0,64},{8,72},{16,80},{24,88},{32,96},{40,104},{48,112},{56,120},{... | collective-permute-start | bytes 12296 | tf_op jit(solution)/shard_map/ppermute | solution.py:320
  138.3 2.1 %collective-permute-done.13 = f32[8,128]{1,0:T(8,128)S(1)} collective-permute-done((f32[8,128]{1,0:T(8,128)S(1)}, f32[8,128]{1,0:T(8,128)S(1)}, u32[]{:S(2)}, u32[]{:S(2)}) %collective-permute-start.13) | collective-permute-done | bytes 4128 | tf_op jit(solution)/shard_map/ppermute | solution.py:320
  140.4 5.4 %collective-permute-start.14 = (f32[8,128]{1,0:T(8,128)S(1)}, f32[8,128]{1,0:T(8,128)S(1)}, u32[]{:S(2)}, u32[]{:S(2)}) collective-permute-start(f32[8,128]{1,0:T(8,128)S(1)} %max.18), channel_id=1, source_target_pairs={{0,128},{8,136},{16,144},{24,152},{32,160},{40,168},{48,176},{56,1... | collective-permute-start | bytes 12296 | tf_op jit(solution)/shard_map/ppermute | solution.py:320
  145.8 2.1 %collective-permute-done.14 = f32[8,128]{1,0:T(8,128)S(1)} collective-permute-done((f32[8,128]{1,0:T(8,128)S(1)}, f32[8,128]{1,0:T(8,128)S(1)}, u32[]{:S(2)}, u32[]{:S(2)}) %collective-permute-start.14) | collective-permute-done | bytes 4128 | tf_op jit(solution)/shard_map/ppermute | solution.py:320
  149.1 2.1 %conditional.1 = (f32[256,768]{1,0:T(8,128)S(1)}, f32[8,256]{1,0:T(8,128)S(1)}) conditional(s32[]{:T(128)} %bitcast.11, (f32[96,256]{1,0:T(8,128)S(1)}, f32[96,256]{1,0:T(8,128)S(1)}, f32[96,256]{1,0:T(8,128)S(1)}, f32[96,256]{1,0:T(8,128)S(1)}, f32[96,256]{1,0:T(8,128)S(1)}, /*index=5*/f32[96,256]{1,0:T(8,128)S(1)}, f32[96,256]{1,0:T(8,128)S(1)}, ...), branch_computations={%region_0.1_spmd, %region_1.2_spmd} | conditional | flops 11509366784 | bytes 24660392 | solution.py:331
  (34 shorter events, 7.2 us)
Async XLA Ops:
  1.3 1.1 copy-start
  91.2 1.4 collective-permute-start.15
  92.7 5.6 %collective-permute-start.16 = (f32[32,8,128]{2,1,0:T(8,128)S(1)}, f32[32,8,128]{2,1,0:T(8,128)S(1)}, u32[]{:S(2)}, u32[]{:S(2)}) collective-permute-start(f32[32,8,128]{2,1,0:T(8,128)S(1)} %add.31), channel_id=1, source_target_pairs={{0,2},{1,3},{2,0},{3,1},{4,6},{5,7},{6,4},{7,5},{8,10},{9,11},{10,... | collective-permute-start | bytes 393224 | tf_op jit(solution)/shard_map/ppermute | solution.py:229
  98.3 6.3 %collective-permute-start.17 = (f32[32,8,128]{2,1,0:T(8,128)S(1)}, f32[32,8,128]{2,1,0:T(8,128)S(1)}, u32[]{:S(2)}, u32[]{:S(2)}) collective-permute-start(f32[32,8,128]{2,1,0:T(8,128)S(1)} %add.32), channel_id=1, source_target_pairs={{0,6},{1,7},{2,4},{3,5},{4,2},{5,3},{6,0},{7,1},{8,14},{9,15},{10,... | collective-permute-start | bytes 393224 | tf_op jit(solution)/shard_map/ppermute | solution.py:230
  109.6 39.6 %all-to-all-start.4 = ((f32[32,8,128]{2,1,0:T(8,128)}), f32[32,8,128]{2,1,0:T(8,128)S(1)}, u32[]{:S(2)}, u32[]{:S(2)}) async-start(f32[32,8,128]{2,1,0:T(8,128)} %get-tuple-element.47), calls=%async_computation.4 | async-start | bytes 262144 | tf_op jit(solution)/shard_map/all_to_all | solution.py:271
  115.1 4.7 %collective-permute-start.23 = (f32[96,256]{1,0:T(8,128)S(1)}, f32[96,256]{1,0:T(8,128)S(1)}, u32[]{:S(2)}, u32[]{:S(2)}) collective-permute-start(f32[96,256]{1,0:T(8,128)S(1)} %get-tuple-element.46), channel_id=1, source_target_pairs={{0,6},{1,7},{2,0},{3,1},{4,2},{5,3},{6,4},{7,5},{8,14},{9,15},{10,... | collective-permute-start | bytes 294920 | tf_op jit(solution)/shard_map/ppermute | solution.py:276
  116.4 6.2 %collective-permute-start.21 = (f32[96,256]{1,0:T(8,128)S(1)}, f32[96,256]{1,0:T(8,128)S(1)}, u32[]{:S(2)}, u32[]{:S(2)}) collective-permute-start(f32[96,256]{1,0:T(8,128)S(1)} %get-tuple-element.46), channel_id=1, source_target_pairs={{0,4},{1,5},{2,6},{3,7},{4,0},{5,1},{6,2},{7,3},{8,12},{9,13},{10,... | collective-permute-start | bytes 294920 | tf_op jit(solution)/shard_map/ppermute | solution.py:276
  116.6 6.9 %collective-permute-start.19 = (f32[96,256]{1,0:T(8,128)S(1)}, f32[96,256]{1,0:T(8,128)S(1)}, u32[]{:S(2)}, u32[]{:S(2)}) collective-permute-start(f32[96,256]{1,0:T(8,128)S(1)} %get-tuple-element.46), channel_id=1, source_target_pairs={{0,2},{1,3},{2,4},{3,5},{4,6},{5,7},{6,0},{7,1},{8,10},{9,11},{10,... | collective-permute-start | bytes 294920 | tf_op jit(solution)/shard_map/ppermute | solution.py:276
  117.3 31.8 %collective-permute-start.18 = (f32[96,256]{1,0:T(8,128)S(1)}, f32[96,256]{1,0:T(8,128)S(1)}, u32[]{:S(2)}, u32[]{:S(2)}) collective-permute-start(f32[96,256]{1,0:T(8,128)S(1)} %get-tuple-element.46), channel_id=1, source_target_pairs={{0,1},{1,0},{2,3},{3,2},{4,5},{5,4},{6,7},{7,6},{8,9},{9,8},{10,11... | collective-permute-start | bytes 294920 | tf_op jit(solution)/shard_map/ppermute | solution.py:277
  119.8 29.3 %collective-permute-start.24 = (f32[96,256]{1,0:T(8,128)S(1)}, f32[96,256]{1,0:T(8,128)S(1)}, u32[]{:S(2)}, u32[]{:S(2)}) collective-permute-start(f32[96,256]{1,0:T(8,128)S(1)} %collective-permute-done.23), channel_id=1, source_target_pairs={{0,1},{1,0},{2,3},{3,2},{4,5},{5,4},{6,7},{7,6},{8,9},{9,8},{10,11... | collective-permute-start | bytes 294920 | tf_op jit(solution)/shard_map/ppermute | solution.py:277
  122.6 26.5 %collective-permute-start.22 = (f32[96,256]{1,0:T(8,128)S(1)}, f32[96,256]{1,0:T(8,128)S(1)}, u32[]{:S(2)}, u32[]{:S(2)}) collective-permute-start(f32[96,256]{1,0:T(8,128)S(1)} %collective-permute-done.21), channel_id=1, source_target_pairs={{0,1},{1,0},{2,3},{3,2},{4,5},{5,4},{6,7},{7,6},{8,9},{9,8},{10,11... | collective-permute-start | bytes 294920 | tf_op jit(solution)/shard_map/ppermute | solution.py:277
  123.5 25.6 %collective-permute-start.20 = (f32[96,256]{1,0:T(8,128)S(1)}, f32[96,256]{1,0:T(8,128)S(1)}, u32[]{:S(2)}, u32[]{:S(2)}) collective-permute-start(f32[96,256]{1,0:T(8,128)S(1)} %collective-permute-done.19), channel_id=1, source_target_pairs={{0,1},{1,0},{2,3},{3,2},{4,5},{5,4},{6,7},{7,6},{8,9},{9,8},{10,11... | collective-permute-start | bytes 294920 | tf_op jit(solution)/shard_map/ppermute | solution.py:277
  123.5 3.6 %collective-permute-start.10 = (f32[8,128]{1,0:T(8,128)S(1)}, f32[8,128]{1,0:T(8,128)S(1)}, u32[]{:S(2)}, u32[]{:S(2)}) collective-permute-start(f32[8,128]{1,0:T(8,128)S(1)} %get-tuple-element.44), channel_id=1, source_target_pairs={{0,8},{8,0},{16,24},{24,16},{32,40},{40,32},{48,56},{56,48},{64,72... | collective-permute-start | bytes 12296 | tf_op jit(solution)/shard_map/ppermute | solution.py:320
  127.2 5.1 %collective-permute-start.11 = (f32[8,128]{1,0:T(8,128)S(1)}, f32[8,128]{1,0:T(8,128)S(1)}, u32[]{:S(2)}, u32[]{:S(2)}) collective-permute-start(f32[8,128]{1,0:T(8,128)S(1)} %max.15), channel_id=1, source_target_pairs={{0,16},{8,24},{16,0},{24,8},{32,48},{40,56},{48,32},{56,40},{64,80... | collective-permute-start | bytes 12296 | tf_op jit(solution)/shard_map/ppermute | solution.py:320
  132.3 3.6 %collective-permute-start.12 = (f32[8,128]{1,0:T(8,128)S(1)}, f32[8,128]{1,0:T(8,128)S(1)}, u32[]{:S(2)}, u32[]{:S(2)}) collective-permute-start(f32[8,128]{1,0:T(8,128)S(1)} %max.16), channel_id=1, source_target_pairs={{0,32},{8,40},{16,48},{24,56},{32,0},{40,8},{48,16},{56,24},{64,96... | collective-permute-start | bytes 12296 | tf_op jit(solution)/shard_map/ppermute | solution.py:320
  135.9 4.5 %collective-permute-start.13 = (f32[8,128]{1,0:T(8,128)S(1)}, f32[8,128]{1,0:T(8,128)S(1)}, u32[]{:S(2)}, u32[]{:S(2)}) collective-permute-start(f32[8,128]{1,0:T(8,128)S(1)} %max.17), channel_id=1, source_target_pairs={{0,64},{8,72},{16,80},{24,88},{32,96},{40,104},{48,112},{56,120},{... | collective-permute-start | bytes 12296 | tf_op jit(solution)/shard_map/ppermute | solution.py:320
  140.4 7.5 %collective-permute-start.14 = (f32[8,128]{1,0:T(8,128)S(1)}, f32[8,128]{1,0:T(8,128)S(1)}, u32[]{:S(2)}, u32[]{:S(2)}) collective-permute-start(f32[8,128]{1,0:T(8,128)S(1)} %max.18), channel_id=1, source_target_pairs={{0,128},{8,136},{16,144},{24,152},{32,160},{40,168},{48,176},{56,1... | collective-permute-start | bytes 12296 | tf_op jit(solution)/shard_map/ppermute | solution.py:320
  151.3 0.9 copy-start.1
  151.3 0.9 copy-start.2

commit v2 on v1

--- a/solution.py
+++ b/solution.py
@@ -52,7 +52,7 @@
         out_ref[part, PART:ROWS, :] = slots
 
 
-def pack_kernel(cap, in_ref, out_ref, target_ref, most_ref, left, column):
+def pack_kernel(cap, in_ref, out_ref, target_ref, left, column):
     groups = OWNERS * cap // PAIR
     before = (iota((VEC, VEC), 0) < iota((VEC, VEC), 1)).astype(F32).astype(BF16)
     carry = jnp.zeros((OWNERS, 1), F32)
@@ -73,7 +73,8 @@
         left[src, PART + 16 : STACK, :] = low
     rows = jnp.concatenate(targets, axis=0)
     target_ref[...] = rows.astype(jnp.int32)
-    most_ref[...] = jnp.broadcast_to(jnp.max(carry, axis=0, keepdims=True), (8, LANES))
+    most = jnp.broadcast_to(jnp.max(carry, axis=0, keepdims=True), (8, LANES))
+    first_row = iota((8, LANES), 0) == 0
     turned = jnp.concatenate([rows, jnp.zeros((LANES - REPS, VEC), F32)], axis=0).T
     for src in range(REPS):
         column[src] = jnp.broadcast_to(turned[:, src : src + 1], (VEC, LANES))
@@ -96,10 +97,12 @@
         for half in range(2):
             cut = slice(half * LANES, (half + 1) * LANES)
             out_ref[2 * n + half, 0:PART, :] = values[:, cut]
-            out_ref[2 * n + half, PART:ROWS, :] = total[PART : PART + 8, cut]
+            out_ref[2 * n + half, PART:ROWS, :] = jnp.where(
+                first_row, total[PART : PART + 8, cut], most
+            )
         return 0
 
-    lax.fori_loop(0, groups, group, 0)
+    lax.fori_loop(0, groups, group, 0, unroll=2)
 
 
 def load_pair(x_ref, n):
@@ -115,8 +118,9 @@
     return jnp.concatenate([high, jnp.ones((16, PAIR), BF16), low], axis=0)
 
 
-def distance_kernel(blocks, x_ref, out_ref, total):
+def distance_kernel(blocks, x_ref, out_ref, most_ref, total, scaled):
     total[...] = jnp.zeros_like(total)
+    most_ref[...] = jnp.max(x_ref[:, PART:ROWS, :], axis=0)
 
     def add(n, _):
         x, slot = load_pair(x_ref, n)
@@ -124,34 +128,38 @@
         total[...] += lax.dot_general(stack_of(x), hot, NT, preferred_element_type=F32)
         return 0
 
-    lax.fori_loop(0, blocks // 2, add, 0)
+    lax.fori_loop(0, blocks // 2, add, 0, unroll=2)
     sums = total[0:PART, :] + total[PART + 16 : STACK, :]
     counts = total[PART : PART + 8, :]
-    first = sums / (counts[0:1] + 1.0)
-    turned = jnp.concatenate(
-        [first, counts, jnp.zeros((LANES - PART - 8, SLOTS), F32)], axis=0
-    ).T
-    center = turned[:, 0:PART]
-    count = turned[:, PART : PART + 1].reshape(PAR_DEV, K, 1)
+    high, low = parts_of(sums / (counts[0:1] + 1.0))
+    high, low = high.astype(F32), low.astype(F32)
+    first = high + low
+    turned = jnp.concatenate([high, high, low, low], axis=0).T
+    scaled[0:SLOTS, :] = (turned[:, 0 : 2 * PART] * -2.0).astype(BF16)
+    scaled[SLOTS:, :] = (turned[:, 2 * PART : 4 * PART] * -2.0).astype(BF16)
+    own = jnp.broadcast_to(jnp.sum(first * first, axis=0, keepdims=True), (LANES, SLOTS))
+    row = iota((LANES, SLOTS), 0)
+    columns = jnp.where(row == 0, jnp.broadcast_to(counts[0:1], (LANES, SLOTS)), own).T
+    count = columns[:, 0:1].reshape(PAR_DEV, K, 1)
     mean = jnp.sum(count, axis=1, keepdims=True) / K
     extra = (0.5 * count / (mean + 1.0)).reshape(SLOTS, 1) / REPS
-    own = jnp.sum(center * center, axis=1, keepdims=True) / D + extra
-    scaled = center * (-2.0 / D)
+    own = columns[:, 1:2]
 
     def measure(n, _):
         x, slot = load_pair(x_ref, n)
-        cross = jnp.dot(
-            scaled, x, precision=lax.Precision.HIGHEST, preferred_element_type=F32
+        both = jnp.dot(
+            scaled[...], jnp.concatenate(parts_of(x), axis=0), preferred_element_type=F32
         )
+        cross = both[0:SLOTS] + both[SLOTS : 2 * SLOTS]
         parent = (slot - 1) >> 3
-        terms = (cross + own).reshape(PAR_DEV, K, PAIR)
+        terms = ((cross + own) / D + extra).reshape(PAR_DEV, K, PAIR)
         picked = jnp.where(iota((PAR_DEV, K, PAIR), 0) == parent[None], terms, 0.0)
         part = jnp.sum(picked, axis=0) + jnp.sum(x * x, axis=0, keepdims=True) / D
         out_ref[2 * n] = part[:, 0:LANES]
         out_ref[2 * n + 1] = part[:, LANES:PAIR]
         return 0
 
-    lax.fori_loop(0, blocks // 2, measure, 0)
+    lax.fori_loop(0, blocks // 2, measure, 0, unroll=2)
 
 
 def share_kernel(blocks, x_ref, pen_ref, cent_ref, share_ref, total, rest):
@@ -179,7 +187,7 @@
         )
         return 0
 
-    lax.fori_loop(0, blocks // 2, add, 0)
+    lax.fori_loop(0, blocks // 2, add, 0, unroll=2)
     weighted = total[0:PART, :] + total[PART + 16 : STACK, :] + rest[0:PART, :]
     summed = total[PART : PART + 1, :] + rest[PART : PART + 1, :]
     cent_ref[...] = weighted / (summed + 1.0)
@@ -232,12 +240,11 @@
 
 def refine(cap, got):
     blocks = OWNERS * cap // LANES
-    packed, target, most = pl.pallas_call(
+    packed, target = pl.pallas_call(
         functools.partial(pack_kernel, cap),
         out_shape=(
             shape(blocks, ROWS, LANES),
             shape(REPS, VEC, kind=jnp.int32),
-            shape(8, LANES),
         ),
         scratch_shapes=[pltpu.VMEM((REPS, STACK, VEC), BF16), pltpu.VMEM((REPS, VEC, LANES), F32)],
         compiler_params=params(),
@@ -248,10 +255,13 @@
     rows = lax.all_to_all(
         packed.reshape(OWNERS, per * ROWS, LANES), "cluster", 0, 0, tiled=True
     ).reshape(blocks, ROWS, LANES)
-    partial = pl.pallas_call(
+    partial, most = pl.pallas_call(
         functools.partial(distance_kernel, blocks),
-        out_shape=shape(blocks, K, LANES),
-        scratch_shapes=[pltpu.VMEM((STACK, SLOTS), F32)],
+        out_shape=(shape(blocks, K, LANES), shape(8, LANES)),
+        scratch_shapes=[
+            pltpu.VMEM((STACK, SLOTS), F32),
+            pltpu.VMEM((2 * SLOTS, 2 * PART), BF16),
+        ],
         compiler_params=params(),
         cost_estimate=cost(2 * 8 * PART * SLOTS * OWNERS * cap, 2_000_000),
         name="distance",
@@ -315,11 +325,7 @@
     )(vectors, slot)
     got = lax.all_to_all(turned, "rep", 0, 0, tiled=True)
     pieces, back, target, most = refine(LANES, got)
-    for bit in (1, 2, 4, 8, 16):
-        most = jnp.maximum(
-            most, lax.ppermute(most, "cluster", [(i, i ^ bit) for i in range(OWNERS)])
-        )
-    over = most[0, 0] > LANES
+    over = most[1, 0] > LANES
 
     def wide(got, pieces, back, target):
         pieces, back, target, _ = refine(PAIR, got)

time: 152 us -> 122 us (0.80); the launches traced: 152 us -> 120 us
  waiting for transfers between devices: 30.4 us -> 17.6 us
  starting transfers between devices: 21.3 us -> 9.79 us
  Pallas kernels: 23.9 us -> 16.2 us
    ppermute x5 -> x0, waiting for transfers between devices: 12.8 us -> none  [on_device(): lax.ppermute(most, 'cluster', [(i, i ^ bit) for i in range(OWNERS)])]
    ppermute x5 -> x0, starting transfers between devices: 11.5 us -> none  [on_device(): lax.ppermute(most, 'cluster', [(i, i ^ bit) for i in range(OWNERS)])]
    pallas_call x1, Pallas kernels: 9.63 us -> 5.17 us  [refine(): pl.pallas_call(functools.partial(distance_kernel, blocks), out_shape=(sha...]
    pallas_call x1, Pallas kernels: 4.97 us -> 3.24 us  [refine(): pl.pallas_call(functools.partial(share_kernel, blocks), out_shape=(shape(...]
  transfers between devices with their start and end apart: 16 -> 11, of which waited for: 11 -> 7; matrix products, arithmetic and copies ran while one was open for 0% -> 0% of each run, Pallas kernels for 0% -> 0%
where the time goes in v2:
time: 122 us; the launch traced here: 120 us
  blocking collectives  71.6 us (59%)
  waiting for transfers between devices  17.6 us (14%)
  Pallas kernels  16.2 us (13%)
  starting transfers between devices  9.79 us (8%)
  local copies, waits for them, and re-layouts  2.51 us (2%)
  between operations  1.39 us (1%)
    all_to_all x1, blocking collectives, refine(): lax.all_to_all(packed.reshape(OWNERS, per * ROWS, LANES), 'cluster', 0, 0...  53.5 us
    all_to_all x1, blocking collectives, on_device(): got = lax.all_to_all(turned, 'rep', 0, 0, tiled=True)  18 us
    ppermute x3, waiting for transfers between devices, refine(): mine = lax.ppermute(cent, 'rep', along_x(step)) if step else cent  6.2 us
    pallas_call x1, Pallas kernels, refine(): pl.pallas_call(functools.partial(pack_kernel, cap), out_shape=(shape(bloc...  5.74 us
    all_to_all x1, starting transfers between devices, refine(): lax.all_to_all(share.reshape(OWNERS, per * K, LANES), 'cluster', 0, 0, ti...  5.57 us
    pallas_call x1, Pallas kernels, refine(): pl.pallas_call(functools.partial(distance_kernel, blocks), out_shape=(sha...  5.17 us
    ppermute x1, waiting for transfers between devices, sum_over_rep(): return x + lax.ppermute(x, 'rep', [(i, i ^ 6) for i in range(REPS)])  5 us
    ppermute x1, waiting for transfers between devices, sum_over_rep(): x = x + lax.ppermute(x, 'rep', [(i, i ^ 2) for i in range(REPS)])  4.99 us
  transfers between devices with their start and end apart: 11, of which 7 were waited for; matrix products, arithmetic and copies ran while one was open for 0% of the time, Pallas kernels for 0%

profile of v2, /device:TPU:8, one launch (start us, length us, event | category | flops | bytes accessed | tf_op | source)
XLA Modules:
  0.0 120.2 jit_solution(11833165228023789623)
XLA Ops:
  0.6 0.7 add_convert_fusion
  1.3 1.1 copy-done
  2.5 0.3 turn.1
  2.7 18.0 %all_to_all.27.in_ref = f32[8,104,256]{2,1,0:T(8,128)S(1)} all-to-all(f32[8,104,256]{2,1,0:T(8,128)S(1)} %turn.1), channel_id=1, replica_groups=mesh['cluster'=32,'rep'=8] {'rep'}, dimensions={0} | all-to-all | bytes 1703936 | tf_op jit(solution)/shard_map/all_to_all | solution.py:326
  20.8 5.7 %pack.3 = (f32[32,104,128]{2,1,0:T(8,128)S(1)}, s32[8,256]{1,0:T(8,128)S(1)}) custom-call(f32[8,104,256]{2,1,0:T(8,128)S(1)} %all_to_all.27.in_ref), custom_call_target="tpu_custom_call" | custom-call | flops 3489660928 | bytes 3000000 | tf_op jit(solution)/shard_map/pack/pallas_call | solution.py:243
  26.5 53.5 %all_to_all.28.x_ref = f32[32,104,128]{2,1,0:T(8,128)S(1)} all-to-all(f32[32,104,128]{2,1,0:T(8,128)S(1)} %get-tuple-element.46), channel_id=1, replica_groups=mesh['cluster'=32,'rep'=8] {'cluster'}, dimensions={0} | all-to-all | bytes 3407872 | tf_op jit(solution)/shard_map/all_to_all | solution.py:255
  80.1 5.2 %distance.3 = (f32[32,8,128]{2,1,0:T(8,128)S(1)}, f32[8,128]{1,0:T(8,128)S(1)}) custom-call(f32[32,104,128]{2,1,0:T(8,128)S(1)} %all_to_all.28.x_ref), custom_call_target="tpu_custom_call" | custom-call | flops 1610612736 | bytes 2000000 | tf_op jit(solution)/shard_map/distance/pallas_call | solution.py:258
  85.4 1.3 %collective-permute-done.10 = f32[32,8,128]{2,1,0:T(8,128)S(1)} collective-permute-done((f32[32,8,128]{2,1,0:T(8,128)S(1)}, f32[32,8,128]{2,1,0:T(8,128)S(1)}, u32[]{:S(2)}, u32[]{:S(2)}) %collective-permute-start.10) | collective-permute-done | bytes 131104 | tf_op jit(solution)/shard_map/ppermute | solution.py:236
  86.7 0.6 collective-permute-start.11
  87.4 5.0 %collective-permute-done.11 = f32[32,8,128]{2,1,0:T(8,128)S(1)} collective-permute-done((f32[32,8,128]{2,1,0:T(8,128)S(1)}, f32[32,8,128]{2,1,0:T(8,128)S(1)}, u32[]{:S(2)}, u32[]{:S(2)}) %collective-permute-start.11) | collective-permute-done | bytes 131104 | tf_op jit(solution)/shard_map/ppermute | solution.py:237
  92.4 1.3 %collective-permute-start.12 = (f32[32,8,128]{2,1,0:T(8,128)S(1)}, f32[32,8,128]{2,1,0:T(8,128)S(1)}, u32[]{:S(2)}, u32[]{:S(2)}) collective-permute-start(f32[32,8,128]{2,1,0:T(8,128)S(1)} %add.32), channel_id=1, source_target_pairs={{0,6},{1,7},{2,4},{3,5},{4,2},{5,3},{6,0},{7,1},{8,14},{9,15},{10,... | collective-permute-start | bytes 393224 | tf_op jit(solution)/shard_map/ppermute | solution.py:238
  93.6 5.0 %collective-permute-done.12 = f32[32,8,128]{2,1,0:T(8,128)S(1)} collective-permute-done((f32[32,8,128]{2,1,0:T(8,128)S(1)}, f32[32,8,128]{2,1,0:T(8,128)S(1)}, u32[]{:S(2)}, u32[]{:S(2)}) %collective-permute-start.12) | collective-permute-done | bytes 131104 | tf_op jit(solution)/shard_map/ppermute | solution.py:238
  98.6 3.2 %share.3 = (f32[96,256]{1,0:T(8,128)S(1)}, f32[32,8,128]{2,1,0:T(8,128)}) custom-call(f32[32,104,128]{2,1,0:T(8,128)S(1)} %all_to_all.28.x_ref, f32[32,8,128]{2,1,0:T(8,128)S(1)} %add.33.pen_ref), custom_call_target="tpu_custom_call" | custom-call | flops 603979776 | bytes 2000000 | tf_op jit(solution)/shard_map/share/pallas_call | solution.py:270
  101.9 5.6 %all-to-all-start.4 = ((f32[32,8,128]{2,1,0:T(8,128)}), f32[32,8,128]{2,1,0:T(8,128)S(1)}, u32[]{:S(2)}, u32[]{:S(2)}) async-start(f32[32,8,128]{2,1,0:T(8,128)} %get-tuple-element.50), calls=%async_computation.4 | async-start | bytes 262144 | tf_op jit(solution)/shard_map/all_to_all | solution.py:281
  107.5 1.3 %collective-permute-start.18 = (f32[96,256]{1,0:T(8,128)S(1)}, f32[96,256]{1,0:T(8,128)S(1)}, u32[]{:S(2)}, u32[]{:S(2)}) collective-permute-start(f32[96,256]{1,0:T(8,128)S(1)} %get-tuple-element.49), channel_id=1, source_target_pairs={{0,6},{1,7},{2,0},{3,1},{4,2},{5,3},{6,4},{7,5},{8,14},{9,15},{10,... | collective-permute-start | bytes 294920 | tf_op jit(solution)/shard_map/ppermute | solution.py:286
  109.0 0.7 collective-permute-start.14
  109.7 2.5 %collective-permute-done.18 = f32[96,256]{1,0:T(8,128)S(1)} collective-permute-done((f32[96,256]{1,0:T(8,128)S(1)}, f32[96,256]{1,0:T(8,128)S(1)}, u32[]{:S(2)}, u32[]{:S(2)}) %collective-permute-start.18) | collective-permute-done | bytes 98336 | tf_op jit(solution)/shard_map/ppermute | solution.py:286
  112.2 2.8 %collective-permute-done.16 = f32[96,256]{1,0:T(8,128)S(1)} collective-permute-done((f32[96,256]{1,0:T(8,128)S(1)}, f32[96,256]{1,0:T(8,128)S(1)}, u32[]{:S(2)}, u32[]{:S(2)}) %collective-permute-start.16) | collective-permute-done | bytes 98336 | tf_op jit(solution)/shard_map/ppermute | solution.py:286
  114.9 0.9 collective-permute-done.14
  115.9 0.5 slice.3
  117.2 2.1 %conditional.1 = (f32[256,768]{1,0:T(8,128)S(1)}, f32[8,256]{1,0:T(8,128)S(1)}) conditional(s32[]{:T(128)} %bitcast.11, (f32[96,256]{1,0:T(8,128)S(1)}, f32[96,256]{1,0:T(8,128)S(1)}, f32[96,256]{1,0:T(8,128)S(1)}, f32[96,256]{1,0:T(8,128)S(1)}, f32[96,256]{1,0:T(8,128)S(1)}, /*index=5*/f32[96,256]{1,0:T(8,128)S(1)}, f32[96,256]{1,0:T(8,128)S(1)}, ...), branch_computations={%region_0.1_spmd, %region_1.2_spmd} | conditional | flops 11509366784 | bytes 24660392 | solution.py:337
  117.3 0.9 join.2
  118.1 1.0 take.2
  119.4 0.9 copy-done.1
  (19 shorter events, 0.6 us)
Async XLA Ops:
  1.3 1.1 copy-start
  85.3 1.4 %collective-permute-start.10 = (f32[32,8,128]{2,1,0:T(8,128)S(1)}, f32[32,8,128]{2,1,0:T(8,128)S(1)}, u32[]{:S(2)}, u32[]{:S(2)}) collective-permute-start(f32[32,8,128]{2,1,0:T(8,128)S(1)} %get-tuple-element.48), channel_id=1, source_target_pairs={{0,1},{1,0},{2,3},{3,2},{4,5},{5,4},{6,7},{7,6},{8,9},{9,8},{10,11... | collective-permute-start | bytes 393224 | tf_op jit(solution)/shard_map/ppermute | solution.py:236
  86.7 5.6 %collective-permute-start.11 = (f32[32,8,128]{2,1,0:T(8,128)S(1)}, f32[32,8,128]{2,1,0:T(8,128)S(1)}, u32[]{:S(2)}, u32[]{:S(2)}) collective-permute-start(f32[32,8,128]{2,1,0:T(8,128)S(1)} %add.31), channel_id=1, source_target_pairs={{0,2},{1,3},{2,0},{3,1},{4,6},{5,7},{6,4},{7,5},{8,10},{9,11},{10,... | collective-permute-start | bytes 393224 | tf_op jit(solution)/shard_map/ppermute | solution.py:237
  92.4 6.3 %collective-permute-start.12 = (f32[32,8,128]{2,1,0:T(8,128)S(1)}, f32[32,8,128]{2,1,0:T(8,128)S(1)}, u32[]{:S(2)}, u32[]{:S(2)}) collective-permute-start(f32[32,8,128]{2,1,0:T(8,128)S(1)} %add.32), channel_id=1, source_target_pairs={{0,6},{1,7},{2,4},{3,5},{4,2},{5,3},{6,0},{7,1},{8,14},{9,15},{10,... | collective-permute-start | bytes 393224 | tf_op jit(solution)/shard_map/ppermute | solution.py:238
  101.9 15.3 %all-to-all-start.4 = ((f32[32,8,128]{2,1,0:T(8,128)}), f32[32,8,128]{2,1,0:T(8,128)S(1)}, u32[]{:S(2)}, u32[]{:S(2)}) async-start(f32[32,8,128]{2,1,0:T(8,128)} %get-tuple-element.50), calls=%async_computation.4 | async-start | bytes 262144 | tf_op jit(solution)/shard_map/all_to_all | solution.py:281
  107.5 4.7 %collective-permute-start.18 = (f32[96,256]{1,0:T(8,128)S(1)}, f32[96,256]{1,0:T(8,128)S(1)}, u32[]{:S(2)}, u32[]{:S(2)}) collective-permute-start(f32[96,256]{1,0:T(8,128)S(1)} %get-tuple-element.49), channel_id=1, source_target_pairs={{0,6},{1,7},{2,0},{3,1},{4,2},{5,3},{6,4},{7,5},{8,14},{9,15},{10,... | collective-permute-start | bytes 294920 | tf_op jit(solution)/shard_map/ppermute | solution.py:286
  108.7 6.2 %collective-permute-start.16 = (f32[96,256]{1,0:T(8,128)S(1)}, f32[96,256]{1,0:T(8,128)S(1)}, u32[]{:S(2)}, u32[]{:S(2)}) collective-permute-start(f32[96,256]{1,0:T(8,128)S(1)} %get-tuple-element.49), channel_id=1, source_target_pairs={{0,4},{1,5},{2,6},{3,7},{4,0},{5,1},{6,2},{7,3},{8,12},{9,13},{10,... | collective-permute-start | bytes 294920 | tf_op jit(solution)/shard_map/ppermute | solution.py:286
  109.0 6.9 %collective-permute-start.14 = (f32[96,256]{1,0:T(8,128)S(1)}, f32[96,256]{1,0:T(8,128)S(1)}, u32[]{:S(2)}, u32[]{:S(2)}) collective-permute-start(f32[96,256]{1,0:T(8,128)S(1)} %get-tuple-element.49), channel_id=1, source_target_pairs={{0,2},{1,3},{2,4},{3,5},{4,6},{5,7},{6,0},{7,1},{8,10},{9,11},{10,... | collective-permute-start | bytes 294920 | tf_op jit(solution)/shard_map/ppermute | solution.py:286
  109.7 7.4 %collective-permute-start.13 = (f32[96,256]{1,0:T(8,128)S(1)}, f32[96,256]{1,0:T(8,128)S(1)}, u32[]{:S(2)}, u32[]{:S(2)}) collective-permute-start(f32[96,256]{1,0:T(8,128)S(1)} %get-tuple-element.49), channel_id=1, source_target_pairs={{0,1},{1,0},{2,3},{3,2},{4,5},{5,4},{6,7},{7,6},{8,9},{9,8},{10,11... | collective-permute-start | bytes 294920 | tf_op jit(solution)/shard_map/ppermute | solution.py:287
  112.2 4.9 %collective-permute-start.19 = (f32[96,256]{1,0:T(8,128)S(1)}, f32[96,256]{1,0:T(8,128)S(1)}, u32[]{:S(2)}, u32[]{:S(2)}) collective-permute-start(f32[96,256]{1,0:T(8,128)S(1)} %collective-permute-done.18), channel_id=1, source_target_pairs={{0,1},{1,0},{2,3},{3,2},{4,5},{5,4},{6,7},{7,6},{8,9},{9,8},{10,11... | collective-permute-start | bytes 294920 | tf_op jit(solution)/shard_map/ppermute | solution.py:287
  114.9 2.1 %collective-permute-start.17 = (f32[96,256]{1,0:T(8,128)S(1)}, f32[96,256]{1,0:T(8,128)S(1)}, u32[]{:S(2)}, u32[]{:S(2)}) collective-permute-start(f32[96,256]{1,0:T(8,128)S(1)} %collective-permute-done.16), channel_id=1, source_target_pairs={{0,1},{1,0},{2,3},{3,2},{4,5},{5,4},{6,7},{7,6},{8,9},{9,8},{10,11... | collective-permute-start | bytes 294920 | tf_op jit(solution)/shard_map/ppermute | solution.py:287
  115.9 1.3 %collective-permute-start.15 = (f32[96,256]{1,0:T(8,128)S(1)}, f32[96,256]{1,0:T(8,128)S(1)}, u32[]{:S(2)}, u32[]{:S(2)}) collective-permute-start(f32[96,256]{1,0:T(8,128)S(1)} %collective-permute-done.14), channel_id=1, source_target_pairs={{0,1},{1,0},{2,3},{3,2},{4,5},{5,4},{6,7},{7,6},{8,9},{9,8},{10,11... | collective-permute-start | bytes 294920 | tf_op jit(solution)/shard_map/ppermute | solution.py:287
  119.3 0.9 copy-start.1
  119.4 0.9 copy-start.2

commit v3 on v2

--- a/solution.py
+++ b/solution.py
@@ -37,7 +37,7 @@
     return high, (x - high.astype(F32)).astype(BF16)
 
 
-def turn_kernel(v_ref, g_ref, out_ref):
+def turn_kernel(v_ref, parent_ref, child_ref, out_ref):
     for tile in range(D // LANES):
         turned = v_ref[:, tile * LANES : (tile + 1) * LANES].T
         start = tile * LANES
@@ -47,12 +47,13 @@
             at = start - tile * LANES
             out_ref[part, row : row + size, :] = turned[at : at + size, :]
             start += size
-    slots = jnp.broadcast_to(g_ref[...], (ROWS - PART, VEC))
+    slot = (parent_ref[...] * K + child_ref[...]).astype(F32)
+    slots = jnp.broadcast_to(slot, (ROWS - PART, VEC))
     for part in range(REPS):
         out_ref[part, PART:ROWS, :] = slots
 
 
-def pack_kernel(cap, in_ref, out_ref, target_ref, left, column):
+def pack_kernel(cap, in_ref, out_ref, target_ref, left, hot, group_of):
     groups = OWNERS * cap // PAIR
     before = (iota((VEC, VEC), 0) < iota((VEC, VEC), 1)).astype(F32).astype(BF16)
     carry = jnp.zeros((OWNERS, 1), F32)
@@ -61,38 +62,34 @@
         slot = in_ref[src, PART : PART + 1, :].astype(jnp.int32)
         owner = slot >> 8
         local = (slot & (SLOTS - 1)) + 1
-        hot = (owner == iota((OWNERS, VEC), 0)).astype(F32)
-        ahead = jnp.dot(hot.astype(BF16), before, preferred_element_type=F32) + carry
-        position = jnp.sum(hot * ahead, axis=0, keepdims=True)
-        carry = carry + jnp.sum(hot, axis=1, keepdims=True)
-        target = owner.astype(F32) * cap + position
-        targets.append(jnp.where(position < cap, target, -1.0))
+        mine = (owner == iota((OWNERS, VEC), 0)).astype(F32)
+        ahead = jnp.dot(mine.astype(BF16), before, preferred_element_type=F32) + carry
+        position = jnp.sum(mine * ahead, axis=0, keepdims=True)
+        carry = carry + jnp.sum(mine, axis=1, keepdims=True)
+        target = owner * cap + position.astype(jnp.int32)
+        target = jnp.where(position < cap, target, -1)
+        targets.append(target)
+        group_of[src] = jnp.broadcast_to(target >> 8, (16, VEC))
         high, low = parts_of(in_ref[src, 0:PART, :])
         left[src, 0:PART, :] = high
         left[src, PART : PART + 16, :] = jnp.broadcast_to(local.astype(F32), (16, VEC)).astype(BF16)
         left[src, PART + 16 : STACK, :] = low
     rows = jnp.concatenate(targets, axis=0)
-    target_ref[...] = rows.astype(jnp.int32)
+    target_ref[...] = rows
     most = jnp.broadcast_to(jnp.max(carry, axis=0, keepdims=True), (8, LANES))
     first_row = iota((8, LANES), 0) == 0
-    turned = jnp.concatenate([rows, jnp.zeros((LANES - REPS, VEC), F32)], axis=0).T
+    inside = (rows & (PAIR - 1)).astype(F32)
+    turned = jnp.concatenate([inside, jnp.zeros((LANES - REPS, VEC), F32)], axis=0).T
+    lane = iota((VEC, PAIR), 1).astype(F32)
     for src in range(REPS):
-        column[src] = jnp.broadcast_to(turned[:, src : src + 1], (VEC, LANES))
-    lane = iota((VEC, LANES), 1).astype(F32)
+        hot[src] = jnp.where(turned[:, src : src + 1] == lane, 1.0, 0.0).astype(BF16)
 
     def group(n, _):
-        base = (n * PAIR).astype(F32)
         total = jnp.zeros((STACK, PAIR), F32)
         for src in range(REPS):
-            at = column[src] - base
-            hot = jnp.concatenate(
-                [
-                    jnp.where(at == lane, 1.0, 0.0).astype(BF16),
-                    jnp.where(at == lane + LANES, 1.0, 0.0).astype(BF16),
-                ],
-                axis=1,
-            )
-            total = total + jnp.dot(left[src], hot, preferred_element_type=F32)
+            keep = jnp.where(group_of[src] == n, 1.0, 0.0).astype(BF16)
+            kept = left[src] * jnp.concatenate([keep] * (STACK // 16), axis=0)
+            total = total + jnp.dot(kept, hot[src], preferred_element_type=F32)
         values = total[0:PART] + total[PART + 16 : STACK]
         for half in range(2):
             cut = slice(half * LANES, (half + 1) * LANES)
@@ -120,7 +117,7 @@
 
 def distance_kernel(blocks, x_ref, out_ref, most_ref, total, scaled):
     total[...] = jnp.zeros_like(total)
-    most_ref[...] = jnp.max(x_ref[:, PART:ROWS, :], axis=0)
+    most_ref[0] = jnp.max(x_ref[:, PART + 1, :]).astype(jnp.int32)
 
     def add(n, _):
         x, slot = load_pair(x_ref, n)
@@ -193,13 +190,12 @@
     cent_ref[...] = weighted / (summed + 1.0)
 
 
-def join_kernel(at_ref, *refs):
-    *pieces, out_ref, whole = refs
+def join_kernel(at_ref, own_ref, other_ref, out_ref, whole):
     x, core = at_ref[0], at_ref[1]
-    for index, piece in enumerate(pieces):
-        step, other = divmod(index, 2)
-        where = ((x - step) & 3) * 2 + (core ^ other)
-        whole[pl.ds(pl.multiple_of(where * PART, 8), PART), :] = piece[...]
+    for other, piece in enumerate((own_ref, other_ref)):
+        for step in range(4):
+            where = ((x - step) & 3) * 2 + (core ^ other)
+            whole[pl.ds(pl.multiple_of(where * PART, 8), PART), :] = piece[step]
     for tile in range(D // LANES):
         cut = slice(tile * LANES, (tile + 1) * LANES)
         out_ref[:, cut] = whole[cut, :].T
@@ -238,6 +234,10 @@
     return x + lax.ppermute(x, "rep", [(i, i ^ 6) for i in range(REPS)])
 
 
+SMEM = pl.BlockSpec(memory_space=pltpu.SMEM)
+VMEM = pl.BlockSpec(memory_space=pltpu.VMEM)
+
+
 def refine(cap, got):
     blocks = OWNERS * cap // LANES
     packed, target = pl.pallas_call(
@@ -246,7 +246,11 @@
             shape(blocks, ROWS, LANES),
             shape(REPS, VEC, kind=jnp.int32),
         ),
-        scratch_shapes=[pltpu.VMEM((REPS, STACK, VEC), BF16), pltpu.VMEM((REPS, VEC, LANES), F32)],
+        scratch_shapes=[
+            pltpu.VMEM((REPS, STACK, VEC), BF16),
+            pltpu.VMEM((REPS, VEC, PAIR), BF16),
+            pltpu.VMEM((REPS, 16, VEC), jnp.int32),
+        ],
         compiler_params=params(),
         cost_estimate=cost(2 * STACK * 2048 * OWNERS * cap, 3_000_000),
         name="pack",
@@ -257,7 +261,8 @@
     ).reshape(blocks, ROWS, LANES)
     partial, most = pl.pallas_call(
         functools.partial(distance_kernel, blocks),
-        out_shape=(shape(blocks, K, LANES), shape(8, LANES)),
+        out_shape=(shape(blocks, K, LANES), shape(1, kind=jnp.int32)),
+        out_specs=(VMEM, SMEM),
         scratch_shapes=[
             pltpu.VMEM((STACK, SLOTS), F32),
             pltpu.VMEM((2 * SLOTS, 2 * PART), BF16),
@@ -281,60 +286,62 @@
     back = lax.all_to_all(
         share.reshape(OWNERS, per * K, LANES), "cluster", 0, 0, tiled=True
     ).reshape(blocks, K, LANES)
-    pieces = []
-    for step in range(4):
-        mine = lax.ppermute(cent, "rep", along_x(step)) if step else cent
-        pieces += [mine, lax.ppermute(mine, "rep", CORES)]
+    line = jnp.stack([cent] + [lax.ppermute(cent, "rep", along_x(step)) for step in (1, 2, 3)])
+    pieces = [line, lax.ppermute(line, "rep", CORES)]
     return pieces, back, target, most
 
 
-def finish(cap, pieces, back, target):
-    blocks = OWNERS * cap // LANES
+def place():
     rep = lax.axis_index("rep")
-    at = jnp.stack([rep // 2, rep % 2, rep]).astype(jnp.int32)
-    smem = pl.BlockSpec(memory_space=pltpu.SMEM)
-    vmem = pl.BlockSpec(memory_space=pltpu.VMEM)
-    centroids = pl.pallas_call(
+    return jnp.stack([rep // 2, rep % 2, rep]).astype(jnp.int32)
+
+
+def join(pieces):
+    return pl.pallas_call(
         join_kernel,
         out_shape=shape(SLOTS, D),
-        in_specs=[smem] + [vmem] * REPS,
+        in_specs=[SMEM, VMEM, VMEM],
         scratch_shapes=[pltpu.VMEM((D, SLOTS), F32)],
         compiler_params=params(),
         cost_estimate=cost(0, 1_600_000),
         name="join",
-    )(at, *pieces)
-    shares = pl.pallas_call(
+    )(place(), *pieces)
+
+
+def take(cap, back, target):
+    blocks = OWNERS * cap // LANES
+    return pl.pallas_call(
         functools.partial(take_kernel, blocks),
         out_shape=shape(K, VEC),
-        in_specs=[smem, vmem, vmem],
+        in_specs=[SMEM, VMEM, VMEM],
         compiler_params=params(),
         cost_estimate=cost(2 * 24 * VEC * OWNERS * cap, 200_000),
         name="take",
-    )(at, back, target)
-    return centroids, shares
+    )(place(), back, target)
 
 
 def on_device(vectors, parent_id, child_id):
-    slot = (parent_id * K + child_id).astype(F32).reshape(1, VEC)
     turned = pl.pallas_call(
         turn_kernel,
         out_shape=shape(REPS, ROWS, VEC),
         compiler_params=params(),
         cost_estimate=cost(0, 1_600_000),
         name="turn",
-    )(vectors, slot)
+    )(vectors, parent_id.reshape(1, VEC), child_id.reshape(1, VEC))
     got = lax.all_to_all(turned, "rep", 0, 0, tiled=True)
     pieces, back, target, most = refine(LANES, got)
-    over = most[1, 0] > LANES
-
-    def wide(got, pieces, back, target):
+    over = most[0] > LANES
+
+    picked = take(LANES, back, target)
+
+    def wide(got, pieces, picked):
         pieces, back, target, _ = refine(PAIR, got)
-        return finish(PAIR, pieces, back, target)
-
-    def narrow(got, pieces, back, target):
-        return finish(LANES, pieces, back, target)
-
-    centroids, shares = lax.cond(over, wide, narrow, got, pieces, back, target)
+        return join(pieces), take(PAIR, back, target)
+
+    def narrow(got, pieces, picked):
+        return join(pieces), picked
+
+    centroids, shares = lax.cond(over, wide, narrow, got, pieces, picked)
     return centroids, shares.T
 
 

time: 122 us -> 131 us (1.074)
  waiting for transfers between devices: 17.6 us -> 26.1 us
    all_to_all x1, waiting for transfers between devices: 0.01 us -> 8.41 us  [refine(): lax.all_to_all(share.reshape(OWNERS, per * K, LANES), 'cluster', 0, 0, ti...]
    unnamed x6 -> x10, local copies, waits for them, and re-layouts: 2 us -> 3.35 us
    ppermute x7 -> x4, waiting for transfers between devices: 6.31 us -> 6.31 us  [the longest x3 6.3 us: refine(): lax.ppermute(cent, 'rep', along_x(step))]
  transfers between devices with their start and end apart: 11 -> 8, of which waited for: 7 -> 7; matrix products, arithmetic and copies ran while one was open for 0% -> 0% of each run, Pallas kernels for 0% -> 1%
where the time goes in v3:
time: 131 us; the launch traced here: 129 us
  blocking collectives  71.6 us (55%)
  waiting for transfers between devices  26.1 us (20%)
  Pallas kernels  16.5 us (13%)
  starting transfers between devices  9.69 us (7%)
  local copies, waits for them, and re-layouts  3.35 us (3%)
  between operations  1.42 us (1%)
    all_to_all x1, blocking collectives, refine(): lax.all_to_all(packed.reshape(OWNERS, per * ROWS, LANES), 'cluster', 0, 0...  53.5 us
    all_to_all x1, blocking collectives, on_device(): got = lax.all_to_all(turned, 'rep', 0, 0, tiled=True)  18 us
    all_to_all x1, waiting for transfers between devices, refine(): lax.all_to_all(share.reshape(OWNERS, per * K, LANES), 'cluster', 0, 0, ti...  8.41 us
    ppermute x3, waiting for transfers between devices, refine(): lax.ppermute(cent, 'rep', along_x(step))  6.3 us
    pallas_call x1, Pallas kernels, refine(): pl.pallas_call(functools.partial(pack_kernel, cap), out_shape=(shape(bloc...  5.75 us
    all_to_all x1, starting transfers between devices, refine(): lax.all_to_all(share.reshape(OWNERS, per * K, LANES), 'cluster', 0, 0, ti...  5.58 us
    pallas_call x1, Pallas kernels, refine(): pl.pallas_call(functools.partial(distance_kernel, blocks), out_shape=(sha...  5.46 us
    ppermute x1, waiting for transfers between devices, sum_over_rep(): return x + lax.ppermute(x, 'rep', [(i, i ^ 6) for i in range(REPS)])  5.02 us
  transfers between devices with their start and end apart: 8, of which 7 were waited for; matrix products, arithmetic and copies ran while one was open for 0% of the time, Pallas kernels for 1%

profile of v3, /device:TPU:8, one launch (start us, length us, event | category | flops | bytes accessed | tf_op | source)
XLA Modules:
  0.0 129.1 jit_solution(1907574486981200634)
XLA Ops:
  0.6 1.1 copy-done
  1.8 0.7 copy-done.1
  2.4 0.7 copy-done.2
  3.4 18.0 %all_to_all.27.in_ref = f32[8,104,256]{2,1,0:T(8,128)S(1)} all-to-all(f32[8,104,256]{2,1,0:T(8,128)S(1)} %turn.1), channel_id=1, replica_groups=mesh['cluster'=32,'rep'=8] {'rep'}, dimensions={0} | all-to-all | bytes 1703936 | tf_op jit(solution)/shard_map/all_to_all | solution.py:331
  21.4 5.7 %pack.3 = (f32[32,104,128]{2,1,0:T(8,128)S(1)}, s32[8,256]{1,0:T(8,128)S(1)}) custom-call(f32[8,104,256]{2,1,0:T(8,128)S(1)} %all_to_all.27.in_ref), custom_call_target="tpu_custom_call" | custom-call | flops 3489660928 | bytes 3000000 | tf_op jit(solution)/shard_map/pack/pallas_call | solution.py:243
  27.2 53.5 %all_to_all.28.x_ref = f32[32,104,128]{2,1,0:T(8,128)S(1)} all-to-all(f32[32,104,128]{2,1,0:T(8,128)S(1)} %get-tuple-element.25), channel_id=1, replica_groups=mesh['cluster'=32,'rep'=8] {'cluster'}, dimensions={0} | all-to-all | bytes 3407872 | tf_op jit(solution)/shard_map/all_to_all | solution.py:259
  80.7 5.5 %distance.3 = (f32[32,8,128]{2,1,0:T(8,128)S(1)}, s32[1]{0:T(128)}) custom-call(f32[32,104,128]{2,1,0:T(8,128)S(1)} %all_to_all.28.x_ref), custom_call_target="tpu_custom_call" | custom-call | flops 1610612736 | bytes 2000000 | tf_op jit(solution)/shard_map/distance/pallas_call | solution.py:262
  86.3 1.3 %collective-permute-done.7 = f32[32,8,128]{2,1,0:T(8,128)S(1)} collective-permute-done((f32[32,8,128]{2,1,0:T(8,128)S(1)}, f32[32,8,128]{2,1,0:T(8,128)S(1)}, u32[]{:S(2)}, u32[]{:S(2)}) %collective-permute-start.7) | collective-permute-done | bytes 131104 | tf_op jit(solution)/shard_map/ppermute | solution.py:232
  87.7 0.6 collective-permute-start.8
  88.3 5.0 %collective-permute-done.8 = f32[32,8,128]{2,1,0:T(8,128)S(1)} collective-permute-done((f32[32,8,128]{2,1,0:T(8,128)S(1)}, f32[32,8,128]{2,1,0:T(8,128)S(1)}, u32[]{:S(2)}, u32[]{:S(2)}) %collective-permute-start.8) | collective-permute-done | bytes 131104 | tf_op jit(solution)/shard_map/ppermute | solution.py:233
  93.3 1.2 collective-permute-start.9
  94.6 5.0 %collective-permute-done.9 = f32[32,8,128]{2,1,0:T(8,128)S(1)} collective-permute-done((f32[32,8,128]{2,1,0:T(8,128)S(1)}, f32[32,8,128]{2,1,0:T(8,128)S(1)}, u32[]{:S(2)}, u32[]{:S(2)}) %collective-permute-start.9) | collective-permute-done | bytes 131104 | tf_op jit(solution)/shard_map/ppermute | solution.py:234
  99.6 3.2 %share.3 = (f32[96,256]{1,0:T(8,128)S(1)}, f32[32,8,128]{2,1,0:T(8,128)}) custom-call(f32[32,104,128]{2,1,0:T(8,128)S(1)} %all_to_all.28.x_ref, f32[32,8,128]{2,1,0:T(8,128)S(1)} %add.34.pen_ref), custom_call_target="tpu_custom_call" | custom-call | flops 603979776 | bytes 2000000 | tf_op jit(solution)/shard_map/share/pallas_call | solution.py:275
  102.8 1.2 collective-permute-start.12
  104.3 0.6 collective-permute-start.10
  104.9 2.6 %collective-permute-done.12 = f32[96,256]{1,0:T(8,128)S(1)} collective-permute-done((f32[96,256]{1,0:T(8,128)S(1)}, f32[96,256]{1,0:T(8,128)S(1)}, u32[]{:S(2)}, u32[]{:S(2)}) %collective-permute-start.12) | collective-permute-done | bytes 98336 | tf_op jit(solution)/shard_map/ppermute | solution.py:289
  107.5 2.8 %collective-permute-done.11 = f32[96,256]{1,0:T(8,128)S(1)} collective-permute-done((f32[96,256]{1,0:T(8,128)S(1)}, f32[96,256]{1,0:T(8,128)S(1)}, u32[]{:S(2)}, u32[]{:S(2)}) %collective-permute-start.11) | collective-permute-done | bytes 98336 | tf_op jit(solution)/shard_map/ppermute | solution.py:289
  110.2 0.9 collective-permute-done.10
  111.3 5.6 %all-to-all-start.4 = ((f32[32,8,128]{2,1,0:T(8,128)}), f32[32,8,128]{2,1,0:T(8,128)S(1)}, u32[]{:S(2)}, u32[]{:S(2)}) async-start(f32[32,8,128]{2,1,0:T(8,128)} %get-tuple-element.29), calls=%async_computation.4 | async-start | bytes 262144 | tf_op jit(solution)/shard_map/all_to_all | solution.py:286
  117.6 8.4 %all-to-all-done.4.back_ref = f32[32,8,128]{2,1,0:T(8,128)S(1)} async-done(((f32[32,8,128]{2,1,0:T(8,128)}), f32[32,8,128]{2,1,0:T(8,128)S(1)}, u32[]{:S(2)}, u32[]{:S(2)}) %all-to-all-start.4) | async-done | bytes 131104 | tf_op jit(solution)/shard_map/all_to_all | solution.py:286
  126.1 1.0 take.3
  127.0 1.2 conditional.1
  127.1 0.9 join.2
  128.3 0.9 copy-done.3
  (17 shorter events, 1.0 us)
Async XLA Ops:
  0.6 1.1 copy-start
  1.8 0.7 copy-start.1
  2.4 0.7 copy-start.2
  86.2 1.4 %collective-permute-start.7 = (f32[32,8,128]{2,1,0:T(8,128)S(1)}, f32[32,8,128]{2,1,0:T(8,128)S(1)}, u32[]{:S(2)}, u32[]{:S(2)}) collective-permute-start(f32[32,8,128]{2,1,0:T(8,128)S(1)} %get-tuple-element.27), channel_id=1, source_target_pairs={{0,1},{1,0},{2,3},{3,2},{4,5},{5,4},{6,7},{7,6},{8,9},{9,8},{10,11... | collective-permute-start | bytes 393224 | tf_op jit(solution)/shard_map/ppermute | solution.py:232
  87.7 5.6 %collective-permute-start.8 = (f32[32,8,128]{2,1,0:T(8,128)S(1)}, f32[32,8,128]{2,1,0:T(8,128)S(1)}, u32[]{:S(2)}, u32[]{:S(2)}) collective-permute-start(f32[32,8,128]{2,1,0:T(8,128)S(1)} %add.32), channel_id=1, source_target_pairs={{0,2},{1,3},{2,0},{3,1},{4,6},{5,7},{6,4},{7,5},{8,10},{9,11},{10,... | collective-permute-start | bytes 393224 | tf_op jit(solution)/shard_map/ppermute | solution.py:233
  93.3 6.3 %collective-permute-start.9 = (f32[32,8,128]{2,1,0:T(8,128)S(1)}, f32[32,8,128]{2,1,0:T(8,128)S(1)}, u32[]{:S(2)}, u32[]{:S(2)}) collective-permute-start(f32[32,8,128]{2,1,0:T(8,128)S(1)} %add.33), channel_id=1, source_target_pairs={{0,6},{1,7},{2,4},{3,5},{4,2},{5,3},{6,0},{7,1},{8,14},{9,15},{10,... | collective-permute-start | bytes 393224 | tf_op jit(solution)/shard_map/ppermute | solution.py:234
  102.8 4.6 %collective-permute-start.12 = (f32[96,256]{1,0:T(8,128)S(1)}, f32[96,256]{1,0:T(8,128)S(1)}, u32[]{:S(2)}, u32[]{:S(2)}) collective-permute-start(f32[96,256]{1,0:T(8,128)S(1)} %get-tuple-element.28), channel_id=1, source_target_pairs={{0,6},{1,7},{2,0},{3,1},{4,2},{5,3},{6,4},{7,5},{8,14},{9,15},{10,... | collective-permute-start | bytes 294920 | tf_op jit(solution)/shard_map/ppermute | solution.py:289
  104.0 6.2 %collective-permute-start.11 = (f32[96,256]{1,0:T(8,128)S(1)}, f32[96,256]{1,0:T(8,128)S(1)}, u32[]{:S(2)}, u32[]{:S(2)}) collective-permute-start(f32[96,256]{1,0:T(8,128)S(1)} %get-tuple-element.28), channel_id=1, source_target_pairs={{0,4},{1,5},{2,6},{3,7},{4,0},{5,1},{6,2},{7,3},{8,12},{9,13},{10,... | collective-permute-start | bytes 294920 | tf_op jit(solution)/shard_map/ppermute | solution.py:289
  104.3 6.9 %collective-permute-start.10 = (f32[96,256]{1,0:T(8,128)S(1)}, f32[96,256]{1,0:T(8,128)S(1)}, u32[]{:S(2)}, u32[]{:S(2)}) collective-permute-start(f32[96,256]{1,0:T(8,128)S(1)} %get-tuple-element.28), channel_id=1, source_target_pairs={{0,2},{1,3},{2,4},{3,5},{4,6},{5,7},{6,0},{7,1},{8,10},{9,11},{10,... | collective-permute-start | bytes 294920 | tf_op jit(solution)/shard_map/ppermute | solution.py:289
  111.2 15.8 %collective-permute-start.13 = (f32[4,96,256]{2,1,0:T(8,128)S(1)}, f32[4,96,256]{2,1,0:T(8,128)S(1)}, u32[]{:S(2)}, u32[]{:S(2)}) collective-permute-start(f32[4,96,256]{2,1,0:T(8,128)S(1)} %pad_maximum_fusion.1), channel_id=1, source_target_pairs={{0,1},{1,0},{2,3},{3,2},{4,5},{5,4},{6,7},{7,6},{8,9},{9,8},{10,11... | collective-permute-start | bytes 1179656 | tf_op jit(solution)/shard_map/ppermute | solution.py:290
  111.3 14.7 %all-to-all-start.4 = ((f32[32,8,128]{2,1,0:T(8,128)}), f32[32,8,128]{2,1,0:T(8,128)S(1)}, u32[]{:S(2)}, u32[]{:S(2)}) async-start(f32[32,8,128]{2,1,0:T(8,128)} %get-tuple-element.29), calls=%async_computation.4 | async-start | bytes 262144 | tf_op jit(solution)/shard_map/all_to_all | solution.py:286
  128.2 0.9 copy-start.3
  128.3 0.9 copy-start.4

commit v4 on v2

--- a/solution.py
+++ b/solution.py
@@ -14,7 +14,9 @@
 SLOTS = PAR_DEV * K
 D = 768
 PART = D // REPS
-ROWS = PART + 8
+EARLY = 32
+LATE = PART - EARLY
+ROWS = EARLY + 8
 VEC = 256
 LANES = 128
 PAIR = 2 * LANES
@@ -37,79 +39,101 @@
     return high, (x - high.astype(F32)).astype(BF16)
 
 
-def turn_kernel(v_ref, g_ref, out_ref):
+def turn_kernel(at_ref, v_ref, slot_ref, early_ref, late_ref):
     for tile in range(D // LANES):
         turned = v_ref[:, tile * LANES : (tile + 1) * LANES].T
-        start = tile * LANES
-        while start < (tile + 1) * LANES:
-            part, row = divmod(start, PART)
-            size = min(PART - row, (tile + 1) * LANES - start)
-            at = start - tile * LANES
-            out_ref[part, row : row + size, :] = turned[at : at + size, :]
-            start += size
-    slots = jnp.broadcast_to(g_ref[...], (ROWS - PART, VEC))
+        for start in range(0, LANES, EARLY):
+            part, row = divmod(tile * LANES + start, PART)
+            piece = turned[start : start + EARLY, :]
+            if row < EARLY:
+                early_ref[part, 0:EARLY, :] = piece
+            else:
+                step = (part - at_ref[2]) & (REPS - 1)
+                late_ref[step, row - EARLY : row, :] = piece
+    slots = jnp.broadcast_to(slot_ref[...], (ROWS - EARLY, VEC))
     for part in range(REPS):
-        out_ref[part, PART:ROWS, :] = slots
-
-
-def pack_kernel(cap, in_ref, out_ref, target_ref, left, column):
-    groups = OWNERS * cap // PAIR
+        early_ref[part, EARLY:ROWS, :] = slots
+
+
+def pack_early_kernel(cap, in_ref, out_ref, target_ref, hot, group_of, left):
     before = (iota((VEC, VEC), 0) < iota((VEC, VEC), 1)).astype(F32).astype(BF16)
     carry = jnp.zeros((OWNERS, 1), F32)
     targets = []
     for src in range(REPS):
-        slot = in_ref[src, PART : PART + 1, :].astype(jnp.int32)
+        slot = in_ref[src, EARLY : EARLY + 1, :].astype(jnp.int32)
         owner = slot >> 8
         local = (slot & (SLOTS - 1)) + 1
-        hot = (owner == iota((OWNERS, VEC), 0)).astype(F32)
-        ahead = jnp.dot(hot.astype(BF16), before, preferred_element_type=F32) + carry
-        position = jnp.sum(hot * ahead, axis=0, keepdims=True)
-        carry = carry + jnp.sum(hot, axis=1, keepdims=True)
-        target = owner.astype(F32) * cap + position
-        targets.append(jnp.where(position < cap, target, -1.0))
-        high, low = parts_of(in_ref[src, 0:PART, :])
-        left[src, 0:PART, :] = high
-        left[src, PART : PART + 16, :] = jnp.broadcast_to(local.astype(F32), (16, VEC)).astype(BF16)
-        left[src, PART + 16 : STACK, :] = low
+        mine = (owner == iota((OWNERS, VEC), 0)).astype(F32)
+        ahead = jnp.dot(mine.astype(BF16), before, preferred_element_type=F32) + carry
+        position = jnp.sum(mine * ahead, axis=0, keepdims=True)
+        carry = carry + jnp.sum(mine, axis=1, keepdims=True)
+        target = owner * cap + position.astype(jnp.int32)
+        target = jnp.where(position < cap, target, -1)
+        targets.append(target)
+        group_of[src] = jnp.broadcast_to(target >> 8, (16, VEC))
+        high, low = parts_of(in_ref[src, 0:EARLY, :])
+        slots = jnp.broadcast_to(local.astype(F32), (16, VEC)).astype(BF16)
+        left[src] = jnp.concatenate([high, low, slots], axis=0)
     rows = jnp.concatenate(targets, axis=0)
-    target_ref[...] = rows.astype(jnp.int32)
+    target_ref[...] = rows
     most = jnp.broadcast_to(jnp.max(carry, axis=0, keepdims=True), (8, LANES))
     first_row = iota((8, LANES), 0) == 0
-    turned = jnp.concatenate([rows, jnp.zeros((LANES - REPS, VEC), F32)], axis=0).T
+    inside = (rows & (PAIR - 1)).astype(F32)
+    turned = jnp.concatenate([inside, jnp.zeros((LANES - REPS, VEC), F32)], axis=0).T
+    lane = iota((VEC, PAIR), 1).astype(F32)
     for src in range(REPS):
-        column[src] = jnp.broadcast_to(turned[:, src : src + 1], (VEC, LANES))
-    lane = iota((VEC, LANES), 1).astype(F32)
+        hot[src] = jnp.where(turned[:, src : src + 1] == lane, 1.0, 0.0).astype(BF16)
 
     def group(n, _):
-        base = (n * PAIR).astype(F32)
-        total = jnp.zeros((STACK, PAIR), F32)
+        total = jnp.zeros((2 * EARLY + 16, PAIR), F32)
         for src in range(REPS):
-            at = column[src] - base
-            hot = jnp.concatenate(
-                [
-                    jnp.where(at == lane, 1.0, 0.0).astype(BF16),
-                    jnp.where(at == lane + LANES, 1.0, 0.0).astype(BF16),
-                ],
-                axis=1,
-            )
-            total = total + jnp.dot(left[src], hot, preferred_element_type=F32)
-        values = total[0:PART] + total[PART + 16 : STACK]
+            total = total + picked(left[src], group_of[src], n, hot[src])
+        values = total[0:EARLY] + total[EARLY : 2 * EARLY]
+        slots = total[2 * EARLY : 2 * EARLY + 8]
         for half in range(2):
             cut = slice(half * LANES, (half + 1) * LANES)
-            out_ref[2 * n + half, 0:PART, :] = values[:, cut]
-            out_ref[2 * n + half, PART:ROWS, :] = jnp.where(
-                first_row, total[PART : PART + 8, cut], most
-            )
-        return 0
-
-    lax.fori_loop(0, groups, group, 0, unroll=2)
-
-
-def load_pair(x_ref, n):
-    x = jnp.concatenate([x_ref[2 * n, 0:PART, :], x_ref[2 * n + 1, 0:PART, :]], axis=1)
-    slot = jnp.concatenate(
-        [x_ref[2 * n, PART : PART + 1, :], x_ref[2 * n + 1, PART : PART + 1, :]], axis=1
+            out_ref[2 * n + half, 0:EARLY, :] = values[:, cut]
+            out_ref[2 * n + half, EARLY:ROWS, :] = jnp.where(first_row, slots[:, cut], most)
+        return 0
+
+    lax.fori_loop(0, OWNERS * cap // PAIR, group, 0, unroll=2)
+
+
+def picked(left, group_of, n, hot):
+    keep = jnp.where(group_of == n, 1.0, 0.0).astype(BF16)
+    kept = left * jnp.concatenate([keep] * (left.shape[0] // 16), axis=0)
+    return jnp.dot(kept, hot, preferred_element_type=F32)
+
+
+def pack_late_kernel(cap, at_ref, hot, group_of, *refs):
+    *in_refs, out_ref, left = refs
+    for step, in_ref in enumerate(in_refs):
+        high, low = parts_of(in_ref[...])
+        left[step] = jnp.concatenate([high, low], axis=0)
+
+    def group(n, _):
+        total = jnp.zeros((2 * LATE, PAIR), F32)
+        for step in range(REPS):
+            src = (at_ref[2] - step) & (REPS - 1)
+            total = total + picked(left[step], group_of[src], n, hot[src])
+        values = total[0:LATE] + total[LATE : 2 * LATE]
+        for half in range(2):
+            out_ref[2 * n + half] = values[:, half * LANES : (half + 1) * LANES]
+        return 0
+
+    lax.fori_loop(0, OWNERS * cap // PAIR, group, 0, unroll=2)
+
+
+def load_pair(early_ref, late_ref, n):
+    pair = (2 * n, 2 * n + 1)
+    x = jnp.concatenate(
+        [
+            jnp.concatenate([early_ref[i, 0:EARLY, :] for i in pair], axis=1),
+            jnp.concatenate([late_ref[i] for i in pair], axis=1),
+        ],
+        axis=0,
     )
+    slot = jnp.concatenate([early_ref[i, EARLY : EARLY + 1, :] for i in pair], axis=1)
     return x, slot.astype(jnp.int32)
 
 
@@ -118,12 +142,12 @@
     return jnp.concatenate([high, jnp.ones((16, PAIR), BF16), low], axis=0)
 
 
-def distance_kernel(blocks, x_ref, out_ref, most_ref, total, scaled):
+def distance_kernel(blocks, early_ref, late_ref, out_ref, most_ref, total, scaled):
     total[...] = jnp.zeros_like(total)
-    most_ref[...] = jnp.max(x_ref[:, PART:ROWS, :], axis=0)
+    most_ref[0] = jnp.max(early_ref[:, EARLY + 1, :]).astype(jnp.int32)
 
     def add(n, _):
-        x, slot = load_pair(x_ref, n)
+        x, slot = load_pair(early_ref, late_ref, n)
         hot = jnp.where(iota((SLOTS, PAIR), 0) + 1 == slot, 1.0, 0.0).astype(BF16)
         total[...] += lax.dot_general(stack_of(x), hot, NT, preferred_element_type=F32)
         return 0
@@ -146,7 +170,7 @@
     own = columns[:, 1:2]
 
     def measure(n, _):
-        x, slot = load_pair(x_ref, n)
+        x, slot = load_pair(early_ref, late_ref, n)
         both = jnp.dot(
             scaled[...], jnp.concatenate(parts_of(x), axis=0), preferred_element_type=F32
         )
@@ -162,12 +186,12 @@
     lax.fori_loop(0, blocks // 2, measure, 0, unroll=2)
 
 
-def share_kernel(blocks, x_ref, pen_ref, cent_ref, share_ref, total, rest):
+def share_kernel(blocks, early_ref, late_ref, pen_ref, cent_ref, share_ref, total, rest):
     total[...] = jnp.zeros_like(total)
     rest[...] = jnp.zeros_like(rest)
 
     def add(n, _):
-        x, slot = load_pair(x_ref, n)
+        x, slot = load_pair(early_ref, late_ref, n)
         grown = 1.0 + jnp.concatenate([pen_ref[2 * n], pen_ref[2 * n + 1]], axis=1)
         square = grown * grown
         weight = 1.0 / (square * square)
@@ -238,26 +262,50 @@
     return x + lax.ppermute(x, "rep", [(i, i ^ 6) for i in range(REPS)])
 
 
-def refine(cap, got):
+SMEM = pl.BlockSpec(memory_space=pltpu.SMEM)
+VMEM = pl.BlockSpec(memory_space=pltpu.VMEM)
+
+
+def place():
+    rep = lax.axis_index("rep")
+    return jnp.stack([rep // 2, rep % 2, rep]).astype(jnp.int32)
+
+
+def to_owners(packed):
+    flat = packed.reshape(OWNERS, -1, LANES)
+    return lax.all_to_all(flat, "cluster", 0, 0, tiled=True).reshape(packed.shape)
+
+
+def refine(cap, early, late):
     blocks = OWNERS * cap // LANES
-    packed, target = pl.pallas_call(
-        functools.partial(pack_kernel, cap),
+    packed, target, hot, group_of = pl.pallas_call(
+        functools.partial(pack_early_kernel, cap),
         out_shape=(
             shape(blocks, ROWS, LANES),
             shape(REPS, VEC, kind=jnp.int32),
+            shape(REPS, VEC, PAIR, kind=BF16),
+            shape(REPS, 16, VEC, kind=jnp.int32),
         ),
-        scratch_shapes=[pltpu.VMEM((REPS, STACK, VEC), BF16), pltpu.VMEM((REPS, VEC, LANES), F32)],
-        compiler_params=params(),
-        cost_estimate=cost(2 * STACK * 2048 * OWNERS * cap, 3_000_000),
-        name="pack",
-    )(got)
-    per = cap // LANES
-    rows = lax.all_to_all(
-        packed.reshape(OWNERS, per * ROWS, LANES), "cluster", 0, 0, tiled=True
-    ).reshape(blocks, ROWS, LANES)
+        scratch_shapes=[pltpu.VMEM((REPS, 2 * EARLY + 16, VEC), BF16)],
+        compiler_params=params(),
+        cost_estimate=cost(2 * 80 * 2048 * OWNERS * cap, 3_000_000),
+        name="pack_early",
+    )(early)
+    rows_early = to_owners(packed)
+    packed = pl.pallas_call(
+        functools.partial(pack_late_kernel, cap),
+        out_shape=shape(blocks, LATE, LANES),
+        in_specs=[SMEM] + [VMEM] * (2 + REPS),
+        scratch_shapes=[pltpu.VMEM((REPS, 2 * LATE, VEC), BF16)],
+        compiler_params=params(),
+        cost_estimate=cost(2 * 128 * 2048 * OWNERS * cap, 3_000_000),
+        name="pack_late",
+    )(place(), hot, group_of, *late)
+    rows_late = to_owners(packed)
     partial, most = pl.pallas_call(
         functools.partial(distance_kernel, blocks),
-        out_shape=(shape(blocks, K, LANES), shape(8, LANES)),
+        out_shape=(shape(blocks, K, LANES), shape(1, kind=jnp.int32)),
+        out_specs=(VMEM, SMEM),
         scratch_shapes=[
             pltpu.VMEM((STACK, SLOTS), F32),
             pltpu.VMEM((2 * SLOTS, 2 * PART), BF16),
@@ -265,7 +313,7 @@
         compiler_params=params(),
         cost_estimate=cost(2 * 8 * PART * SLOTS * OWNERS * cap, 2_000_000),
         name="distance",
-    )(rows)
+    )(rows_early, rows_late)
     pen = sum_over_rep(partial)
     cent, share = pl.pallas_call(
         functools.partial(share_kernel, blocks),
@@ -277,10 +325,8 @@
         compiler_params=params(),
         cost_estimate=cost(2 * 3 * PART * SLOTS * OWNERS * cap, 2_000_000),
         name="share",
-    )(rows, pen)
-    back = lax.all_to_all(
-        share.reshape(OWNERS, per * K, LANES), "cluster", 0, 0, tiled=True
-    ).reshape(blocks, K, LANES)
+    )(rows_early, rows_late, pen)
+    back = to_owners(share)
     pieces = []
     for step in range(4):
         mine = lax.ppermute(cent, "rep", along_x(step)) if step else cent
@@ -290,14 +336,11 @@
 
 def finish(cap, pieces, back, target):
     blocks = OWNERS * cap // LANES
-    rep = lax.axis_index("rep")
-    at = jnp.stack([rep // 2, rep % 2, rep]).astype(jnp.int32)
-    smem = pl.BlockSpec(memory_space=pltpu.SMEM)
-    vmem = pl.BlockSpec(memory_space=pltpu.VMEM)
+    at = place()
     centroids = pl.pallas_call(
         join_kernel,
         out_shape=shape(SLOTS, D),
-        in_specs=[smem] + [vmem] * REPS,
+        in_specs=[SMEM] + [VMEM] * REPS,
         scratch_shapes=[pltpu.VMEM((D, SLOTS), F32)],
         compiler_params=params(),
         cost_estimate=cost(0, 1_600_000),
@@ -306,7 +349,7 @@
     shares = pl.pallas_call(
         functools.partial(take_kernel, blocks),
         out_shape=shape(K, VEC),
-        in_specs=[smem, vmem, vmem],
+        in_specs=[SMEM, VMEM, VMEM],
         compiler_params=params(),
         cost_estimate=cost(2 * 24 * VEC * OWNERS * cap, 200_000),
         name="take",
@@ -316,25 +359,30 @@
 
 def on_device(vectors, parent_id, child_id):
     slot = (parent_id * K + child_id).astype(F32).reshape(1, VEC)
-    turned = pl.pallas_call(
+    early, late = pl.pallas_call(
         turn_kernel,
-        out_shape=shape(REPS, ROWS, VEC),
+        out_shape=(shape(REPS, ROWS, VEC), shape(REPS, LATE, VEC)),
+        in_specs=[SMEM, VMEM, VMEM],
         compiler_params=params(),
         cost_estimate=cost(0, 1_600_000),
         name="turn",
-    )(vectors, slot)
-    got = lax.all_to_all(turned, "rep", 0, 0, tiled=True)
-    pieces, back, target, most = refine(LANES, got)
-    over = most[1, 0] > LANES
-
-    def wide(got, pieces, back, target):
-        pieces, back, target, _ = refine(PAIR, got)
+    )(place(), vectors, slot)
+    early = lax.all_to_all(early, "rep", 0, 0, tiled=True)
+    late = [late[0]] + [
+        lax.ppermute(late[step], "rep", [(i, (i + step) % REPS) for i in range(REPS)])
+        for step in range(1, REPS)
+    ]
+    pieces, back, target, most = refine(LANES, early, late)
+    over = most[0] > LANES
+
+    def wide(early, late, pieces, back, target):
+        pieces, back, target, _ = refine(PAIR, early, late)
         return finish(PAIR, pieces, back, target)
 
-    def narrow(got, pieces, back, target):
+    def narrow(early, late, pieces, back, target):
         return finish(LANES, pieces, back, target)
 
-    centroids, shares = lax.cond(over, wide, narrow, got, pieces, back, target)
+    centroids, shares = lax.cond(over, wide, narrow, early, late, pieces, back, target)
     return centroids, shares.T
 
 

time: 122 us -> 130 us (1.066)
  blocking collectives: 71.6 us -> 47.8 us
  starting transfers between devices: 9.79 us -> 26.9 us
  waiting for transfers between devices: 17.6 us -> 25.8 us
  Pallas kernels: 16.2 us -> 22.4 us
    all_to_all x2, blocking collectives: 71.6 us -> 47.8 us  [the longest x1 35.4 us: to_owners(): lax.all_to_all(flat, 'cluster', 0, 0, tiled=True).reshape(packed.shape)]
    all_to_all x1 -> x2, starting transfers between devices: 5.57 us -> 17.3 us  [to_owners(): lax.all_to_all(flat, 'cluster', 0, 0, tiled=True).reshape(packed.shape)]
    ppermute x0 -> x7, starting transfers between devices: none -> 6.13 us  [on_device(): lax.ppermute(late[step], 'rep', [(i, (i + step) % REPS) for i in range(RE...]
    pallas_call x3 -> x4, Pallas kernels: 6.86 us -> 12.7 us  [the longest x1 5.51 us: refine(): pl.pallas_call(functools.partial(pack_early_kernel, cap), out_shape=(shap...]
    ppermute x0 -> x7, waiting for transfers between devices: none -> 5.7 us  [on_device(): lax.ppermute(late[step], 'rep', [(i, (i + step) % REPS) for i in range(RE...]
    all_to_all x1 -> x2, waiting for transfers between devices: 0.01 us -> 1.81 us  [to_owners(): lax.all_to_all(flat, 'cluster', 0, 0, tiled=True).reshape(packed.shape)]
  transfers between devices with their start and end apart: 11 -> 19, of which waited for: 7 -> 12; matrix products, arithmetic and copies ran while one was open for 0% -> 1% of each run, Pallas kernels for 0% -> 4%
where the time goes in v4:
time: 130 us; the launch traced here: 128 us
  blocking collectives  47.8 us (37%)
  starting transfers between devices  26.9 us (21%)
  waiting for transfers between devices  25.8 us (20%)
  Pallas kernels  22.4 us (17%)
  local copies, waits for them, and re-layouts  3 us (2%)
  between operations  1.43 us (1%)
    all_to_all x1, blocking collectives, to_owners(): lax.all_to_all(flat, 'cluster', 0, 0, tiled=True).reshape(packed.shape)  35.4 us
    all_to_all x2, starting transfers between devices, to_owners(): lax.all_to_all(flat, 'cluster', 0, 0, tiled=True).reshape(packed.shape)  17.3 us
    all_to_all x1, blocking collectives, on_device(): early = lax.all_to_all(early, 'rep', 0, 0, tiled=True)  12.3 us
    ppermute x7, starting transfers between devices, on_device(): lax.ppermute(late[step], 'rep', [(i, (i + step) % REPS) for i in range(RE...  6.13 us
    ppermute x3, waiting for transfers between devices, refine(): mine = lax.ppermute(cent, 'rep', along_x(step)) if step else cent  5.75 us
    ppermute x7, waiting for transfers between devices, on_device(): lax.ppermute(late[step], 'rep', [(i, (i + step) % REPS) for i in range(RE...  5.7 us
    ppermute x1, waiting for transfers between devices, sum_over_rep(): return x + lax.ppermute(x, 'rep', [(i, i ^ 6) for i in range(REPS)])  5.57 us
    pallas_call x1, Pallas kernels, refine(): pl.pallas_call(functools.partial(pack_early_kernel, cap), out_shape=(shap...  5.51 us
  transfers between devices with their start and end apart: 19, of which 12 were waited for; matrix products, arithmetic and copies ran while one was open for 1% of the time, Pallas kernels for 4%

profile of v4, /device:TPU:8, one launch (start us, length us, event | category | flops | bytes accessed | tf_op | source)
XLA Modules:
  0.0 128.2 jit_solution(11034669550999991348)
XLA Ops:
  1.4 1.1 copy-done
  3.4 12.3 %all_to_all.33.in_ref = f32[8,40,256]{2,1,0:T(8,128)S(1)} all-to-all(f32[8,40,256]{2,1,0:T(8,128)S(1)} %get-tuple-element.78), channel_id=1, replica_groups=mesh['cluster'=32,'rep'=8] {'rep'}, dimensions={0} | all-to-all | bytes 655360 | tf_op jit(solution)/shard_map/all_to_all | solution.py:370
  15.7 5.5 %pack_early.3 = (f32[32,40,128]{2,1,0:T(8,128)}, s32[8,256]{1,0:T(8,128)S(1)}, bf16[8,256,256]{2,1,0:T(8,128)(2,1)S(1)}, s32[8,16,256]{2,1,0:T(8,128)S(1)}) custom-call(f32[8,40,256]{2,1,0:T(8,128)S(1)} %all_to_all.33.in_ref), custom_call_target="tpu_custom_call" | custom-call | flops 1342177280 | bytes 3000000 | tf_op jit(solution)/shard_map/pack_early/pallas_call | solution.py:281
  21.2 11.7 %all-to-all-start.4 = ((f32[32,40,128]{2,1,0:T(8,128)}), f32[32,40,128]{2,1,0:T(8,128)S(1)}, u32[]{:S(2)}, u32[]{:S(2)}) async-start(f32[32,40,128]{2,1,0:T(8,128)} %get-tuple-element.79), calls=%async_computation.4 | async-start | bytes 1310720 | tf_op jit(solution)/shard_map/all_to_all | solution.py:276
  33.6 1.2 collective-permute-start.15
  34.8 1.3 %collective-permute-start.14 = (f32[64,256]{1,0:T(8,128)S(1)}, f32[64,256]{1,0:T(8,128)}, u32[]{:S(2)}, u32[]{:S(2)}) collective-permute-start(f32[64,256]{1,0:T(8,128)S(1)} %get-tuple-element.92), channel_id=1, source_target_pairs={{0,5},{1,6},{2,7},{3,0},{4,1},{5,2},{6,3},{7,4},{8,13},{9,14},{10,... | collective-permute-start | bytes 196616 | tf_op jit(solution)/shard_map/ppermute | solution.py:372
  36.1 2.1 %collective-permute-start.13 = (f32[64,256]{1,0:T(8,128)S(1)}, f32[64,256]{1,0:T(8,128)S(1)}, u32[]{:S(2)}, u32[]{:S(2)}) collective-permute-start(f32[64,256]{1,0:T(8,128)S(1)} %get-tuple-element.93), channel_id=1, source_target_pairs={{0,4},{1,5},{2,6},{3,7},{4,0},{5,1},{6,2},{7,3},{8,12},{9,13},{10,... | collective-permute-start | bytes 196616 | tf_op jit(solution)/shard_map/ppermute | solution.py:372
  39.7 2.1 %collective-permute-done.13.refs_4_ = f32[64,256]{1,0:T(8,128)S(1)} collective-permute-done((f32[64,256]{1,0:T(8,128)S(1)}, f32[64,256]{1,0:T(8,128)S(1)}, u32[]{:S(2)}, u32[]{:S(2)}) %collective-permute-start.13) | collective-permute-done | bytes 65568 | tf_op jit(solution)/shard_map/ppermute | solution.py:372
  41.8 1.5 %collective-permute-done.12.refs_3_ = f32[64,256]{1,0:T(8,128)S(1)} collective-permute-done((f32[64,256]{1,0:T(8,128)S(1)}, f32[64,256]{1,0:T(8,128)S(1)}, u32[]{:S(2)}, u32[]{:S(2)}) %collective-permute-start.12) | collective-permute-done | bytes 65568 | tf_op jit(solution)/shard_map/ppermute | solution.py:372
  43.4 1.2 collective-permute-done.11.refs_2_
  46.0 4.6 %pack_late.3 = f32[32,64,128]{2,1,0:T(8,128)S(1)} custom-call(s32[3]{0:T(128)S(1)} %pad_add_fusion.2.at_ref, bf16[8,256,256]{2,1,0:T(8,128)(2,1)S(1)} %get-tuple-element.80.hot, s32[8,16,256]{2,1,0:T(8,128)S(1)} %get-tuple-element.81.group_of, f32[64,256]{1,0:T(8,128)} %get-tuple-element.97.refs_0_, f32[64,256]{1,0:T(8,128)S(1)} %collective-permute-done.10.refs_1_, ...), custom_call_target="tpu_custom_call" | custom-call | flops 2147483648 | bytes 3000000 | tf_op jit(solution)/shard_map/pack_late/pallas_call | solution.py:295
  50.7 1.8 %all-to-all-done.4.early_ref = f32[32,40,128]{2,1,0:T(8,128)S(1)} async-done(((f32[32,40,128]{2,1,0:T(8,128)}), f32[32,40,128]{2,1,0:T(8,128)S(1)}, u32[]{:S(2)}, u32[]{:S(2)}) %all-to-all-start.4) | async-done | bytes 655392 | tf_op jit(solution)/shard_map/all_to_all | solution.py:276
  52.5 35.4 %all_to_all.34.late_ref = f32[32,64,128]{2,1,0:T(8,128)S(1)} all-to-all(f32[32,64,128]{2,1,0:T(8,128)S(1)} %pack_late.3), channel_id=1, replica_groups=mesh['cluster'=32,'rep'=8] {'cluster'}, dimensions={0} | all-to-all | bytes 2097152 | tf_op jit(solution)/shard_map/all_to_all | solution.py:276
  87.9 5.5 %distance.3 = (f32[32,8,128]{2,1,0:T(8,128)S(1)}, s32[1]{0:T(128)}) custom-call(f32[32,40,128]{2,1,0:T(8,128)S(1)} %all-to-all-done.4.early_ref, f32[32,64,128]{2,1,0:T(8,128)S(1)} %all_to_all.34.late_ref), custom_call_target="tpu_custom_call" | custom-call | flops 1610612736 | bytes 2000000 | tf_op jit(solution)/shard_map/distance/pallas_call | solution.py:305
  93.5 1.3 %collective-permute-done.17 = f32[32,8,128]{2,1,0:T(8,128)S(1)} collective-permute-done((f32[32,8,128]{2,1,0:T(8,128)S(1)}, f32[32,8,128]{2,1,0:T(8,128)S(1)}, u32[]{:S(2)}, u32[]{:S(2)}) %collective-permute-start.17) | collective-permute-done | bytes 131104 | tf_op jit(solution)/shard_map/ppermute | solution.py:260
  95.4 5.1 %collective-permute-done.18 = f32[32,8,128]{2,1,0:T(8,128)S(1)} collective-permute-done((f32[32,8,128]{2,1,0:T(8,128)S(1)}, f32[32,8,128]{2,1,0:T(8,128)S(1)}, u32[]{:S(2)}, u32[]{:S(2)}) %collective-permute-start.18) | collective-permute-done | bytes 131104 | tf_op jit(solution)/shard_map/ppermute | solution.py:261
  101.2 5.6 %collective-permute-done.19 = f32[32,8,128]{2,1,0:T(8,128)S(1)} collective-permute-done((f32[32,8,128]{2,1,0:T(8,128)S(1)}, f32[32,8,128]{2,1,0:T(8,128)S(1)}, u32[]{:S(2)}, u32[]{:S(2)}) %collective-permute-start.19) | collective-permute-done | bytes 131104 | tf_op jit(solution)/shard_map/ppermute | solution.py:262
  106.8 3.2 %share.3 = (f32[96,256]{1,0:T(8,128)S(1)}, f32[32,8,128]{2,1,0:T(8,128)}) custom-call(f32[32,40,128]{2,1,0:T(8,128)S(1)} %all-to-all-done.4.early_ref, f32[32,64,128]{2,1,0:T(8,128)S(1)} %all_to_all.34.late_ref, f32[32,8,128]{2,1,0:T(8,128)S(1)} %add.40.pen_ref), custom_call_target="tpu_custom_call" | custom-call | flops 603979776 | bytes 2000000 | tf_op jit(solution)/shard_map/share/pallas_call | solution.py:318
  110.0 5.6 %all-to-all-start.6 = ((f32[32,8,128]{2,1,0:T(8,128)}), f32[32,8,128]{2,1,0:T(8,128)S(1)}, u32[]{:S(2)}, u32[]{:S(2)}) async-start(f32[32,8,128]{2,1,0:T(8,128)} %get-tuple-element.86), calls=%async_computation.6 | async-start | bytes 262144 | tf_op jit(solution)/shard_map/all_to_all | solution.py:276
  117.7 2.6 %collective-permute-done.25 = f32[96,256]{1,0:T(8,128)S(1)} collective-permute-done((f32[96,256]{1,0:T(8,128)S(1)}, f32[96,256]{1,0:T(8,128)S(1)}, u32[]{:S(2)}, u32[]{:S(2)}) %collective-permute-start.25) | collective-permute-done | bytes 98336 | tf_op jit(solution)/shard_map/ppermute | solution.py:332
  120.3 2.2 %collective-permute-done.23 = f32[96,256]{1,0:T(8,128)S(1)} collective-permute-done((f32[96,256]{1,0:T(8,128)S(1)}, f32[96,256]{1,0:T(8,128)S(1)}, u32[]{:S(2)}, u32[]{:S(2)}) %collective-permute-start.23) | collective-permute-done | bytes 98336 | tf_op jit(solution)/shard_map/ppermute | solution.py:332
  122.5 1.0 collective-permute-done.21
  124.8 2.8 %conditional.1 = (f32[256,768]{1,0:T(8,128)}, f32[8,256]{1,0:T(8,128)S(1)}) conditional(s32[]{:T(128)} %bitcast.24, (f32[96,256]{1,0:T(8,128)S(1)}, f32[96,256]{1,0:T(8,128)S(1)}, f32[96,256]{1,0:T(8,128)S(1)}, f32[96,256]{1,0:T(8,128)S(1)}, f32[96,256]{1,0:T(8,128)S(1)}, /*index=5*/f32[96,256]{1,0:T(8,128)S(1)}, f32[96,256]{1,0:T(8,128)S(1)}, ...), branch_computations={%region_0.1_spmd, %region_1.2_spmd} | conditional | flops 11509366784 | bytes 37359808 | solution.py:385
  124.9 1.7 %join.2 = f32[256,768]{1,0:T(8,128)} custom-call(s32[3]{0:T(128)S(1)} %pad_add_fusion.at_ref, f32[96,256]{1,0:T(8,128)S(1)} %get-tuple-element.38.refs_0_, f32[96,256]{1,0:T(8,128)S(1)} %get-tuple-element.39.refs_1_, f32[96,256]{1,0:T(8,128)S(1)} %get-tuple-element.40.refs_2_, f32[96,256]{1,0:T(8,128)S(1)} %get-tuple-element.41.refs_3_, ...), custom_call_target="tpu_custom_call" | custom-call | bytes 1600000 | tf_op jit(solution)/shard_map/cond/branch_0_fun/join/pallas_call | solution.py:340
  (43 shorter events, 11.1 us)
Async XLA Ops:
  1.4 1.1 copy-start
  21.2 31.3 %all-to-all-start.4 = ((f32[32,40,128]{2,1,0:T(8,128)}), f32[32,40,128]{2,1,0:T(8,128)S(1)}, u32[]{:S(2)}, u32[]{:S(2)}) async-start(f32[32,40,128]{2,1,0:T(8,128)} %get-tuple-element.79), calls=%async_computation.4 | async-start | bytes 1310720 | tf_op jit(solution)/shard_map/all_to_all | solution.py:276
  33.6 4.5 %collective-permute-start.16 = (f32[64,256]{1,0:T(8,128)S(1)}, f32[64,256]{1,0:T(8,128)}, u32[]{:S(2)}, u32[]{:S(2)}) collective-permute-start(f32[64,256]{1,0:T(8,128)S(1)} %get-tuple-element.90), channel_id=1, source_target_pairs={{0,7},{1,0},{2,1},{3,2},{4,3},{5,4},{6,5},{7,6},{8,15},{9,8},{10,9... | collective-permute-start | bytes 196616 | tf_op jit(solution)/shard_map/ppermute | solution.py:372
  33.6 5.4 %collective-permute-start.15 = (f32[64,256]{1,0:T(8,128)S(1)}, f32[64,256]{1,0:T(8,128)}, u32[]{:S(2)}, u32[]{:S(2)}) collective-permute-start(f32[64,256]{1,0:T(8,128)S(1)} %get-tuple-element.91), channel_id=1, source_target_pairs={{0,6},{1,7},{2,0},{3,1},{4,2},{5,3},{6,4},{7,5},{8,14},{9,15},{10,... | collective-permute-start | bytes 196616 | tf_op jit(solution)/shard_map/ppermute | solution.py:372
  34.8 5.0 %collective-permute-start.14 = (f32[64,256]{1,0:T(8,128)S(1)}, f32[64,256]{1,0:T(8,128)}, u32[]{:S(2)}, u32[]{:S(2)}) collective-permute-start(f32[64,256]{1,0:T(8,128)S(1)} %get-tuple-element.92), channel_id=1, source_target_pairs={{0,5},{1,6},{2,7},{3,0},{4,1},{5,2},{6,3},{7,4},{8,13},{9,14},{10,... | collective-permute-start | bytes 196616 | tf_op jit(solution)/shard_map/ppermute | solution.py:372
  36.1 5.8 %collective-permute-start.13 = (f32[64,256]{1,0:T(8,128)S(1)}, f32[64,256]{1,0:T(8,128)S(1)}, u32[]{:S(2)}, u32[]{:S(2)}) collective-permute-start(f32[64,256]{1,0:T(8,128)S(1)} %get-tuple-element.93), channel_id=1, source_target_pairs={{0,4},{1,5},{2,6},{3,7},{4,0},{5,1},{6,2},{7,3},{8,12},{9,13},{10,... | collective-permute-start | bytes 196616 | tf_op jit(solution)/shard_map/ppermute | solution.py:372
  38.1 5.2 %collective-permute-start.12 = (f32[64,256]{1,0:T(8,128)S(1)}, f32[64,256]{1,0:T(8,128)S(1)}, u32[]{:S(2)}, u32[]{:S(2)}) collective-permute-start(f32[64,256]{1,0:T(8,128)S(1)} %get-tuple-element.94), channel_id=1, source_target_pairs={{0,3},{1,4},{2,5},{3,6},{4,7},{5,0},{6,1},{7,2},{8,11},{9,12},{10,... | collective-permute-start | bytes 196616 | tf_op jit(solution)/shard_map/ppermute | solution.py:372
  38.1 6.4 %collective-permute-start.11 = (f32[64,256]{1,0:T(8,128)S(1)}, f32[64,256]{1,0:T(8,128)S(1)}, u32[]{:S(2)}, u32[]{:S(2)}) collective-permute-start(f32[64,256]{1,0:T(8,128)S(1)} %get-tuple-element.95), channel_id=1, source_target_pairs={{0,2},{1,3},{2,4},{3,5},{4,6},{5,7},{6,0},{7,1},{8,10},{9,11},{10,... | collective-permute-start | bytes 196616 | tf_op jit(solution)/shard_map/ppermute | solution.py:372
  39.0 6.4 %collective-permute-start.10 = (f32[64,256]{1,0:T(8,128)S(1)}, f32[64,256]{1,0:T(8,128)S(1)}, u32[]{:S(2)}, u32[]{:S(2)}) collective-permute-start(f32[64,256]{1,0:T(8,128)S(1)} %get-tuple-element.96), channel_id=1, source_target_pairs={{0,1},{1,2},{2,3},{3,4},{4,5},{5,6},{6,7},{7,0},{8,9},{9,10},{10,1... | collective-permute-start | bytes 196616 | tf_op jit(solution)/shard_map/ppermute | solution.py:372
  41.8 3.6 %copy-start.3 = (f32[64,256]{1,0:T(8,128)}, f32[64,256]{1,0:T(8,128)S(1)}, u32[]{:S(2)}) copy-start(f32[64,256]{1,0:T(8,128)S(1)} %collective-permute-done.13.refs_4_) | copy-start | bytes 196612
  43.4 2.1 %copy-start.4 = (f32[64,256]{1,0:T(8,128)}, f32[64,256]{1,0:T(8,128)S(1)}, u32[]{:S(2)}) copy-start(f32[64,256]{1,0:T(8,128)S(1)} %collective-permute-done.12.refs_3_) | copy-start | bytes 196612
  44.5 0.9 copy-start.5
  45.4 0.6 copy-start.6
  93.4 1.4 %collective-permute-start.17 = (f32[32,8,128]{2,1,0:T(8,128)S(1)}, f32[32,8,128]{2,1,0:T(8,128)S(1)}, u32[]{:S(2)}, u32[]{:S(2)}) collective-permute-start(f32[32,8,128]{2,1,0:T(8,128)S(1)} %get-tuple-element.84), channel_id=1, source_target_pairs={{0,1},{1,0},{2,3},{3,2},{4,5},{5,4},{6,7},{7,6},{8,9},{9,8},{10,11... | collective-permute-start | bytes 393224 | tf_op jit(solution)/shard_map/ppermute | solution.py:260
  94.9 5.6 %collective-permute-start.18 = (f32[32,8,128]{2,1,0:T(8,128)S(1)}, f32[32,8,128]{2,1,0:T(8,128)S(1)}, u32[]{:S(2)}, u32[]{:S(2)}) collective-permute-start(f32[32,8,128]{2,1,0:T(8,128)S(1)} %add.38), channel_id=1, source_target_pairs={{0,2},{1,3},{2,0},{3,1},{4,6},{5,7},{6,4},{7,5},{8,10},{9,11},{10,... | collective-permute-start | bytes 393224 | tf_op jit(solution)/shard_map/ppermute | solution.py:261
  100.5 6.3 %collective-permute-start.19 = (f32[32,8,128]{2,1,0:T(8,128)S(1)}, f32[32,8,128]{2,1,0:T(8,128)S(1)}, u32[]{:S(2)}, u32[]{:S(2)}) collective-permute-start(f32[32,8,128]{2,1,0:T(8,128)S(1)} %add.39), channel_id=1, source_target_pairs={{0,6},{1,7},{2,4},{3,5},{4,2},{5,3},{6,0},{7,1},{8,14},{9,15},{10,... | collective-permute-start | bytes 393224 | tf_op jit(solution)/shard_map/ppermute | solution.py:262
  110.0 14.8 %all-to-all-start.6 = ((f32[32,8,128]{2,1,0:T(8,128)}), f32[32,8,128]{2,1,0:T(8,128)S(1)}, u32[]{:S(2)}, u32[]{:S(2)}) async-start(f32[32,8,128]{2,1,0:T(8,128)} %get-tuple-element.86), calls=%async_computation.6 | async-start | bytes 262144 | tf_op jit(solution)/shard_map/all_to_all | solution.py:276
  115.6 4.7 %collective-permute-start.25 = (f32[96,256]{1,0:T(8,128)S(1)}, f32[96,256]{1,0:T(8,128)S(1)}, u32[]{:S(2)}, u32[]{:S(2)}) collective-permute-start(f32[96,256]{1,0:T(8,128)S(1)} %get-tuple-element.85), channel_id=1, source_target_pairs={{0,6},{1,7},{2,0},{3,1},{4,2},{5,3},{6,4},{7,5},{8,14},{9,15},{10,... | collective-permute-start | bytes 294920 | tf_op jit(solution)/shard_map/ppermute | solution.py:332
  116.3 6.2 %collective-permute-start.23 = (f32[96,256]{1,0:T(8,128)S(1)}, f32[96,256]{1,0:T(8,128)S(1)}, u32[]{:S(2)}, u32[]{:S(2)}) collective-permute-start(f32[96,256]{1,0:T(8,128)S(1)} %get-tuple-element.85), channel_id=1, source_target_pairs={{0,4},{1,5},{2,6},{3,7},{4,0},{5,1},{6,2},{7,3},{8,12},{9,13},{10,... | collective-permute-start | bytes 294920 | tf_op jit(solution)/shard_map/ppermute | solution.py:332
  117.0 6.4 %collective-permute-start.21 = (f32[96,256]{1,0:T(8,128)S(1)}, f32[96,256]{1,0:T(8,128)S(1)}, u32[]{:S(2)}, u32[]{:S(2)}) collective-permute-start(f32[96,256]{1,0:T(8,128)S(1)} %get-tuple-element.85), channel_id=1, source_target_pairs={{0,2},{1,3},{2,4},{3,5},{4,6},{5,7},{6,0},{7,1},{8,10},{9,11},{10,... | collective-permute-start | bytes 294920 | tf_op jit(solution)/shard_map/ppermute | solution.py:332
  117.7 6.4 %collective-permute-start.20 = (f32[96,256]{1,0:T(8,128)S(1)}, f32[96,256]{1,0:T(8,128)S(1)}, u32[]{:S(2)}, u32[]{:S(2)}) collective-permute-start(f32[96,256]{1,0:T(8,128)S(1)} %get-tuple-element.85), channel_id=1, source_target_pairs={{0,1},{1,0},{2,3},{3,2},{4,5},{5,4},{6,7},{7,6},{8,9},{9,8},{10,11... | collective-permute-start | bytes 294920 | tf_op jit(solution)/shard_map/ppermute | solution.py:333
  120.3 3.8 %collective-permute-start.26 = (f32[96,256]{1,0:T(8,128)S(1)}, f32[96,256]{1,0:T(8,128)S(1)}, u32[]{:S(2)}, u32[]{:S(2)}) collective-permute-start(f32[96,256]{1,0:T(8,128)S(1)} %collective-permute-done.25), channel_id=1, source_target_pairs={{0,1},{1,0},{2,3},{3,2},{4,5},{5,4},{6,7},{7,6},{8,9},{9,8},{10,11... | collective-permute-start | bytes 294920 | tf_op jit(solution)/shard_map/ppermute | solution.py:333
  122.5 1.7 %collective-permute-start.24 = (f32[96,256]{1,0:T(8,128)S(1)}, f32[96,256]{1,0:T(8,128)S(1)}, u32[]{:S(2)}, u32[]{:S(2)}) collective-permute-start(f32[96,256]{1,0:T(8,128)S(1)} %collective-permute-done.23), channel_id=1, source_target_pairs={{0,1},{1,0},{2,3},{3,2},{4,5},{5,4},{6,7},{7,6},{8,9},{9,8},{10,11... | collective-permute-start | bytes 294920 | tf_op jit(solution)/shard_map/ppermute | solution.py:333
  123.5 1.3 %collective-permute-start.22 = (f32[96,256]{1,0:T(8,128)S(1)}, f32[96,256]{1,0:T(8,128)S(1)}, u32[]{:S(2)}, u32[]{:S(2)}) collective-permute-start(f32[96,256]{1,0:T(8,128)S(1)} %collective-permute-done.21), channel_id=1, source_target_pairs={{0,1},{1,0},{2,3},{3,2},{4,5},{5,4},{6,7},{7,6},{8,9},{9,8},{10,11... | collective-permute-start | bytes 294920 | tf_op jit(solution)/shard_map/ppermute | solution.py:333
  (1 other events, 0.6 us)

commit v5 on v2

--- a/solution.py
+++ b/solution.py
@@ -45,7 +45,7 @@
             part, row = divmod(start, PART)
             size = min(PART - row, (tile + 1) * LANES - start)
             at = start - tile * LANES
-            out_ref[part, row : row + size, :] = turned[at : at + size, :]
+            out_ref[BY_CORE.index(part), row : row + size, :] = turned[at : at + size, :]
             start += size
     slots = jnp.broadcast_to(g_ref[...], (ROWS - PART, VEC))
     for part in range(REPS):
@@ -120,7 +120,7 @@
 
 def distance_kernel(blocks, x_ref, out_ref, most_ref, total, scaled):
     total[...] = jnp.zeros_like(total)
-    most_ref[...] = jnp.max(x_ref[:, PART:ROWS, :], axis=0)
+    most_ref[0] = jnp.max(x_ref[:, PART + 1, :]).astype(jnp.int32)
 
     def add(n, _):
         x, slot = load_pair(x_ref, n)
@@ -128,7 +128,7 @@
         total[...] += lax.dot_general(stack_of(x), hot, NT, preferred_element_type=F32)
         return 0
 
-    lax.fori_loop(0, blocks // 2, add, 0, unroll=2)
+    lax.fori_loop(0, blocks // 2, add, 0, unroll=4)
     sums = total[0:PART, :] + total[PART + 16 : STACK, :]
     counts = total[PART : PART + 8, :]
     high, low = parts_of(sums / (counts[0:1] + 1.0))
@@ -159,7 +159,7 @@
         out_ref[2 * n + 1] = part[:, LANES:PAIR]
         return 0
 
-    lax.fori_loop(0, blocks // 2, measure, 0, unroll=2)
+    lax.fori_loop(0, blocks // 2, measure, 0, unroll=4)
 
 
 def share_kernel(blocks, x_ref, pen_ref, cent_ref, share_ref, total, rest):
@@ -187,7 +187,7 @@
         )
         return 0
 
-    lax.fori_loop(0, blocks // 2, add, 0, unroll=2)
+    lax.fori_loop(0, blocks // 2, add, 0, unroll=4)
     weighted = total[0:PART, :] + total[PART + 16 : STACK, :] + rest[0:PART, :]
     summed = total[PART : PART + 1, :] + rest[PART : PART + 1, :]
     cent_ref[...] = weighted / (summed + 1.0)
@@ -229,6 +229,7 @@
     return [(i, ((i // 2 + step) % 4) * 2 + i % 2) for i in range(REPS)]
 
 
+BY_CORE = [0, 2, 4, 6, 1, 3, 5, 7]
 CORES = [(i, i ^ 1) for i in range(REPS)]
 
 
@@ -236,6 +237,10 @@
     x = x + lax.ppermute(x, "rep", CORES)
     x = x + lax.ppermute(x, "rep", [(i, i ^ 2) for i in range(REPS)])
     return x + lax.ppermute(x, "rep", [(i, i ^ 6) for i in range(REPS)])
+
+
+SMEM = pl.BlockSpec(memory_space=pltpu.SMEM)
+VMEM = pl.BlockSpec(memory_space=pltpu.VMEM)
 
 
 def refine(cap, got):
@@ -257,7 +262,8 @@
     ).reshape(blocks, ROWS, LANES)
     partial, most = pl.pallas_call(
         functools.partial(distance_kernel, blocks),
-        out_shape=(shape(blocks, K, LANES), shape(8, LANES)),
+        out_shape=(shape(blocks, K, LANES), shape(1, kind=jnp.int32)),
+        out_specs=(VMEM, SMEM),
         scratch_shapes=[
             pltpu.VMEM((STACK, SLOTS), F32),
             pltpu.VMEM((2 * SLOTS, 2 * PART), BF16),
@@ -288,30 +294,33 @@
     return pieces, back, target, most
 
 
-def finish(cap, pieces, back, target):
-    blocks = OWNERS * cap // LANES
+def place():
     rep = lax.axis_index("rep")
-    at = jnp.stack([rep // 2, rep % 2, rep]).astype(jnp.int32)
-    smem = pl.BlockSpec(memory_space=pltpu.SMEM)
-    vmem = pl.BlockSpec(memory_space=pltpu.VMEM)
-    centroids = pl.pallas_call(
+    return jnp.stack([rep // 2, rep % 2, rep % 2 * 4 + rep // 2]).astype(jnp.int32)
+
+
+def join(pieces):
+    return pl.pallas_call(
         join_kernel,
         out_shape=shape(SLOTS, D),
-        in_specs=[smem] + [vmem] * REPS,
+        in_specs=[SMEM] + [VMEM] * REPS,
         scratch_shapes=[pltpu.VMEM((D, SLOTS), F32)],
         compiler_params=params(),
         cost_estimate=cost(0, 1_600_000),
         name="join",
-    )(at, *pieces)
-    shares = pl.pallas_call(
+    )(place(), *pieces)
+
+
+def take(cap, back, target):
+    blocks = OWNERS * cap // LANES
+    return pl.pallas_call(
         functools.partial(take_kernel, blocks),
         out_shape=shape(K, VEC),
-        in_specs=[smem, vmem, vmem],
+        in_specs=[SMEM, VMEM, VMEM],
         compiler_params=params(),
         cost_estimate=cost(2 * 24 * VEC * OWNERS * cap, 200_000),
         name="take",
-    )(at, back, target)
-    return centroids, shares
+    )(place(), back, target)
 
 
 def on_device(vectors, parent_id, child_id):
@@ -323,18 +332,22 @@
         cost_estimate=cost(0, 1_600_000),
         name="turn",
     )(vectors, slot)
-    got = lax.all_to_all(turned, "rep", 0, 0, tiled=True)
+    got = lax.all_to_all(
+        turned, "rep", 0, 0, axis_index_groups=[BY_CORE], tiled=True
+    )
     pieces, back, target, most = refine(LANES, got)
-    over = most[1, 0] > LANES
-
-    def wide(got, pieces, back, target):
+    over = most[0] > LANES
+
+    picked = take(LANES, back, target)
+
+    def wide(got, pieces, picked):
         pieces, back, target, _ = refine(PAIR, got)
-        return finish(PAIR, pieces, back, target)
-
-    def narrow(got, pieces, back, target):
-        return finish(LANES, pieces, back, target)
-
-    centroids, shares = lax.cond(over, wide, narrow, got, pieces, back, target)
+        return join(pieces), take(PAIR, back, target)
+
+    def narrow(got, pieces, picked):
+        return join(pieces), picked
+
+    centroids, shares = lax.cond(over, wide, narrow, got, pieces, picked)
     return centroids, shares.T
 
 

time: 122 us -> 119 us (0.975)
  Pallas kernels: 16.2 us -> 13.9 us
    pallas_call x1, Pallas kernels: 5.17 us -> 3.82 us  [refine(): pl.pallas_call(functools.partial(distance_kernel, blocks), out_shape=(sha...]
  transfers between devices with their start and end apart: 11 -> 11, of which waited for: 7 -> 6; matrix products, arithmetic and copies ran while one was open for 0% -> 0% of each run, Pallas kernels for 0% -> 1%
where the time goes in v5:
time: 119 us; the launch traced here: 117 us
  blocking collectives  71.6 us (60%)
  waiting for transfers between devices  17.5 us (15%)
  Pallas kernels  13.9 us (12%)
  starting transfers between devices  9.75 us (8%)
  local copies, waits for them, and re-layouts  2 us (2%)
  between operations  1.42 us (1%)
    all_to_all x1, blocking collectives, refine(): lax.all_to_all(packed.reshape(OWNERS, per * ROWS, LANES), 'cluster', 0, 0...  53.9 us
    all_to_all x1, blocking collectives, on_device(): lax.all_to_all(turned, 'rep', 0, 0, axis_index_groups=[BY_CORE], tiled=True)  17.7 us
    ppermute x3, waiting for transfers between devices, refine(): mine = lax.ppermute(cent, 'rep', along_x(step)) if step else cent  6.21 us
    pallas_call x1, Pallas kernels, refine(): pl.pallas_call(functools.partial(pack_kernel, cap), out_shape=(shape(bloc...  5.74 us
    all_to_all x1, starting transfers between devices, refine(): lax.all_to_all(share.reshape(OWNERS, per * K, LANES), 'cluster', 0, 0, ti...  5.57 us
    ppermute x1, waiting for transfers between devices, sum_over_rep(): return x + lax.ppermute(x, 'rep', [(i, i ^ 6) for i in range(REPS)])  5.1 us
    ppermute x1, waiting for transfers between devices, sum_over_rep(): x = x + lax.ppermute(x, 'rep', [(i, i ^ 2) for i in range(REPS)])  4.83 us
    pallas_call x1, Pallas kernels, refine(): pl.pallas_call(functools.partial(distance_kernel, blocks), out_shape=(sha...  3.82 us
  transfers between devices with their start and end apart: 11, of which 6 were waited for; matrix products, arithmetic and copies ran while one was open for 0% of the time, Pallas kernels for 1%

profile of v5, /device:TPU:8, one launch (start us, length us, event | category | flops | bytes accessed | tf_op | source)
XLA Modules:
  0.0 117.3 jit_solution(16452041611745209550)
XLA Ops:
  0.6 0.7 add_convert_fusion
  1.3 1.1 copy-done
  2.5 0.3 turn.1
  2.7 17.7 %all_to_all.27.in_ref = f32[8,104,256]{2,1,0:T(8,128)S(1)} all-to-all(f32[8,104,256]{2,1,0:T(8,128)S(1)} %turn.1), channel_id=1, replica_groups={{0,2,4,6,1,3,5,7},{8,10,12,14,9,11,13,15},{16,18,20,22,17,19,21,23},{24..., dimensions={0} | all-to-all | bytes 1703936 | tf_op jit(solution)/shard_map/all_to_all | solution.py:335
  20.4 5.7 %pack.3 = (f32[32,104,128]{2,1,0:T(8,128)S(1)}, s32[8,256]{1,0:T(8,128)S(1)}) custom-call(f32[8,104,256]{2,1,0:T(8,128)S(1)} %all_to_all.27.in_ref), custom_call_target="tpu_custom_call" | custom-call | flops 3489660928 | bytes 3000000 | tf_op jit(solution)/shard_map/pack/pallas_call | solution.py:248
  26.2 53.9 %all_to_all.28.x_ref = f32[32,104,128]{2,1,0:T(8,128)S(1)} all-to-all(f32[32,104,128]{2,1,0:T(8,128)S(1)} %get-tuple-element.43), channel_id=1, replica_groups=mesh['cluster'=32,'rep'=8] {'cluster'}, dimensions={0} | all-to-all | bytes 3407872 | tf_op jit(solution)/shard_map/all_to_all | solution.py:260
  80.1 3.8 %distance.3 = (f32[32,8,128]{2,1,0:T(8,128)S(1)}, s32[1]{0:T(128)}) custom-call(f32[32,104,128]{2,1,0:T(8,128)S(1)} %all_to_all.28.x_ref), custom_call_target="tpu_custom_call" | custom-call | flops 1610612736 | bytes 2000000 | tf_op jit(solution)/shard_map/distance/pallas_call | solution.py:263
  84.0 1.3 %collective-permute-done.10 = f32[32,8,128]{2,1,0:T(8,128)S(1)} collective-permute-done((f32[32,8,128]{2,1,0:T(8,128)S(1)}, f32[32,8,128]{2,1,0:T(8,128)S(1)}, u32[]{:S(2)}, u32[]{:S(2)}) %collective-permute-start.10) | collective-permute-done | bytes 131104 | tf_op jit(solution)/shard_map/ppermute | solution.py:237
  85.4 0.8 collective-permute-start.11
  86.2 4.8 %collective-permute-done.11 = f32[32,8,128]{2,1,0:T(8,128)S(1)} collective-permute-done((f32[32,8,128]{2,1,0:T(8,128)S(1)}, f32[32,8,128]{2,1,0:T(8,128)S(1)}, u32[]{:S(2)}, u32[]{:S(2)}) %collective-permute-start.11) | collective-permute-done | bytes 131104 | tf_op jit(solution)/shard_map/ppermute | solution.py:238
  91.0 1.2 collective-permute-start.12
  92.2 5.1 %collective-permute-done.12 = f32[32,8,128]{2,1,0:T(8,128)S(1)} collective-permute-done((f32[32,8,128]{2,1,0:T(8,128)S(1)}, f32[32,8,128]{2,1,0:T(8,128)S(1)}, u32[]{:S(2)}, u32[]{:S(2)}) %collective-permute-start.12) | collective-permute-done | bytes 131104 | tf_op jit(solution)/shard_map/ppermute | solution.py:239
  97.3 2.2 %share.3 = (f32[96,256]{1,0:T(8,128)S(1)}, f32[32,8,128]{2,1,0:T(8,128)}) custom-call(f32[32,104,128]{2,1,0:T(8,128)S(1)} %all_to_all.28.x_ref, f32[32,8,128]{2,1,0:T(8,128)S(1)} %add.52.pen_ref), custom_call_target="tpu_custom_call" | custom-call | flops 603979776 | bytes 2000000 | tf_op jit(solution)/shard_map/share/pallas_call | solution.py:276
  99.5 5.6 %all-to-all-start.4 = ((f32[32,8,128]{2,1,0:T(8,128)}), f32[32,8,128]{2,1,0:T(8,128)S(1)}, u32[]{:S(2)}, u32[]{:S(2)}) async-start(f32[32,8,128]{2,1,0:T(8,128)} %get-tuple-element.47), calls=%async_computation.4 | async-start | bytes 262144 | tf_op jit(solution)/shard_map/all_to_all | solution.py:287
  105.1 1.2 collective-permute-start.18
  106.3 0.5 collective-permute-start.16
  106.8 0.5 collective-permute-start.14
  107.2 2.6 %collective-permute-done.18 = f32[96,256]{1,0:T(8,128)S(1)} collective-permute-done((f32[96,256]{1,0:T(8,128)S(1)}, f32[96,256]{1,0:T(8,128)S(1)}, u32[]{:S(2)}, u32[]{:S(2)}) %collective-permute-start.18) | collective-permute-done | bytes 98336 | tf_op jit(solution)/shard_map/ppermute | solution.py:292
  109.8 2.7 %collective-permute-done.16 = f32[96,256]{1,0:T(8,128)S(1)} collective-permute-done((f32[96,256]{1,0:T(8,128)S(1)}, f32[96,256]{1,0:T(8,128)S(1)}, u32[]{:S(2)}, u32[]{:S(2)}) %collective-permute-start.16) | collective-permute-done | bytes 98336 | tf_op jit(solution)/shard_map/ppermute | solution.py:292
  112.5 1.0 collective-permute-done.14
  114.2 1.0 take.3
  115.2 1.2 %conditional.1 = (f32[256,768]{1,0:T(8,128)S(1)}, f32[8,256]{1,0:T(8,128)S(1)}) conditional(s32[]{:T(128)} %bitcast.11, (f32[96,256]{1,0:T(8,128)S(1)}, f32[96,256]{1,0:T(8,128)S(1)}, f32[96,256]{1,0:T(8,128)S(1)}, f32[96,256]{1,0:T(8,128)S(1)}, f32[96,256]{1,0:T(8,128)S(1)}, /*index=5*/f32[96,256]{1,0:T(8,128)S(1)}, f32[96,256]{1,0:T(8,128)S(1)}, ...), branch_computations={%region_0.1_spmd, %region_1.2_spmd} | conditional | flops 11509366784 | bytes 24660416 | solution.py:350
  115.3 0.9 join.2
  116.4 0.9 copy-done.1
  (19 shorter events, 0.3 us)
Async XLA Ops:
  1.3 1.1 copy-start
  83.9 1.4 %collective-permute-start.10 = (f32[32,8,128]{2,1,0:T(8,128)S(1)}, f32[32,8,128]{2,1,0:T(8,128)S(1)}, u32[]{:S(2)}, u32[]{:S(2)}) collective-permute-start(f32[32,8,128]{2,1,0:T(8,128)S(1)} %get-tuple-element.45), channel_id=1, source_target_pairs={{0,1},{1,0},{2,3},{3,2},{4,5},{5,4},{6,7},{7,6},{8,9},{9,8},{10,11... | collective-permute-start | bytes 393224 | tf_op jit(solution)/shard_map/ppermute | solution.py:237
  85.4 5.6 %collective-permute-start.11 = (f32[32,8,128]{2,1,0:T(8,128)S(1)}, f32[32,8,128]{2,1,0:T(8,128)S(1)}, u32[]{:S(2)}, u32[]{:S(2)}) collective-permute-start(f32[32,8,128]{2,1,0:T(8,128)S(1)} %add.50), channel_id=1, source_target_pairs={{0,2},{1,3},{2,0},{3,1},{4,6},{5,7},{6,4},{7,5},{8,10},{9,11},{10,... | collective-permute-start | bytes 393224 | tf_op jit(solution)/shard_map/ppermute | solution.py:238
  91.0 6.3 %collective-permute-start.12 = (f32[32,8,128]{2,1,0:T(8,128)S(1)}, f32[32,8,128]{2,1,0:T(8,128)S(1)}, u32[]{:S(2)}, u32[]{:S(2)}) collective-permute-start(f32[32,8,128]{2,1,0:T(8,128)S(1)} %add.51), channel_id=1, source_target_pairs={{0,6},{1,7},{2,4},{3,5},{4,2},{5,3},{6,0},{7,1},{8,14},{9,15},{10,... | collective-permute-start | bytes 393224 | tf_op jit(solution)/shard_map/ppermute | solution.py:239
  99.5 14.6 %all-to-all-start.4 = ((f32[32,8,128]{2,1,0:T(8,128)}), f32[32,8,128]{2,1,0:T(8,128)S(1)}, u32[]{:S(2)}, u32[]{:S(2)}) async-start(f32[32,8,128]{2,1,0:T(8,128)} %get-tuple-element.47), calls=%async_computation.4 | async-start | bytes 262144 | tf_op jit(solution)/shard_map/all_to_all | solution.py:287
  105.1 4.7 %collective-permute-start.18 = (f32[96,256]{1,0:T(8,128)S(1)}, f32[96,256]{1,0:T(8,128)S(1)}, u32[]{:S(2)}, u32[]{:S(2)}) collective-permute-start(f32[96,256]{1,0:T(8,128)S(1)} %get-tuple-element.46), channel_id=1, source_target_pairs={{0,6},{1,7},{2,0},{3,1},{4,2},{5,3},{6,4},{7,5},{8,14},{9,15},{10,... | collective-permute-start | bytes 294920 | tf_op jit(solution)/shard_map/ppermute | solution.py:292
  106.3 6.2 %collective-permute-start.16 = (f32[96,256]{1,0:T(8,128)S(1)}, f32[96,256]{1,0:T(8,128)S(1)}, u32[]{:S(2)}, u32[]{:S(2)}) collective-permute-start(f32[96,256]{1,0:T(8,128)S(1)} %get-tuple-element.46), channel_id=1, source_target_pairs={{0,4},{1,5},{2,6},{3,7},{4,0},{5,1},{6,2},{7,3},{8,12},{9,13},{10,... | collective-permute-start | bytes 294920 | tf_op jit(solution)/shard_map/ppermute | solution.py:292
  106.8 6.7 %collective-permute-start.14 = (f32[96,256]{1,0:T(8,128)S(1)}, f32[96,256]{1,0:T(8,128)S(1)}, u32[]{:S(2)}, u32[]{:S(2)}) collective-permute-start(f32[96,256]{1,0:T(8,128)S(1)} %get-tuple-element.46), channel_id=1, source_target_pairs={{0,2},{1,3},{2,4},{3,5},{4,6},{5,7},{6,0},{7,1},{8,10},{9,11},{10,... | collective-permute-start | bytes 294920 | tf_op jit(solution)/shard_map/ppermute | solution.py:292
  107.2 7.9 %collective-permute-start.13 = (f32[96,256]{1,0:T(8,128)S(1)}, f32[96,256]{1,0:T(8,128)S(1)}, u32[]{:S(2)}, u32[]{:S(2)}) collective-permute-start(f32[96,256]{1,0:T(8,128)S(1)} %get-tuple-element.46), channel_id=1, source_target_pairs={{0,1},{1,0},{2,3},{3,2},{4,5},{5,4},{6,7},{7,6},{8,9},{9,8},{10,11... | collective-permute-start | bytes 294920 | tf_op jit(solution)/shard_map/ppermute | solution.py:293
  109.8 5.4 %collective-permute-start.19 = (f32[96,256]{1,0:T(8,128)S(1)}, f32[96,256]{1,0:T(8,128)S(1)}, u32[]{:S(2)}, u32[]{:S(2)}) collective-permute-start(f32[96,256]{1,0:T(8,128)S(1)} %collective-permute-done.18), channel_id=1, source_target_pairs={{0,1},{1,0},{2,3},{3,2},{4,5},{5,4},{6,7},{7,6},{8,9},{9,8},{10,11... | collective-permute-start | bytes 294920 | tf_op jit(solution)/shard_map/ppermute | solution.py:293
  112.5 2.7 %collective-permute-start.17 = (f32[96,256]{1,0:T(8,128)S(1)}, f32[96,256]{1,0:T(8,128)S(1)}, u32[]{:S(2)}, u32[]{:S(2)}) collective-permute-start(f32[96,256]{1,0:T(8,128)S(1)} %collective-permute-done.16), channel_id=1, source_target_pairs={{0,1},{1,0},{2,3},{3,2},{4,5},{5,4},{6,7},{7,6},{8,9},{9,8},{10,11... | collective-permute-start | bytes 294920 | tf_op jit(solution)/shard_map/ppermute | solution.py:293
  113.4 1.8 %collective-permute-start.15 = (f32[96,256]{1,0:T(8,128)S(1)}, f32[96,256]{1,0:T(8,128)S(1)}, u32[]{:S(2)}, u32[]{:S(2)}) collective-permute-start(f32[96,256]{1,0:T(8,128)S(1)} %collective-permute-done.14), channel_id=1, source_target_pairs={{0,1},{1,0},{2,3},{3,2},{4,5},{5,4},{6,7},{7,6},{8,9},{9,8},{10,11... | collective-permute-start | bytes 294920 | tf_op jit(solution)/shard_map/ppermute | solution.py:293
  116.4 0.9 copy-start.1
  116.4 0.9 copy-start.2

commit v6 on v5

--- a/solution.py
+++ b/solution.py
@@ -102,7 +102,7 @@
             )
         return 0
 
-    lax.fori_loop(0, groups, group, 0, unroll=2)
+    lax.fori_loop(0, groups, group, 0, unroll=4)
 
 
 def load_pair(x_ref, n):
@@ -128,7 +128,7 @@
         total[...] += lax.dot_general(stack_of(x), hot, NT, preferred_element_type=F32)
         return 0
 
-    lax.fori_loop(0, blocks // 2, add, 0, unroll=4)
+    lax.fori_loop(0, blocks // 2, add, 0, unroll=8)
     sums = total[0:PART, :] + total[PART + 16 : STACK, :]
     counts = total[PART : PART + 8, :]
     high, low = parts_of(sums / (counts[0:1] + 1.0))
@@ -159,7 +159,7 @@
         out_ref[2 * n + 1] = part[:, LANES:PAIR]
         return 0
 
-    lax.fori_loop(0, blocks // 2, measure, 0, unroll=4)
+    lax.fori_loop(0, blocks // 2, measure, 0, unroll=8)
 
 
 def share_kernel(blocks, x_ref, pen_ref, cent_ref, share_ref, total, rest):
@@ -187,7 +187,7 @@
         )
         return 0
 
-    lax.fori_loop(0, blocks // 2, add, 0, unroll=4)
+    lax.fori_loop(0, blocks // 2, add, 0, unroll=8)
     weighted = total[0:PART, :] + total[PART + 16 : STACK, :] + rest[0:PART, :]
     summed = total[PART : PART + 1, :] + rest[PART : PART + 1, :]
     cent_ref[...] = weighted / (summed + 1.0)

time: 119 us -> 117 us (0.983)
  Pallas kernels: 13.9 us -> 12.1 us
where the time goes in v6:
time: 117 us; the launch traced here: 115 us
  blocking collectives  71.6 us (61%)
  waiting for transfers between devices  17.5 us (15%)
  Pallas kernels  12.1 us (10%)
  starting transfers between devices  9.77 us (8%)
  local copies, waits for them, and re-layouts  2 us (2%)
  between operations  1.42 us (1%)
    all_to_all x1, blocking collectives, refine(): lax.all_to_all(packed.reshape(OWNERS, per * ROWS, LANES), 'cluster', 0, 0...  53.9 us
    all_to_all x1, blocking collectives, on_device(): lax.all_to_all(turned, 'rep', 0, 0, axis_index_groups=[BY_CORE], tiled=True)  17.7 us
    ppermute x3, waiting for transfers between devices, refine(): mine = lax.ppermute(cent, 'rep', along_x(step)) if step else cent  6.21 us
    all_to_all x1, starting transfers between devices, refine(): lax.all_to_all(share.reshape(OWNERS, per * K, LANES), 'cluster', 0, 0, ti...  5.57 us
    ppermute x1, waiting for transfers between devices, sum_over_rep(): return x + lax.ppermute(x, 'rep', [(i, i ^ 6) for i in range(REPS)])  5.1 us
    pallas_call x1, Pallas kernels, refine(): pl.pallas_call(functools.partial(pack_kernel, cap), out_shape=(shape(bloc...  5.04 us
    ppermute x1, waiting for transfers between devices, sum_over_rep(): x = x + lax.ppermute(x, 'rep', [(i, i ^ 2) for i in range(REPS)])  4.83 us
    pallas_call x1, Pallas kernels, refine(): pl.pallas_call(functools.partial(distance_kernel, blocks), out_shape=(sha...  3.2 us
  transfers between devices with their start and end apart: 11, of which 6 were waited for; matrix products, arithmetic and copies ran while one was open for 0% of the time, Pallas kernels for 1%

profile of v6, /device:TPU:8, one launch (start us, length us, event | category | flops | bytes accessed | tf_op | source)
XLA Modules:
  0.0 115.5 jit_solution(9697002403170186570)
XLA Ops:
  0.6 0.7 add_convert_fusion
  1.3 1.1 copy-done
  2.5 0.3 turn.1
  2.7 17.7 %all_to_all.27.in_ref = f32[8,104,256]{2,1,0:T(8,128)S(1)} all-to-all(f32[8,104,256]{2,1,0:T(8,128)S(1)} %turn.1), channel_id=1, replica_groups={{0,2,4,6,1,3,5,7},{8,10,12,14,9,11,13,15},{16,18,20,22,17,19,21,23},{24..., dimensions={0} | all-to-all | bytes 1703936 | tf_op jit(solution)/shard_map/all_to_all | solution.py:335
  20.4 5.0 %pack.3 = (f32[32,104,128]{2,1,0:T(8,128)S(1)}, s32[8,256]{1,0:T(8,128)S(1)}) custom-call(f32[8,104,256]{2,1,0:T(8,128)S(1)} %all_to_all.27.in_ref), custom_call_target="tpu_custom_call" | custom-call | flops 3489660928 | bytes 3000000 | tf_op jit(solution)/shard_map/pack/pallas_call | solution.py:248
  25.5 53.9 %all_to_all.28.x_ref = f32[32,104,128]{2,1,0:T(8,128)S(1)} all-to-all(f32[32,104,128]{2,1,0:T(8,128)S(1)} %get-tuple-element.43), channel_id=1, replica_groups=mesh['cluster'=32,'rep'=8] {'cluster'}, dimensions={0} | all-to-all | bytes 3407872 | tf_op jit(solution)/shard_map/all_to_all | solution.py:260
  79.4 3.2 %distance.3 = (f32[32,8,128]{2,1,0:T(8,128)S(1)}, s32[1]{0:T(128)}) custom-call(f32[32,104,128]{2,1,0:T(8,128)S(1)} %all_to_all.28.x_ref), custom_call_target="tpu_custom_call" | custom-call | flops 1610612736 | bytes 2000000 | tf_op jit(solution)/shard_map/distance/pallas_call | solution.py:263
  82.7 1.3 %collective-permute-done.10 = f32[32,8,128]{2,1,0:T(8,128)S(1)} collective-permute-done((f32[32,8,128]{2,1,0:T(8,128)S(1)}, f32[32,8,128]{2,1,0:T(8,128)S(1)}, u32[]{:S(2)}, u32[]{:S(2)}) %collective-permute-start.10) | collective-permute-done | bytes 131104 | tf_op jit(solution)/shard_map/ppermute | solution.py:237
  84.0 0.8 collective-permute-start.11
  84.8 4.8 %collective-permute-done.11 = f32[32,8,128]{2,1,0:T(8,128)S(1)} collective-permute-done((f32[32,8,128]{2,1,0:T(8,128)S(1)}, f32[32,8,128]{2,1,0:T(8,128)S(1)}, u32[]{:S(2)}, u32[]{:S(2)}) %collective-permute-start.11) | collective-permute-done | bytes 131104 | tf_op jit(solution)/shard_map/ppermute | solution.py:238
  89.7 1.2 %collective-permute-start.12 = (f32[32,8,128]{2,1,0:T(8,128)S(1)}, f32[32,8,128]{2,1,0:T(8,128)S(1)}, u32[]{:S(2)}, u32[]{:S(2)}) collective-permute-start(f32[32,8,128]{2,1,0:T(8,128)S(1)} %add.51), channel_id=1, source_target_pairs={{0,6},{1,7},{2,4},{3,5},{4,2},{5,3},{6,0},{7,1},{8,14},{9,15},{10,... | collective-permute-start | bytes 393224 | tf_op jit(solution)/shard_map/ppermute | solution.py:239
  90.9 5.1 %collective-permute-done.12 = f32[32,8,128]{2,1,0:T(8,128)S(1)} collective-permute-done((f32[32,8,128]{2,1,0:T(8,128)S(1)}, f32[32,8,128]{2,1,0:T(8,128)S(1)}, u32[]{:S(2)}, u32[]{:S(2)}) %collective-permute-start.12) | collective-permute-done | bytes 131104 | tf_op jit(solution)/shard_map/ppermute | solution.py:239
  96.0 1.7 %share.3 = (f32[96,256]{1,0:T(8,128)S(1)}, f32[32,8,128]{2,1,0:T(8,128)}) custom-call(f32[32,104,128]{2,1,0:T(8,128)S(1)} %all_to_all.28.x_ref, f32[32,8,128]{2,1,0:T(8,128)S(1)} %add.52.pen_ref), custom_call_target="tpu_custom_call" | custom-call | flops 603979776 | bytes 2000000 | tf_op jit(solution)/shard_map/share/pallas_call | solution.py:276
  97.7 5.6 %all-to-all-start.4 = ((f32[32,8,128]{2,1,0:T(8,128)}), f32[32,8,128]{2,1,0:T(8,128)S(1)}, u32[]{:S(2)}, u32[]{:S(2)}) async-start(f32[32,8,128]{2,1,0:T(8,128)} %get-tuple-element.47), calls=%async_computation.4 | async-start | bytes 262144 | tf_op jit(solution)/shard_map/all_to_all | solution.py:287
  103.3 1.2 %collective-permute-start.18 = (f32[96,256]{1,0:T(8,128)S(1)}, f32[96,256]{1,0:T(8,128)S(1)}, u32[]{:S(2)}, u32[]{:S(2)}) collective-permute-start(f32[96,256]{1,0:T(8,128)S(1)} %get-tuple-element.46), channel_id=1, source_target_pairs={{0,6},{1,7},{2,0},{3,1},{4,2},{5,3},{6,4},{7,5},{8,14},{9,15},{10,... | collective-permute-start | bytes 294920 | tf_op jit(solution)/shard_map/ppermute | solution.py:292
  104.5 0.5 collective-permute-start.16
  105.0 0.5 collective-permute-start.14
  105.4 2.6 %collective-permute-done.18 = f32[96,256]{1,0:T(8,128)S(1)} collective-permute-done((f32[96,256]{1,0:T(8,128)S(1)}, f32[96,256]{1,0:T(8,128)S(1)}, u32[]{:S(2)}, u32[]{:S(2)}) %collective-permute-start.18) | collective-permute-done | bytes 98336 | tf_op jit(solution)/shard_map/ppermute | solution.py:292
  108.0 2.7 %collective-permute-done.16 = f32[96,256]{1,0:T(8,128)S(1)} collective-permute-done((f32[96,256]{1,0:T(8,128)S(1)}, f32[96,256]{1,0:T(8,128)S(1)}, u32[]{:S(2)}, u32[]{:S(2)}) %collective-permute-start.16) | collective-permute-done | bytes 98336 | tf_op jit(solution)/shard_map/ppermute | solution.py:292
  110.7 1.0 collective-permute-done.14
  112.4 1.0 take.3
  113.4 1.2 %conditional.1 = (f32[256,768]{1,0:T(8,128)S(1)}, f32[8,256]{1,0:T(8,128)S(1)}) conditional(s32[]{:T(128)} %bitcast.11, (f32[96,256]{1,0:T(8,128)S(1)}, f32[96,256]{1,0:T(8,128)S(1)}, f32[96,256]{1,0:T(8,128)S(1)}, f32[96,256]{1,0:T(8,128)S(1)}, f32[96,256]{1,0:T(8,128)S(1)}, /*index=5*/f32[96,256]{1,0:T(8,128)S(1)}, f32[96,256]{1,0:T(8,128)S(1)}, ...), branch_computations={%region_0.1_spmd, %region_1.2_spmd} | conditional | flops 11509366784 | bytes 24660416 | solution.py:350
  113.5 0.9 join.2
  114.6 0.9 copy-done.1
  (19 shorter events, 0.3 us)
Async XLA Ops:
  1.3 1.1 copy-start
  82.6 1.4 %collective-permute-start.10 = (f32[32,8,128]{2,1,0:T(8,128)S(1)}, f32[32,8,128]{2,1,0:T(8,128)S(1)}, u32[]{:S(2)}, u32[]{:S(2)}) collective-permute-start(f32[32,8,128]{2,1,0:T(8,128)S(1)} %get-tuple-element.45), channel_id=1, source_target_pairs={{0,1},{1,0},{2,3},{3,2},{4,5},{5,4},{6,7},{7,6},{8,9},{9,8},{10,11... | collective-permute-start | bytes 393224 | tf_op jit(solution)/shard_map/ppermute | solution.py:237
  84.0 5.6 %collective-permute-start.11 = (f32[32,8,128]{2,1,0:T(8,128)S(1)}, f32[32,8,128]{2,1,0:T(8,128)S(1)}, u32[]{:S(2)}, u32[]{:S(2)}) collective-permute-start(f32[32,8,128]{2,1,0:T(8,128)S(1)} %add.50), channel_id=1, source_target_pairs={{0,2},{1,3},{2,0},{3,1},{4,6},{5,7},{6,4},{7,5},{8,10},{9,11},{10,... | collective-permute-start | bytes 393224 | tf_op jit(solution)/shard_map/ppermute | solution.py:238
  89.7 6.3 %collective-permute-start.12 = (f32[32,8,128]{2,1,0:T(8,128)S(1)}, f32[32,8,128]{2,1,0:T(8,128)S(1)}, u32[]{:S(2)}, u32[]{:S(2)}) collective-permute-start(f32[32,8,128]{2,1,0:T(8,128)S(1)} %add.51), channel_id=1, source_target_pairs={{0,6},{1,7},{2,4},{3,5},{4,2},{5,3},{6,0},{7,1},{8,14},{9,15},{10,... | collective-permute-start | bytes 393224 | tf_op jit(solution)/shard_map/ppermute | solution.py:239
  97.7 14.7 %all-to-all-start.4 = ((f32[32,8,128]{2,1,0:T(8,128)}), f32[32,8,128]{2,1,0:T(8,128)S(1)}, u32[]{:S(2)}, u32[]{:S(2)}) async-start(f32[32,8,128]{2,1,0:T(8,128)} %get-tuple-element.47), calls=%async_computation.4 | async-start | bytes 262144 | tf_op jit(solution)/shard_map/all_to_all | solution.py:287
  103.3 4.7 %collective-permute-start.18 = (f32[96,256]{1,0:T(8,128)S(1)}, f32[96,256]{1,0:T(8,128)S(1)}, u32[]{:S(2)}, u32[]{:S(2)}) collective-permute-start(f32[96,256]{1,0:T(8,128)S(1)} %get-tuple-element.46), channel_id=1, source_target_pairs={{0,6},{1,7},{2,0},{3,1},{4,2},{5,3},{6,4},{7,5},{8,14},{9,15},{10,... | collective-permute-start | bytes 294920 | tf_op jit(solution)/shard_map/ppermute | solution.py:292
  104.5 6.2 %collective-permute-start.16 = (f32[96,256]{1,0:T(8,128)S(1)}, f32[96,256]{1,0:T(8,128)S(1)}, u32[]{:S(2)}, u32[]{:S(2)}) collective-permute-start(f32[96,256]{1,0:T(8,128)S(1)} %get-tuple-element.46), channel_id=1, source_target_pairs={{0,4},{1,5},{2,6},{3,7},{4,0},{5,1},{6,2},{7,3},{8,12},{9,13},{10,... | collective-permute-start | bytes 294920 | tf_op jit(solution)/shard_map/ppermute | solution.py:292
  105.0 6.7 %collective-permute-start.14 = (f32[96,256]{1,0:T(8,128)S(1)}, f32[96,256]{1,0:T(8,128)S(1)}, u32[]{:S(2)}, u32[]{:S(2)}) collective-permute-start(f32[96,256]{1,0:T(8,128)S(1)} %get-tuple-element.46), channel_id=1, source_target_pairs={{0,2},{1,3},{2,4},{3,5},{4,6},{5,7},{6,0},{7,1},{8,10},{9,11},{10,... | collective-permute-start | bytes 294920 | tf_op jit(solution)/shard_map/ppermute | solution.py:292
  105.4 7.9 %collective-permute-start.13 = (f32[96,256]{1,0:T(8,128)S(1)}, f32[96,256]{1,0:T(8,128)S(1)}, u32[]{:S(2)}, u32[]{:S(2)}) collective-permute-start(f32[96,256]{1,0:T(8,128)S(1)} %get-tuple-element.46), channel_id=1, source_target_pairs={{0,1},{1,0},{2,3},{3,2},{4,5},{5,4},{6,7},{7,6},{8,9},{9,8},{10,11... | collective-permute-start | bytes 294920 | tf_op jit(solution)/shard_map/ppermute | solution.py:293
  108.0 5.4 %collective-permute-start.19 = (f32[96,256]{1,0:T(8,128)S(1)}, f32[96,256]{1,0:T(8,128)S(1)}, u32[]{:S(2)}, u32[]{:S(2)}) collective-permute-start(f32[96,256]{1,0:T(8,128)S(1)} %collective-permute-done.18), channel_id=1, source_target_pairs={{0,1},{1,0},{2,3},{3,2},{4,5},{5,4},{6,7},{7,6},{8,9},{9,8},{10,11... | collective-permute-start | bytes 294920 | tf_op jit(solution)/shard_map/ppermute | solution.py:293
  110.7 2.7 %collective-permute-start.17 = (f32[96,256]{1,0:T(8,128)S(1)}, f32[96,256]{1,0:T(8,128)S(1)}, u32[]{:S(2)}, u32[]{:S(2)}) collective-permute-start(f32[96,256]{1,0:T(8,128)S(1)} %collective-permute-done.16), channel_id=1, source_target_pairs={{0,1},{1,0},{2,3},{3,2},{4,5},{5,4},{6,7},{7,6},{8,9},{9,8},{10,11... | collective-permute-start | bytes 294920 | tf_op jit(solution)/shard_map/ppermute | solution.py:293
  111.6 1.8 %collective-permute-start.15 = (f32[96,256]{1,0:T(8,128)S(1)}, f32[96,256]{1,0:T(8,128)S(1)}, u32[]{:S(2)}, u32[]{:S(2)}) collective-permute-start(f32[96,256]{1,0:T(8,128)S(1)} %collective-permute-done.14), channel_id=1, source_target_pairs={{0,1},{1,0},{2,3},{3,2},{4,5},{5,4},{6,7},{7,6},{8,9},{9,8},{10,11... | collective-permute-start | bytes 294920 | tf_op jit(solution)/shard_map/ppermute | solution.py:293
  114.6 0.9 copy-start.1
  114.6 0.9 copy-start.2

commit v7 on v3

--- a/solution.py
+++ b/solution.py
@@ -17,6 +17,7 @@
 ROWS = PART + 8
 VEC = 256
 LANES = 128
+TILES = D // LANES
 PAIR = 2 * LANES
 STACK = PART + 16 + PART
 F32 = jnp.float32
@@ -24,8 +25,8 @@
 NT = (((1,), (1,)), ((), ()))
 
 
-def params():
-    return pltpu.CompilerParams(vmem_limit_bytes=48 * 2**20)
+def params(limit=48 * 1024):
+    return pltpu.CompilerParams(vmem_limit_bytes=limit * 1024)
 
 
 def iota(shape, dim):
@@ -37,18 +38,17 @@
     return high, (x - high.astype(F32)).astype(BF16)
 
 
-def turn_kernel(v_ref, parent_ref, child_ref, out_ref):
-    for tile in range(D // LANES):
+def turn_kernel(v_ref, g_ref, out_ref):
+    for tile in range(TILES):
         turned = v_ref[:, tile * LANES : (tile + 1) * LANES].T
         start = tile * LANES
         while start < (tile + 1) * LANES:
             part, row = divmod(start, PART)
             size = min(PART - row, (tile + 1) * LANES - start)
             at = start - tile * LANES
-            out_ref[part, row : row + size, :] = turned[at : at + size, :]
+            out_ref[BY_CORE.index(part), row : row + size, :] = turned[at : at + size, :]
             start += size
-    slot = (parent_ref[...] * K + child_ref[...]).astype(F32)
-    slots = jnp.broadcast_to(slot, (ROWS - PART, VEC))
+    slots = jnp.broadcast_to(g_ref[...], (ROWS - PART, VEC))
     for part in range(REPS):
         out_ref[part, PART:ROWS, :] = slots
 
@@ -99,7 +99,7 @@
             )
         return 0
 
-    lax.fori_loop(0, groups, group, 0, unroll=2)
+    lax.fori_loop(0, groups, group, 0, unroll=4)
 
 
 def load_pair(x_ref, n):
@@ -125,7 +125,7 @@
         total[...] += lax.dot_general(stack_of(x), hot, NT, preferred_element_type=F32)
         return 0
 
-    lax.fori_loop(0, blocks // 2, add, 0, unroll=2)
+    lax.fori_loop(0, blocks // 2, add, 0, unroll=8)
     sums = total[0:PART, :] + total[PART + 16 : STACK, :]
     counts = total[PART : PART + 8, :]
     high, low = parts_of(sums / (counts[0:1] + 1.0))
@@ -156,7 +156,7 @@
         out_ref[2 * n + 1] = part[:, LANES:PAIR]
         return 0
 
-    lax.fori_loop(0, blocks // 2, measure, 0, unroll=2)
+    lax.fori_loop(0, blocks // 2, measure, 0, unroll=8)
 
 
 def share_kernel(blocks, x_ref, pen_ref, cent_ref, share_ref, total, rest):
@@ -184,21 +184,30 @@
         )
         return 0
 
-    lax.fori_loop(0, blocks // 2, add, 0, unroll=2)
+    lax.fori_loop(0, blocks // 2, add, 0, unroll=8)
     weighted = total[0:PART, :] + total[PART + 16 : STACK, :] + rest[0:PART, :]
     summed = total[PART : PART + 1, :] + rest[PART : PART + 1, :]
     cent_ref[...] = weighted / (summed + 1.0)
 
 
-def join_kernel(at_ref, own_ref, other_ref, out_ref, whole):
+def join_kernel(at_ref, *refs):
+    *pieces, out_ref, whole, columns, sems = refs
     x, core = at_ref[0], at_ref[1]
-    for other, piece in enumerate((own_ref, other_ref)):
-        for step in range(4):
-            where = ((x - step) & 3) * 2 + (core ^ other)
-            whole[pl.ds(pl.multiple_of(where * PART, 8), PART), :] = piece[step]
-    for tile in range(D // LANES):
-        cut = slice(tile * LANES, (tile + 1) * LANES)
-        out_ref[:, cut] = whole[cut, :].T
+    for index, piece in enumerate(pieces):
+        step, other = divmod(index, 2)
+        where = ((x - step) & 3) * 2 + (core ^ other)
+        whole[pl.ds(pl.multiple_of(where * PART, 8), PART), :] = piece[...]
+    copies = []
+    for tile in range(TILES):
+        columns[tile] = whole[tile * LANES : (tile + 1) * LANES, :].T
+        copies.append(
+            pltpu.make_async_copy(
+                columns.at[tile], out_ref.at[:, pl.ds(tile * LANES, LANES)], sems.at[tile]
+            )
+        )
+        copies[-1].start()
+    for copy in copies:
+        copy.wait()
 
 
 def take_kernel(blocks, at_ref, back_ref, target_ref, out_ref):
@@ -225,6 +234,7 @@
     return [(i, ((i // 2 + step) % 4) * 2 + i % 2) for i in range(REPS)]
 
 
+BY_CORE = [0, 2, 4, 6, 1, 3, 5, 7]
 CORES = [(i, i ^ 1) for i in range(REPS)]
 
 
@@ -236,6 +246,7 @@
 
 SMEM = pl.BlockSpec(memory_space=pltpu.SMEM)
 VMEM = pl.BlockSpec(memory_space=pltpu.VMEM)
+ANY = pl.BlockSpec(memory_space=pltpu.HBM)
 
 
 def refine(cap, got):
@@ -286,23 +297,30 @@
     back = lax.all_to_all(
         share.reshape(OWNERS, per * K, LANES), "cluster", 0, 0, tiled=True
     ).reshape(blocks, K, LANES)
-    line = jnp.stack([cent] + [lax.ppermute(cent, "rep", along_x(step)) for step in (1, 2, 3)])
-    pieces = [line, lax.ppermute(line, "rep", CORES)]
+    pieces = []
+    for step in range(4):
+        mine = lax.ppermute(cent, "rep", along_x(step)) if step else cent
+        pieces += [mine, lax.ppermute(mine, "rep", CORES)]
     return pieces, back, target, most
 
 
 def place():
     rep = lax.axis_index("rep")
-    return jnp.stack([rep // 2, rep % 2, rep]).astype(jnp.int32)
+    return jnp.stack([rep // 2, rep % 2, rep % 2 * 4 + rep // 2]).astype(jnp.int32)
 
 
 def join(pieces):
     return pl.pallas_call(
         join_kernel,
         out_shape=shape(SLOTS, D),
-        in_specs=[SMEM, VMEM, VMEM],
-        scratch_shapes=[pltpu.VMEM((D, SLOTS), F32)],
-        compiler_params=params(),
+        in_specs=[SMEM] + [VMEM] * REPS,
+        out_specs=ANY,
+        scratch_shapes=[
+            pltpu.VMEM((D, SLOTS), F32),
+            pltpu.VMEM((TILES, SLOTS, LANES), F32),
+            pltpu.SemaphoreType.DMA((TILES,)),
+        ],
+        compiler_params=params(63700),
         cost_estimate=cost(0, 1_600_000),
         name="join",
     )(place(), *pieces)
@@ -321,14 +339,17 @@
 
 
 def on_device(vectors, parent_id, child_id):
+    slot = (parent_id * K + child_id).astype(F32).reshape(1, VEC)
     turned = pl.pallas_call(
         turn_kernel,
         out_shape=shape(REPS, ROWS, VEC),
         compiler_params=params(),
         cost_estimate=cost(0, 1_600_000),
         name="turn",
-    )(vectors, parent_id.reshape(1, VEC), child_id.reshape(1, VEC))
-    got = lax.all_to_all(turned, "rep", 0, 0, tiled=True)
+    )(vectors, slot)
+    got = lax.all_to_all(
+        turned, "rep", 0, 0, axis_index_groups=[BY_CORE], tiled=True
+    )
     pieces, back, target, most = refine(LANES, got)
     over = most[0] > LANES
 

time: 131 us -> 118 us (0.901)
  waiting for transfers between devices: 26.1 us -> 17.5 us
  Pallas kernels: 16.5 us -> 13.5 us
  local copies, waits for them, and re-layouts: 3.35 us -> 1.13 us
    all_to_all x1, waiting for transfers between devices: 8.41 us -> 0.01 us  [refine(): lax.all_to_all(share.reshape(OWNERS, per * K, LANES), 'cluster', 0, 0, ti...]
    pallas_call x1, Pallas kernels: 5.46 us -> 3.2 us  [refine(): pl.pallas_call(functools.partial(distance_kernel, blocks), out_shape=(sha...]
    unnamed x10 -> x2, local copies, waits for them, and re-layouts: 3.35 us -> 1.13 us
    pallas_call x1, Pallas kernels: 3.24 us -> 1.73 us  [refine(): pl.pallas_call(functools.partial(share_kernel, blocks), out_shape=(shape(...]
    ppermute x4 -> x7, waiting for transfers between devices: 6.31 us -> 6.22 us  [the longest x3 6.21 us: refine(): mine = lax.ppermute(cent, 'rep', along_x(step)) if step else cent]
  transfers between devices with their start and end apart: 8 -> 11, of which waited for: 7 -> 6; matrix products, arithmetic and copies ran while one was open for 0% -> 0% of each run, Pallas kernels for 1% -> 1%
where the time goes in v7:
time: 118 us; the launch traced here: 117 us
  blocking collectives  71.6 us (61%)
  waiting for transfers between devices  17.5 us (15%)
  Pallas kernels  13.5 us (11%)
  starting transfers between devices  9.77 us (8%)
  between operations  1.55 us (1%)
  other arithmetic  1.44 us (1%)
    all_to_all x1, blocking collectives, refine(): lax.all_to_all(packed.reshape(OWNERS, per * ROWS, LANES), 'cluster', 0, 0...  53.9 us
    all_to_all x1, blocking collectives, on_device(): lax.all_to_all(turned, 'rep', 0, 0, axis_index_groups=[BY_CORE], tiled=True)  17.7 us
    ppermute x3, waiting for transfers between devices, refine(): mine = lax.ppermute(cent, 'rep', along_x(step)) if step else cent  6.21 us
    all_to_all x1, starting transfers between devices, refine(): lax.all_to_all(share.reshape(OWNERS, per * K, LANES), 'cluster', 0, 0, ti...  5.58 us
    ppermute x1, waiting for transfers between devices, sum_over_rep(): return x + lax.ppermute(x, 'rep', [(i, i ^ 6) for i in range(REPS)])  5.1 us
    pallas_call x1, Pallas kernels, refine(): pl.pallas_call(functools.partial(pack_kernel, cap), out_shape=(shape(bloc...  5.04 us
    ppermute x1, waiting for transfers between devices, sum_over_rep(): x = x + lax.ppermute(x, 'rep', [(i, i ^ 2) for i in range(REPS)])  4.82 us
    pallas_call x1, Pallas kernels, refine(): pl.pallas_call(functools.partial(distance_kernel, blocks), out_shape=(sha...  3.2 us
  transfers between devices with their start and end apart: 11, of which 6 were waited for; matrix products, arithmetic and copies ran while one was open for 0% of the time, Pallas kernels for 1%

profile of v7, /device:TPU:8, one launch (start us, length us, event | category | flops | bytes accessed | tf_op | source)
XLA Modules:
  0.0 116.8 jit_solution(1342222044520113919)
XLA Ops:
  0.6 0.7 add_convert_fusion
  1.3 1.1 copy-done
  2.5 0.3 turn.1
  2.7 17.7 %all_to_all.27.in_ref = f32[8,104,256]{2,1,0:T(8,128)S(1)} all-to-all(f32[8,104,256]{2,1,0:T(8,128)S(1)} %turn.1), channel_id=1, replica_groups={{0,2,4,6,1,3,5,7},{8,10,12,14,9,11,13,15},{16,18,20,22,17,19,21,23},{24..., dimensions={0} | all-to-all | bytes 1703936 | tf_op jit(solution)/shard_map/all_to_all | solution.py:350
  20.4 5.0 %pack.3 = (f32[32,104,128]{2,1,0:T(8,128)S(1)}, s32[8,256]{1,0:T(8,128)S(1)}) custom-call(f32[8,104,256]{2,1,0:T(8,128)S(1)} %all_to_all.27.in_ref), custom_call_target="tpu_custom_call" | custom-call | flops 3489660928 | bytes 3000000 | tf_op jit(solution)/shard_map/pack/pallas_call | solution.py:254
  25.5 53.9 %all_to_all.28.x_ref = f32[32,104,128]{2,1,0:T(8,128)S(1)} all-to-all(f32[32,104,128]{2,1,0:T(8,128)S(1)} %get-tuple-element.43), channel_id=1, replica_groups=mesh['cluster'=32,'rep'=8] {'cluster'}, dimensions={0} | all-to-all | bytes 3407872 | tf_op jit(solution)/shard_map/all_to_all | solution.py:270
  79.4 3.2 %distance.3 = (f32[32,8,128]{2,1,0:T(8,128)S(1)}, s32[1]{0:T(128)}) custom-call(f32[32,104,128]{2,1,0:T(8,128)S(1)} %all_to_all.28.x_ref), custom_call_target="tpu_custom_call" | custom-call | flops 1610612736 | bytes 2000000 | tf_op jit(solution)/shard_map/distance/pallas_call | solution.py:273
  82.7 1.3 %collective-permute-done.10 = f32[32,8,128]{2,1,0:T(8,128)S(1)} collective-permute-done((f32[32,8,128]{2,1,0:T(8,128)S(1)}, f32[32,8,128]{2,1,0:T(8,128)S(1)}, u32[]{:S(2)}, u32[]{:S(2)}) %collective-permute-start.10) | collective-permute-done | bytes 131104 | tf_op jit(solution)/shard_map/ppermute | solution.py:242
  84.0 0.8 collective-permute-start.11
  84.9 4.8 %collective-permute-done.11 = f32[32,8,128]{2,1,0:T(8,128)S(1)} collective-permute-done((f32[32,8,128]{2,1,0:T(8,128)S(1)}, f32[32,8,128]{2,1,0:T(8,128)S(1)}, u32[]{:S(2)}, u32[]{:S(2)}) %collective-permute-start.11) | collective-permute-done | bytes 131104 | tf_op jit(solution)/shard_map/ppermute | solution.py:243
  89.7 1.2 collective-permute-start.12
  90.9 5.1 %collective-permute-done.12 = f32[32,8,128]{2,1,0:T(8,128)S(1)} collective-permute-done((f32[32,8,128]{2,1,0:T(8,128)S(1)}, f32[32,8,128]{2,1,0:T(8,128)S(1)}, u32[]{:S(2)}, u32[]{:S(2)}) %collective-permute-start.12) | collective-permute-done | bytes 131104 | tf_op jit(solution)/shard_map/ppermute | solution.py:244
  96.0 1.7 %share.3 = (f32[96,256]{1,0:T(8,128)S(1)}, f32[32,8,128]{2,1,0:T(8,128)}) custom-call(f32[32,104,128]{2,1,0:T(8,128)S(1)} %all_to_all.28.x_ref, f32[32,8,128]{2,1,0:T(8,128)S(1)} %add.52.pen_ref), custom_call_target="tpu_custom_call" | custom-call | flops 603979776 | bytes 2000000 | tf_op jit(solution)/shard_map/share/pallas_call | solution.py:286
  97.7 5.6 %all-to-all-start.4 = ((f32[32,8,128]{2,1,0:T(8,128)}), f32[32,8,128]{2,1,0:T(8,128)S(1)}, u32[]{:S(2)}, u32[]{:S(2)}) async-start(f32[32,8,128]{2,1,0:T(8,128)} %get-tuple-element.47), calls=%async_computation.4 | async-start | bytes 262144 | tf_op jit(solution)/shard_map/all_to_all | solution.py:297
  103.3 1.2 collective-permute-start.18
  104.4 0.5 collective-permute-start.16
  105.0 0.4 collective-permute-start.14
  105.4 2.6 %collective-permute-done.18 = f32[96,256]{1,0:T(8,128)S(1)} collective-permute-done((f32[96,256]{1,0:T(8,128)S(1)}, f32[96,256]{1,0:T(8,128)S(1)}, u32[]{:S(2)}, u32[]{:S(2)}) %collective-permute-start.18) | collective-permute-done | bytes 98336 | tf_op jit(solution)/shard_map/ppermute | solution.py:302
  108.0 2.7 %collective-permute-done.16 = f32[96,256]{1,0:T(8,128)S(1)} collective-permute-done((f32[96,256]{1,0:T(8,128)S(1)}, f32[96,256]{1,0:T(8,128)S(1)}, u32[]{:S(2)}, u32[]{:S(2)}) %collective-permute-start.16) | collective-permute-done | bytes 98336 | tf_op jit(solution)/shard_map/ppermute | solution.py:302
  110.7 1.0 collective-permute-done.14
  112.4 1.6 %take.3 = f32[8,256]{1,0:T(8,128)} custom-call(s32[3]{0:T(128)S(1)} %pad_add_fusion.2.at_ref, f32[32,8,128]{2,1,0:T(8,128)S(1)} %all-to-all-done.4.back_ref, s32[8,256]{1,0:T(8,128)S(1)} %get-tuple-element.48.target_ref), custom_call_target="tpu_custom_call" | custom-call | flops 50331648 | bytes 200000 | tf_op jit(solution)/shard_map/take/pallas_call | solution.py:331
  114.0 2.6 %conditional.1 = (f32[256,768]{1,0:T(8,128)}, f32[8,256]{1,0:T(8,128)}) conditional(s32[]{:T(128)} %bitcast.11, (f32[96,256]{1,0:T(8,128)S(1)}, f32[96,256]{1,0:T(8,128)S(1)}, f32[96,256]{1,0:T(8,128)S(1)}, f32[96,256]{1,0:T(8,128)S(1)}, f32[96,256]{1,0:T(8,128)S(1)}, /*index=5*/f32[96,256]{1,0:T(8,128)S(1)}, f32[96,256]{1,0:T(8,128)S(1)}, ...), branch_computations={%region_0.1_spmd, %region_1.2_spmd} | conditional | flops 11509366784 | bytes 27806444 | solution.py:365
  114.0 0.6 pad_add_fusion.at_ref
  114.6 1.7 %join.2 = f32[256,768]{1,0:T(8,128)} custom-call(s32[3]{0:T(128)} %pad_add_fusion.at_ref, f32[96,256]{1,0:T(8,128)S(1)} %get-tuple-element.19.refs_0_, f32[96,256]{1,0:T(8,128)S(1)} %get-tuple-element.20.refs_1_, f32[96,256]{1,0:T(8,128)S(1)} %get-tuple-element.21.refs_2_, f32[96,256]{1,0:T(8,128)S(1)} %get-tuple-element.22.refs_3_, ...), custom_call_target="tpu_custom_call" | custom-call | bytes 1600000 | tf_op jit(solution)/shard_map/cond/branch_0_fun/join/pallas_call | solution.py:313
  (15 shorter events, 0.2 us)
Async XLA Ops:
  1.3 1.1 copy-start
  82.6 1.4 %collective-permute-start.10 = (f32[32,8,128]{2,1,0:T(8,128)S(1)}, f32[32,8,128]{2,1,0:T(8,128)S(1)}, u32[]{:S(2)}, u32[]{:S(2)}) collective-permute-start(f32[32,8,128]{2,1,0:T(8,128)S(1)} %get-tuple-element.45), channel_id=1, source_target_pairs={{0,1},{1,0},{2,3},{3,2},{4,5},{5,4},{6,7},{7,6},{8,9},{9,8},{10,11... | collective-permute-start | bytes 393224 | tf_op jit(solution)/shard_map/ppermute | solution.py:242
  84.0 5.6 %collective-permute-start.11 = (f32[32,8,128]{2,1,0:T(8,128)S(1)}, f32[32,8,128]{2,1,0:T(8,128)S(1)}, u32[]{:S(2)}, u32[]{:S(2)}) collective-permute-start(f32[32,8,128]{2,1,0:T(8,128)S(1)} %add.50), channel_id=1, source_target_pairs={{0,2},{1,3},{2,0},{3,1},{4,6},{5,7},{6,4},{7,5},{8,10},{9,11},{10,... | collective-permute-start | bytes 393224 | tf_op jit(solution)/shard_map/ppermute | solution.py:243
  89.7 6.3 %collective-permute-start.12 = (f32[32,8,128]{2,1,0:T(8,128)S(1)}, f32[32,8,128]{2,1,0:T(8,128)S(1)}, u32[]{:S(2)}, u32[]{:S(2)}) collective-permute-start(f32[32,8,128]{2,1,0:T(8,128)S(1)} %add.51), channel_id=1, source_target_pairs={{0,6},{1,7},{2,4},{3,5},{4,2},{5,3},{6,0},{7,1},{8,14},{9,15},{10,... | collective-permute-start | bytes 393224 | tf_op jit(solution)/shard_map/ppermute | solution.py:244
  97.7 14.7 %all-to-all-start.4 = ((f32[32,8,128]{2,1,0:T(8,128)}), f32[32,8,128]{2,1,0:T(8,128)S(1)}, u32[]{:S(2)}, u32[]{:S(2)}) async-start(f32[32,8,128]{2,1,0:T(8,128)} %get-tuple-element.47), calls=%async_computation.4 | async-start | bytes 262144 | tf_op jit(solution)/shard_map/all_to_all | solution.py:297
  103.3 4.7 %collective-permute-start.18 = (f32[96,256]{1,0:T(8,128)S(1)}, f32[96,256]{1,0:T(8,128)S(1)}, u32[]{:S(2)}, u32[]{:S(2)}) collective-permute-start(f32[96,256]{1,0:T(8,128)S(1)} %get-tuple-element.46), channel_id=1, source_target_pairs={{0,6},{1,7},{2,0},{3,1},{4,2},{5,3},{6,4},{7,5},{8,14},{9,15},{10,... | collective-permute-start | bytes 294920 | tf_op jit(solution)/shard_map/ppermute | solution.py:302
  104.4 6.2 %collective-permute-start.16 = (f32[96,256]{1,0:T(8,128)S(1)}, f32[96,256]{1,0:T(8,128)S(1)}, u32[]{:S(2)}, u32[]{:S(2)}) collective-permute-start(f32[96,256]{1,0:T(8,128)S(1)} %get-tuple-element.46), channel_id=1, source_target_pairs={{0,4},{1,5},{2,6},{3,7},{4,0},{5,1},{6,2},{7,3},{8,12},{9,13},{10,... | collective-permute-start | bytes 294920 | tf_op jit(solution)/shard_map/ppermute | solution.py:302
  105.0 6.7 %collective-permute-start.14 = (f32[96,256]{1,0:T(8,128)S(1)}, f32[96,256]{1,0:T(8,128)S(1)}, u32[]{:S(2)}, u32[]{:S(2)}) collective-permute-start(f32[96,256]{1,0:T(8,128)S(1)} %get-tuple-element.46), channel_id=1, source_target_pairs={{0,2},{1,3},{2,4},{3,5},{4,6},{5,7},{6,0},{7,1},{8,10},{9,11},{10,... | collective-permute-start | bytes 294920 | tf_op jit(solution)/shard_map/ppermute | solution.py:302
  105.4 8.5 %collective-permute-start.13 = (f32[96,256]{1,0:T(8,128)S(1)}, f32[96,256]{1,0:T(8,128)S(1)}, u32[]{:S(2)}, u32[]{:S(2)}) collective-permute-start(f32[96,256]{1,0:T(8,128)S(1)} %get-tuple-element.46), channel_id=1, source_target_pairs={{0,1},{1,0},{2,3},{3,2},{4,5},{5,4},{6,7},{7,6},{8,9},{9,8},{10,11... | collective-permute-start | bytes 294920 | tf_op jit(solution)/shard_map/ppermute | solution.py:303
  108.0 6.0 %collective-permute-start.19 = (f32[96,256]{1,0:T(8,128)S(1)}, f32[96,256]{1,0:T(8,128)S(1)}, u32[]{:S(2)}, u32[]{:S(2)}) collective-permute-start(f32[96,256]{1,0:T(8,128)S(1)} %collective-permute-done.18), channel_id=1, source_target_pairs={{0,1},{1,0},{2,3},{3,2},{4,5},{5,4},{6,7},{7,6},{8,9},{9,8},{10,11... | collective-permute-start | bytes 294920 | tf_op jit(solution)/shard_map/ppermute | solution.py:303
  110.7 3.3 %collective-permute-start.17 = (f32[96,256]{1,0:T(8,128)S(1)}, f32[96,256]{1,0:T(8,128)S(1)}, u32[]{:S(2)}, u32[]{:S(2)}) collective-permute-start(f32[96,256]{1,0:T(8,128)S(1)} %collective-permute-done.16), channel_id=1, source_target_pairs={{0,1},{1,0},{2,3},{3,2},{4,5},{5,4},{6,7},{7,6},{8,9},{9,8},{10,11... | collective-permute-start | bytes 294920 | tf_op jit(solution)/shard_map/ppermute | solution.py:303
  111.6 2.3 %collective-permute-start.15 = (f32[96,256]{1,0:T(8,128)S(1)}, f32[96,256]{1,0:T(8,128)S(1)}, u32[]{:S(2)}, u32[]{:S(2)}) collective-permute-start(f32[96,256]{1,0:T(8,128)S(1)} %collective-permute-done.14), channel_id=1, source_target_pairs={{0,1},{1,0},{2,3},{3,2},{4,5},{5,4},{6,7},{7,6},{8,9},{9,8},{10,11... | collective-permute-start | bytes 294920 | tf_op jit(solution)/shard_map/ppermute | solution.py:303

commit v8 on v6

--- a/solution.py
+++ b/solution.py
@@ -102,7 +102,7 @@
             )
         return 0
 
-    lax.fori_loop(0, groups, group, 0, unroll=4)
+    lax.fori_loop(0, groups, group, 0, unroll=8)
 
 
 def load_pair(x_ref, n):
@@ -128,7 +128,7 @@
         total[...] += lax.dot_general(stack_of(x), hot, NT, preferred_element_type=F32)
         return 0
 
-    lax.fori_loop(0, blocks // 2, add, 0, unroll=8)
+    lax.fori_loop(0, blocks // 2, add, 0, unroll=16)
     sums = total[0:PART, :] + total[PART + 16 : STACK, :]
     counts = total[PART : PART + 8, :]
     high, low = parts_of(sums / (counts[0:1] + 1.0))
@@ -159,7 +159,7 @@
         out_ref[2 * n + 1] = part[:, LANES:PAIR]
         return 0
 
-    lax.fori_loop(0, blocks // 2, measure, 0, unroll=8)
+    lax.fori_loop(0, blocks // 2, measure, 0, unroll=16)
 
 
 def share_kernel(blocks, x_ref, pen_ref, cent_ref, share_ref, total, rest):
@@ -187,7 +187,7 @@
         )
         return 0
 
-    lax.fori_loop(0, blocks // 2, add, 0, unroll=8)
+    lax.fori_loop(0, blocks // 2, add, 0, unroll=16)
     weighted = total[0:PART, :] + total[PART + 16 : STACK, :] + rest[0:PART, :]
     summed = total[PART : PART + 1, :] + rest[PART : PART + 1, :]
     cent_ref[...] = weighted / (summed + 1.0)

time: 117 us -> 117 us (level)
  no operation moved by 1% of the time
where the time goes in v8:
time: 117 us; the launch traced here: 116 us
  blocking collectives  71.6 us (61%)
  waiting for transfers between devices  17.5 us (15%)
  Pallas kernels  12.6 us (11%)
  starting transfers between devices  9.77 us (8%)
  local copies, waits for them, and re-layouts  2 us (2%)
  between operations  1.42 us (1%)
    all_to_all x1, blocking collectives, refine(): lax.all_to_all(packed.reshape(OWNERS, per * ROWS, LANES), 'cluster', 0, 0...  53.9 us
    all_to_all x1, blocking collectives, on_device(): lax.all_to_all(turned, 'rep', 0, 0, axis_index_groups=[BY_CORE], tiled=True)  17.7 us
    ppermute x3, waiting for transfers between devices, refine(): mine = lax.ppermute(cent, 'rep', along_x(step)) if step else cent  6.2 us
    all_to_all x1, starting transfers between devices, refine(): lax.all_to_all(share.reshape(OWNERS, per * K, LANES), 'cluster', 0, 0, ti...  5.56 us
    ppermute x1, waiting for transfers between devices, sum_over_rep(): return x + lax.ppermute(x, 'rep', [(i, i ^ 6) for i in range(REPS)])  5.1 us
    ppermute x1, waiting for transfers between devices, sum_over_rep(): x = x + lax.ppermute(x, 'rep', [(i, i ^ 2) for i in range(REPS)])  4.82 us
    pallas_call x1, Pallas kernels, refine(): pl.pallas_call(functools.partial(pack_kernel, cap), out_shape=(shape(bloc...  4.7 us
    pallas_call x1, Pallas kernels, refine(): pl.pallas_call(functools.partial(distance_kernel, blocks), out_shape=(sha...  3.7 us
  transfers between devices with their start and end apart: 11, of which 6 were waited for; matrix products, arithmetic and copies ran while one was open for 0% of the time, Pallas kernels for 1%

profile of v8, /device:TPU:8, one launch (start us, length us, event | category | flops | bytes accessed | tf_op | source)
XLA Modules:
  0.0 115.8 jit_solution(15694451427940034337)
XLA Ops:
  0.6 0.7 add_convert_fusion
  1.3 1.1 copy-done
  2.5 0.3 turn.1
  2.7 17.7 %all_to_all.27.in_ref = f32[8,104,256]{2,1,0:T(8,128)S(1)} all-to-all(f32[8,104,256]{2,1,0:T(8,128)S(1)} %turn.1), channel_id=1, replica_groups={{0,2,4,6,1,3,5,7},{8,10,12,14,9,11,13,15},{16,18,20,22,17,19,21,23},{24..., dimensions={0} | all-to-all | bytes 1703936 | tf_op jit(solution)/shard_map/all_to_all | solution.py:335
  20.4 4.7 %pack.3 = (f32[32,104,128]{2,1,0:T(8,128)S(1)}, s32[8,256]{1,0:T(8,128)S(1)}) custom-call(f32[8,104,256]{2,1,0:T(8,128)S(1)} %all_to_all.27.in_ref), custom_call_target="tpu_custom_call" | custom-call | flops 3489660928 | bytes 3000000 | tf_op jit(solution)/shard_map/pack/pallas_call | solution.py:248
  25.1 53.9 %all_to_all.28.x_ref = f32[32,104,128]{2,1,0:T(8,128)S(1)} all-to-all(f32[32,104,128]{2,1,0:T(8,128)S(1)} %get-tuple-element.43), channel_id=1, replica_groups=mesh['cluster'=32,'rep'=8] {'cluster'}, dimensions={0} | all-to-all | bytes 3407872 | tf_op jit(solution)/shard_map/all_to_all | solution.py:260
  79.0 3.7 %distance.3 = (f32[32,8,128]{2,1,0:T(8,128)S(1)}, s32[1]{0:T(128)}) custom-call(f32[32,104,128]{2,1,0:T(8,128)S(1)} %all_to_all.28.x_ref), custom_call_target="tpu_custom_call" | custom-call | flops 1610612736 | bytes 2000000 | tf_op jit(solution)/shard_map/distance/pallas_call | solution.py:263
  82.8 1.3 %collective-permute-done.10 = f32[32,8,128]{2,1,0:T(8,128)S(1)} collective-permute-done((f32[32,8,128]{2,1,0:T(8,128)S(1)}, f32[32,8,128]{2,1,0:T(8,128)S(1)}, u32[]{:S(2)}, u32[]{:S(2)}) %collective-permute-start.10) | collective-permute-done | bytes 131104 | tf_op jit(solution)/shard_map/ppermute | solution.py:237
  84.2 0.8 collective-permute-start.11
  85.0 4.8 %collective-permute-done.11 = f32[32,8,128]{2,1,0:T(8,128)S(1)} collective-permute-done((f32[32,8,128]{2,1,0:T(8,128)S(1)}, f32[32,8,128]{2,1,0:T(8,128)S(1)}, u32[]{:S(2)}, u32[]{:S(2)}) %collective-permute-start.11) | collective-permute-done | bytes 131104 | tf_op jit(solution)/shard_map/ppermute | solution.py:238
  89.9 1.2 %collective-permute-start.12 = (f32[32,8,128]{2,1,0:T(8,128)S(1)}, f32[32,8,128]{2,1,0:T(8,128)S(1)}, u32[]{:S(2)}, u32[]{:S(2)}) collective-permute-start(f32[32,8,128]{2,1,0:T(8,128)S(1)} %add.51), channel_id=1, source_target_pairs={{0,6},{1,7},{2,4},{3,5},{4,2},{5,3},{6,0},{7,1},{8,14},{9,15},{10,... | collective-permute-start | bytes 393224 | tf_op jit(solution)/shard_map/ppermute | solution.py:239
  91.0 5.1 %collective-permute-done.12 = f32[32,8,128]{2,1,0:T(8,128)S(1)} collective-permute-done((f32[32,8,128]{2,1,0:T(8,128)S(1)}, f32[32,8,128]{2,1,0:T(8,128)S(1)}, u32[]{:S(2)}, u32[]{:S(2)}) %collective-permute-start.12) | collective-permute-done | bytes 131104 | tf_op jit(solution)/shard_map/ppermute | solution.py:239
  96.1 2.1 %share.3 = (f32[96,256]{1,0:T(8,128)S(1)}, f32[32,8,128]{2,1,0:T(8,128)}) custom-call(f32[32,104,128]{2,1,0:T(8,128)S(1)} %all_to_all.28.x_ref, f32[32,8,128]{2,1,0:T(8,128)S(1)} %add.52.pen_ref), custom_call_target="tpu_custom_call" | custom-call | flops 603979776 | bytes 2000000 | tf_op jit(solution)/shard_map/share/pallas_call | solution.py:276
  98.2 5.6 %all-to-all-start.4 = ((f32[32,8,128]{2,1,0:T(8,128)}), f32[32,8,128]{2,1,0:T(8,128)S(1)}, u32[]{:S(2)}, u32[]{:S(2)}) async-start(f32[32,8,128]{2,1,0:T(8,128)} %get-tuple-element.47), calls=%async_computation.4 | async-start | bytes 262144 | tf_op jit(solution)/shard_map/all_to_all | solution.py:287
  103.8 1.2 %collective-permute-start.18 = (f32[96,256]{1,0:T(8,128)S(1)}, f32[96,256]{1,0:T(8,128)S(1)}, u32[]{:S(2)}, u32[]{:S(2)}) collective-permute-start(f32[96,256]{1,0:T(8,128)S(1)} %get-tuple-element.46), channel_id=1, source_target_pairs={{0,6},{1,7},{2,0},{3,1},{4,2},{5,3},{6,4},{7,5},{8,14},{9,15},{10,... | collective-permute-start | bytes 294920 | tf_op jit(solution)/shard_map/ppermute | solution.py:292
  105.0 0.5 collective-permute-start.16
  105.5 0.4 collective-permute-start.14
  105.9 2.6 %collective-permute-done.18 = f32[96,256]{1,0:T(8,128)S(1)} collective-permute-done((f32[96,256]{1,0:T(8,128)S(1)}, f32[96,256]{1,0:T(8,128)S(1)}, u32[]{:S(2)}, u32[]{:S(2)}) %collective-permute-start.18) | collective-permute-done | bytes 98336 | tf_op jit(solution)/shard_map/ppermute | solution.py:292
  108.5 2.7 %collective-permute-done.16 = f32[96,256]{1,0:T(8,128)S(1)} collective-permute-done((f32[96,256]{1,0:T(8,128)S(1)}, f32[96,256]{1,0:T(8,128)S(1)}, u32[]{:S(2)}, u32[]{:S(2)}) %collective-permute-start.16) | collective-permute-done | bytes 98336 | tf_op jit(solution)/shard_map/ppermute | solution.py:292
  111.2 1.0 collective-permute-done.14
  112.9 1.0 take.3
  113.9 1.0 conditional.1
  114.0 0.9 join.2
  114.9 0.9 copy-done.1
  (19 shorter events, 0.3 us)
Async XLA Ops:
  1.3 1.1 copy-start
  82.7 1.4 %collective-permute-start.10 = (f32[32,8,128]{2,1,0:T(8,128)S(1)}, f32[32,8,128]{2,1,0:T(8,128)S(1)}, u32[]{:S(2)}, u32[]{:S(2)}) collective-permute-start(f32[32,8,128]{2,1,0:T(8,128)S(1)} %get-tuple-element.45), channel_id=1, source_target_pairs={{0,1},{1,0},{2,3},{3,2},{4,5},{5,4},{6,7},{7,6},{8,9},{9,8},{10,11... | collective-permute-start | bytes 393224 | tf_op jit(solution)/shard_map/ppermute | solution.py:237
  84.2 5.6 %collective-permute-start.11 = (f32[32,8,128]{2,1,0:T(8,128)S(1)}, f32[32,8,128]{2,1,0:T(8,128)S(1)}, u32[]{:S(2)}, u32[]{:S(2)}) collective-permute-start(f32[32,8,128]{2,1,0:T(8,128)S(1)} %add.50), channel_id=1, source_target_pairs={{0,2},{1,3},{2,0},{3,1},{4,6},{5,7},{6,4},{7,5},{8,10},{9,11},{10,... | collective-permute-start | bytes 393224 | tf_op jit(solution)/shard_map/ppermute | solution.py:238
  89.9 6.3 %collective-permute-start.12 = (f32[32,8,128]{2,1,0:T(8,128)S(1)}, f32[32,8,128]{2,1,0:T(8,128)S(1)}, u32[]{:S(2)}, u32[]{:S(2)}) collective-permute-start(f32[32,8,128]{2,1,0:T(8,128)S(1)} %add.51), channel_id=1, source_target_pairs={{0,6},{1,7},{2,4},{3,5},{4,2},{5,3},{6,0},{7,1},{8,14},{9,15},{10,... | collective-permute-start | bytes 393224 | tf_op jit(solution)/shard_map/ppermute | solution.py:239
  98.2 14.6 %all-to-all-start.4 = ((f32[32,8,128]{2,1,0:T(8,128)}), f32[32,8,128]{2,1,0:T(8,128)S(1)}, u32[]{:S(2)}, u32[]{:S(2)}) async-start(f32[32,8,128]{2,1,0:T(8,128)} %get-tuple-element.47), calls=%async_computation.4 | async-start | bytes 262144 | tf_op jit(solution)/shard_map/all_to_all | solution.py:287
  103.8 4.7 %collective-permute-start.18 = (f32[96,256]{1,0:T(8,128)S(1)}, f32[96,256]{1,0:T(8,128)S(1)}, u32[]{:S(2)}, u32[]{:S(2)}) collective-permute-start(f32[96,256]{1,0:T(8,128)S(1)} %get-tuple-element.46), channel_id=1, source_target_pairs={{0,6},{1,7},{2,0},{3,1},{4,2},{5,3},{6,4},{7,5},{8,14},{9,15},{10,... | collective-permute-start | bytes 294920 | tf_op jit(solution)/shard_map/ppermute | solution.py:292
  105.0 6.2 %collective-permute-start.16 = (f32[96,256]{1,0:T(8,128)S(1)}, f32[96,256]{1,0:T(8,128)S(1)}, u32[]{:S(2)}, u32[]{:S(2)}) collective-permute-start(f32[96,256]{1,0:T(8,128)S(1)} %get-tuple-element.46), channel_id=1, source_target_pairs={{0,4},{1,5},{2,6},{3,7},{4,0},{5,1},{6,2},{7,3},{8,12},{9,13},{10,... | collective-permute-start | bytes 294920 | tf_op jit(solution)/shard_map/ppermute | solution.py:292
  105.5 6.7 %collective-permute-start.14 = (f32[96,256]{1,0:T(8,128)S(1)}, f32[96,256]{1,0:T(8,128)S(1)}, u32[]{:S(2)}, u32[]{:S(2)}) collective-permute-start(f32[96,256]{1,0:T(8,128)S(1)} %get-tuple-element.46), channel_id=1, source_target_pairs={{0,2},{1,3},{2,4},{3,5},{4,6},{5,7},{6,0},{7,1},{8,10},{9,11},{10,... | collective-permute-start | bytes 294920 | tf_op jit(solution)/shard_map/ppermute | solution.py:292
  105.9 7.9 %collective-permute-start.13 = (f32[96,256]{1,0:T(8,128)S(1)}, f32[96,256]{1,0:T(8,128)S(1)}, u32[]{:S(2)}, u32[]{:S(2)}) collective-permute-start(f32[96,256]{1,0:T(8,128)S(1)} %get-tuple-element.46), channel_id=1, source_target_pairs={{0,1},{1,0},{2,3},{3,2},{4,5},{5,4},{6,7},{7,6},{8,9},{9,8},{10,11... | collective-permute-start | bytes 294920 | tf_op jit(solution)/shard_map/ppermute | solution.py:293
  108.5 5.4 %collective-permute-start.19 = (f32[96,256]{1,0:T(8,128)S(1)}, f32[96,256]{1,0:T(8,128)S(1)}, u32[]{:S(2)}, u32[]{:S(2)}) collective-permute-start(f32[96,256]{1,0:T(8,128)S(1)} %collective-permute-done.18), channel_id=1, source_target_pairs={{0,1},{1,0},{2,3},{3,2},{4,5},{5,4},{6,7},{7,6},{8,9},{9,8},{10,11... | collective-permute-start | bytes 294920 | tf_op jit(solution)/shard_map/ppermute | solution.py:293
  111.2 2.7 %collective-permute-start.17 = (f32[96,256]{1,0:T(8,128)S(1)}, f32[96,256]{1,0:T(8,128)S(1)}, u32[]{:S(2)}, u32[]{:S(2)}) collective-permute-start(f32[96,256]{1,0:T(8,128)S(1)} %collective-permute-done.16), channel_id=1, source_target_pairs={{0,1},{1,0},{2,3},{3,2},{4,5},{5,4},{6,7},{7,6},{8,9},{9,8},{10,11... | collective-permute-start | bytes 294920 | tf_op jit(solution)/shard_map/ppermute | solution.py:293
  112.1 1.8 %collective-permute-start.15 = (f32[96,256]{1,0:T(8,128)S(1)}, f32[96,256]{1,0:T(8,128)S(1)}, u32[]{:S(2)}, u32[]{:S(2)}) collective-permute-start(f32[96,256]{1,0:T(8,128)S(1)} %collective-permute-done.14), channel_id=1, source_target_pairs={{0,1},{1,0},{2,3},{3,2},{4,5},{5,4},{6,7},{7,6},{8,9},{9,8},{10,11... | collective-permute-start | bytes 294920 | tf_op jit(solution)/shard_map/ppermute | solution.py:293
  114.9 0.9 copy-start.1
  114.9 0.9 copy-start.2

commit v9 on v6

--- a/solution.py
+++ b/solution.py
@@ -102,7 +102,7 @@
             )
         return 0
 
-    lax.fori_loop(0, groups, group, 0, unroll=4)
+    lax.fori_loop(0, groups, group, 0, unroll=8)
 
 
 def load_pair(x_ref, n):

time: 117 us -> 116 us (level)
  no operation moved by 1% of the time
where the time goes in v9:
time: 116 us; the launch traced here: 115 us
  blocking collectives  71.6 us (62%)
  waiting for transfers between devices  17.5 us (15%)
  Pallas kernels  11.7 us (10%)
  starting transfers between devices  9.76 us (8%)
  local copies, waits for them, and re-layouts  2 us (2%)
  between operations  1.42 us (1%)
    all_to_all x1, blocking collectives, refine(): lax.all_to_all(packed.reshape(OWNERS, per * ROWS, LANES), 'cluster', 0, 0...  53.9 us
    all_to_all x1, blocking collectives, on_device(): lax.all_to_all(turned, 'rep', 0, 0, axis_index_groups=[BY_CORE], tiled=True)  17.7 us
    ppermute x3, waiting for transfers between devices, refine(): mine = lax.ppermute(cent, 'rep', along_x(step)) if step else cent  6.21 us
    all_to_all x1, starting transfers between devices, refine(): lax.all_to_all(share.reshape(OWNERS, per * K, LANES), 'cluster', 0, 0, ti...  5.57 us
    ppermute x1, waiting for transfers between devices, sum_over_rep(): return x + lax.ppermute(x, 'rep', [(i, i ^ 6) for i in range(REPS)])  5.1 us
    ppermute x1, waiting for transfers between devices, sum_over_rep(): x = x + lax.ppermute(x, 'rep', [(i, i ^ 2) for i in range(REPS)])  4.83 us
    pallas_call x1, Pallas kernels, refine(): pl.pallas_call(functools.partial(pack_kernel, cap), out_shape=(shape(bloc...  4.7 us
    pallas_call x1, Pallas kernels, refine(): pl.pallas_call(functools.partial(distance_kernel, blocks), out_shape=(sha...  3.2 us
  transfers between devices with their start and end apart: 11, of which 6 were waited for; matrix products, arithmetic and copies ran while one was open for 0% of the time, Pallas kernels for 1%

profile of v9, /device:TPU:8, one launch (start us, length us, event | category | flops | bytes accessed | tf_op | source)
XLA Modules:
  0.0 114.9 jit_solution(855593876176633000)
XLA Ops:
  0.6 0.7 add_convert_fusion
  1.3 1.1 copy-done
  2.5 0.3 turn.1
  2.7 17.7 %all_to_all.27.in_ref = f32[8,104,256]{2,1,0:T(8,128)S(1)} all-to-all(f32[8,104,256]{2,1,0:T(8,128)S(1)} %turn.1), channel_id=1, replica_groups={{0,2,4,6,1,3,5,7},{8,10,12,14,9,11,13,15},{16,18,20,22,17,19,21,23},{24..., dimensions={0} | all-to-all | bytes 1703936 | tf_op jit(solution)/shard_map/all_to_all | solution.py:335
  20.4 4.7 %pack.3 = (f32[32,104,128]{2,1,0:T(8,128)S(1)}, s32[8,256]{1,0:T(8,128)S(1)}) custom-call(f32[8,104,256]{2,1,0:T(8,128)S(1)} %all_to_all.27.in_ref), custom_call_target="tpu_custom_call" | custom-call | flops 3489660928 | bytes 3000000 | tf_op jit(solution)/shard_map/pack/pallas_call | solution.py:248
  25.1 53.9 %all_to_all.28.x_ref = f32[32,104,128]{2,1,0:T(8,128)S(1)} all-to-all(f32[32,104,128]{2,1,0:T(8,128)S(1)} %get-tuple-element.43), channel_id=1, replica_groups=mesh['cluster'=32,'rep'=8] {'cluster'}, dimensions={0} | all-to-all | bytes 3407872 | tf_op jit(solution)/shard_map/all_to_all | solution.py:260
  79.0 3.2 %distance.3 = (f32[32,8,128]{2,1,0:T(8,128)S(1)}, s32[1]{0:T(128)}) custom-call(f32[32,104,128]{2,1,0:T(8,128)S(1)} %all_to_all.28.x_ref), custom_call_target="tpu_custom_call" | custom-call | flops 1610612736 | bytes 2000000 | tf_op jit(solution)/shard_map/distance/pallas_call | solution.py:263
  82.3 1.3 %collective-permute-done.10 = f32[32,8,128]{2,1,0:T(8,128)S(1)} collective-permute-done((f32[32,8,128]{2,1,0:T(8,128)S(1)}, f32[32,8,128]{2,1,0:T(8,128)S(1)}, u32[]{:S(2)}, u32[]{:S(2)}) %collective-permute-start.10) | collective-permute-done | bytes 131104 | tf_op jit(solution)/shard_map/ppermute | solution.py:237
  83.7 0.8 collective-permute-start.11
  84.5 4.8 %collective-permute-done.11 = f32[32,8,128]{2,1,0:T(8,128)S(1)} collective-permute-done((f32[32,8,128]{2,1,0:T(8,128)S(1)}, f32[32,8,128]{2,1,0:T(8,128)S(1)}, u32[]{:S(2)}, u32[]{:S(2)}) %collective-permute-start.11) | collective-permute-done | bytes 131104 | tf_op jit(solution)/shard_map/ppermute | solution.py:238
  89.4 1.2 %collective-permute-start.12 = (f32[32,8,128]{2,1,0:T(8,128)S(1)}, f32[32,8,128]{2,1,0:T(8,128)S(1)}, u32[]{:S(2)}, u32[]{:S(2)}) collective-permute-start(f32[32,8,128]{2,1,0:T(8,128)S(1)} %add.51), channel_id=1, source_target_pairs={{0,6},{1,7},{2,4},{3,5},{4,2},{5,3},{6,0},{7,1},{8,14},{9,15},{10,... | collective-permute-start | bytes 393224 | tf_op jit(solution)/shard_map/ppermute | solution.py:239
  90.5 5.1 %collective-permute-done.12 = f32[32,8,128]{2,1,0:T(8,128)S(1)} collective-permute-done((f32[32,8,128]{2,1,0:T(8,128)S(1)}, f32[32,8,128]{2,1,0:T(8,128)S(1)}, u32[]{:S(2)}, u32[]{:S(2)}) %collective-permute-start.12) | collective-permute-done | bytes 131104 | tf_op jit(solution)/shard_map/ppermute | solution.py:239
  95.6 1.7 %share.3 = (f32[96,256]{1,0:T(8,128)S(1)}, f32[32,8,128]{2,1,0:T(8,128)}) custom-call(f32[32,104,128]{2,1,0:T(8,128)S(1)} %all_to_all.28.x_ref, f32[32,8,128]{2,1,0:T(8,128)S(1)} %add.52.pen_ref), custom_call_target="tpu_custom_call" | custom-call | flops 603979776 | bytes 2000000 | tf_op jit(solution)/shard_map/share/pallas_call | solution.py:276
  97.4 5.6 %all-to-all-start.4 = ((f32[32,8,128]{2,1,0:T(8,128)}), f32[32,8,128]{2,1,0:T(8,128)S(1)}, u32[]{:S(2)}, u32[]{:S(2)}) async-start(f32[32,8,128]{2,1,0:T(8,128)} %get-tuple-element.47), calls=%async_computation.4 | async-start | bytes 262144 | tf_op jit(solution)/shard_map/all_to_all | solution.py:287
  103.0 1.2 %collective-permute-start.18 = (f32[96,256]{1,0:T(8,128)S(1)}, f32[96,256]{1,0:T(8,128)S(1)}, u32[]{:S(2)}, u32[]{:S(2)}) collective-permute-start(f32[96,256]{1,0:T(8,128)S(1)} %get-tuple-element.46), channel_id=1, source_target_pairs={{0,6},{1,7},{2,0},{3,1},{4,2},{5,3},{6,4},{7,5},{8,14},{9,15},{10,... | collective-permute-start | bytes 294920 | tf_op jit(solution)/shard_map/ppermute | solution.py:292
  104.1 0.5 collective-permute-start.16
  104.6 0.4 collective-permute-start.14
  105.1 2.6 %collective-permute-done.18 = f32[96,256]{1,0:T(8,128)S(1)} collective-permute-done((f32[96,256]{1,0:T(8,128)S(1)}, f32[96,256]{1,0:T(8,128)S(1)}, u32[]{:S(2)}, u32[]{:S(2)}) %collective-permute-start.18) | collective-permute-done | bytes 98336 | tf_op jit(solution)/shard_map/ppermute | solution.py:292
  107.6 2.7 %collective-permute-done.16 = f32[96,256]{1,0:T(8,128)S(1)} collective-permute-done((f32[96,256]{1,0:T(8,128)S(1)}, f32[96,256]{1,0:T(8,128)S(1)}, u32[]{:S(2)}, u32[]{:S(2)}) %collective-permute-start.16) | collective-permute-done | bytes 98336 | tf_op jit(solution)/shard_map/ppermute | solution.py:292
  110.3 1.0 collective-permute-done.14
  112.0 1.0 take.3
  113.1 1.0 conditional.1
  113.2 0.9 join.2
  114.1 0.9 copy-done.1
  (19 shorter events, 0.3 us)
Async XLA Ops:
  1.3 1.1 copy-start
  82.2 1.4 %collective-permute-start.10 = (f32[32,8,128]{2,1,0:T(8,128)S(1)}, f32[32,8,128]{2,1,0:T(8,128)S(1)}, u32[]{:S(2)}, u32[]{:S(2)}) collective-permute-start(f32[32,8,128]{2,1,0:T(8,128)S(1)} %get-tuple-element.45), channel_id=1, source_target_pairs={{0,1},{1,0},{2,3},{3,2},{4,5},{5,4},{6,7},{7,6},{8,9},{9,8},{10,11... | collective-permute-start | bytes 393224 | tf_op jit(solution)/shard_map/ppermute | solution.py:237
  83.7 5.6 %collective-permute-start.11 = (f32[32,8,128]{2,1,0:T(8,128)S(1)}, f32[32,8,128]{2,1,0:T(8,128)S(1)}, u32[]{:S(2)}, u32[]{:S(2)}) collective-permute-start(f32[32,8,128]{2,1,0:T(8,128)S(1)} %add.50), channel_id=1, source_target_pairs={{0,2},{1,3},{2,0},{3,1},{4,6},{5,7},{6,4},{7,5},{8,10},{9,11},{10,... | collective-permute-start | bytes 393224 | tf_op jit(solution)/shard_map/ppermute | solution.py:238
  89.4 6.3 %collective-permute-start.12 = (f32[32,8,128]{2,1,0:T(8,128)S(1)}, f32[32,8,128]{2,1,0:T(8,128)S(1)}, u32[]{:S(2)}, u32[]{:S(2)}) collective-permute-start(f32[32,8,128]{2,1,0:T(8,128)S(1)} %add.51), channel_id=1, source_target_pairs={{0,6},{1,7},{2,4},{3,5},{4,2},{5,3},{6,0},{7,1},{8,14},{9,15},{10,... | collective-permute-start | bytes 393224 | tf_op jit(solution)/shard_map/ppermute | solution.py:239
  97.4 14.7 %all-to-all-start.4 = ((f32[32,8,128]{2,1,0:T(8,128)}), f32[32,8,128]{2,1,0:T(8,128)S(1)}, u32[]{:S(2)}, u32[]{:S(2)}) async-start(f32[32,8,128]{2,1,0:T(8,128)} %get-tuple-element.47), calls=%async_computation.4 | async-start | bytes 262144 | tf_op jit(solution)/shard_map/all_to_all | solution.py:287
  103.0 4.7 %collective-permute-start.18 = (f32[96,256]{1,0:T(8,128)S(1)}, f32[96,256]{1,0:T(8,128)S(1)}, u32[]{:S(2)}, u32[]{:S(2)}) collective-permute-start(f32[96,256]{1,0:T(8,128)S(1)} %get-tuple-element.46), channel_id=1, source_target_pairs={{0,6},{1,7},{2,0},{3,1},{4,2},{5,3},{6,4},{7,5},{8,14},{9,15},{10,... | collective-permute-start | bytes 294920 | tf_op jit(solution)/shard_map/ppermute | solution.py:292
  104.1 6.2 %collective-permute-start.16 = (f32[96,256]{1,0:T(8,128)S(1)}, f32[96,256]{1,0:T(8,128)S(1)}, u32[]{:S(2)}, u32[]{:S(2)}) collective-permute-start(f32[96,256]{1,0:T(8,128)S(1)} %get-tuple-element.46), channel_id=1, source_target_pairs={{0,4},{1,5},{2,6},{3,7},{4,0},{5,1},{6,2},{7,3},{8,12},{9,13},{10,... | collective-permute-start | bytes 294920 | tf_op jit(solution)/shard_map/ppermute | solution.py:292
  104.6 6.7 %collective-permute-start.14 = (f32[96,256]{1,0:T(8,128)S(1)}, f32[96,256]{1,0:T(8,128)S(1)}, u32[]{:S(2)}, u32[]{:S(2)}) collective-permute-start(f32[96,256]{1,0:T(8,128)S(1)} %get-tuple-element.46), channel_id=1, source_target_pairs={{0,2},{1,3},{2,4},{3,5},{4,6},{5,7},{6,0},{7,1},{8,10},{9,11},{10,... | collective-permute-start | bytes 294920 | tf_op jit(solution)/shard_map/ppermute | solution.py:292
  105.1 7.9 %collective-permute-start.13 = (f32[96,256]{1,0:T(8,128)S(1)}, f32[96,256]{1,0:T(8,128)S(1)}, u32[]{:S(2)}, u32[]{:S(2)}) collective-permute-start(f32[96,256]{1,0:T(8,128)S(1)} %get-tuple-element.46), channel_id=1, source_target_pairs={{0,1},{1,0},{2,3},{3,2},{4,5},{5,4},{6,7},{7,6},{8,9},{9,8},{10,11... | collective-permute-start | bytes 294920 | tf_op jit(solution)/shard_map/ppermute | solution.py:293
  107.6 5.4 %collective-permute-start.19 = (f32[96,256]{1,0:T(8,128)S(1)}, f32[96,256]{1,0:T(8,128)S(1)}, u32[]{:S(2)}, u32[]{:S(2)}) collective-permute-start(f32[96,256]{1,0:T(8,128)S(1)} %collective-permute-done.18), channel_id=1, source_target_pairs={{0,1},{1,0},{2,3},{3,2},{4,5},{5,4},{6,7},{7,6},{8,9},{9,8},{10,11... | collective-permute-start | bytes 294920 | tf_op jit(solution)/shard_map/ppermute | solution.py:293
  110.3 2.7 %collective-permute-start.17 = (f32[96,256]{1,0:T(8,128)S(1)}, f32[96,256]{1,0:T(8,128)S(1)}, u32[]{:S(2)}, u32[]{:S(2)}) collective-permute-start(f32[96,256]{1,0:T(8,128)S(1)} %collective-permute-done.16), channel_id=1, source_target_pairs={{0,1},{1,0},{2,3},{3,2},{4,5},{5,4},{6,7},{7,6},{8,9},{9,8},{10,11... | collective-permute-start | bytes 294920 | tf_op jit(solution)/shard_map/ppermute | solution.py:293
  111.3 1.8 %collective-permute-start.15 = (f32[96,256]{1,0:T(8,128)S(1)}, f32[96,256]{1,0:T(8,128)S(1)}, u32[]{:S(2)}, u32[]{:S(2)}) collective-permute-start(f32[96,256]{1,0:T(8,128)S(1)} %collective-permute-done.14), channel_id=1, source_target_pairs={{0,1},{1,0},{2,3},{3,2},{4,5},{5,4},{6,7},{7,6},{8,9},{9,8},{10,11... | collective-permute-start | bytes 294920 | tf_op jit(solution)/shard_map/ppermute | solution.py:293
  114.0 0.9 copy-start.1
  114.0 0.9 copy-start.2
